TPU v7x, 128 devices: a whole 4x4x4 slice. The times are simulated.
128 devices in a mesh: grp: 8 (over x, core), exp: 16 (over z, y).
Axes of the slice: x: 4, y: 4, z: 4, core: 2. Of those that a mesh axis runs over, the one named last changes fastest.
Arguments:
- images: bfloat16 [128, 197, 768], P(('grp', 'exp')), may hold values from -6 to 6
- cotangent: bfloat16 [128, 197, 768], P(('grp', 'exp')), may hold values from -6 to 6
- expert_ids: int32 [128, 197, 2], P(('grp', 'exp')), may hold values from 0 to 15, all different within a row; in each aligned block of 197 rows (0 to 196, 197 to 393, ..., all dimensions but the last counted through in order) at most 33 rows name the same one
- kept_routes: int32 [128, 197, 2], P(('grp', 'exp')), may hold values 0 or 1
- qkv_master: float32 [768, 2304], P('grp'), may hold values from -0.21875 to 0.21875
- qkv_first: float32 [768, 2304], P('grp'), may hold values from -64 to 64
- qkv_second: float32 [768, 2304], P('grp'), may hold values from 12.608 to 50.432
- proj_master: float32 [768, 768], P('grp'), may hold values from -1.25 to 1.25
- proj_first: float32 [768, 768], P('grp'), may hold values from -14 to 14
- proj_second: float32 [768, 768], P('grp'), may hold values from 0.50432 to 2.26944
- router_master: float32 [768, 16], P('grp'), may hold values from -0.15625 to 0.15625
- router_first: float32 [768, 16], P('grp'), may hold values from -768 to 768
- router_second: float32 [768, 16], P('grp'), may hold values from 1765.12 to 7060.48
- norm_master: float32 [768, 4], P('grp'), may hold values from -0.3 to 1.5, as said below
- norm_first: float32 [768, 4], P('grp'), may hold values from -96 to 96
- norm_second: float32 [768, 4], P('grp'), may hold values from 25.216 to 100.864
- inner_master: float32 [16, 768, 3072], P('exp', None, 'grp'), may hold values from -0.21875 to 0.21875
- inner_first: float32 [16, 768, 3072], P('exp', None, 'grp'), may hold values from -10 to 10
- inner_second: float32 [16, 768, 3072], P('exp', None, 'grp'), may hold values from 0.28368 to 1.13472
- outer_master: float32 [16, 3072, 768], P('exp', 'grp'), may hold values from -1.75 to 1.75
- outer_first: float32 [16, 3072, 768], P('exp', 'grp'), may hold values from -1.25 to 1.25
- outer_second: float32 [16, 3072, 768], P('exp', 'grp'), may hold values from 0.0044325 to 0.017853126
Outputs:
- result: bfloat16 [128, 197, 768], P(('grp', 'exp'))
- image_grad: float32 [128, 197, 768], P(('grp', 'exp'))
- qkv_moment: float32 [768, 2304], P('grp')
- qkv_square: float32 [768, 2304], P('grp')
- qkv_weight: float32 [768, 2304], P('grp')
- proj_moment: float32 [768, 768], P('grp')
- proj_square: float32 [768, 768], P('grp')
- proj_weight: float32 [768, 768], P('grp')
- router_moment: float32 [768, 16], P('grp')
- router_square: float32 [768, 16], P('grp')
- router_weight: float32 [768, 16], P('grp')
- norm_moment: float32 [768, 4], P('grp')
- norm_square: float32 [768, 4], P('grp')
- norm_weight: float32 [768, 4], P('grp')
- inner_moment: float32 [16, 768, 3072], P('exp', None, 'grp')
- inner_square: float32 [16, 768, 3072], P('exp', None, 'grp')
- inner_weight: float32 [16, 768, 3072], P('exp', None, 'grp')
- outer_moment: float32 [16, 3072, 768], P('exp', 'grp')
- outer_square: float32 [16, 3072, 768], P('exp', 'grp')
- outer_weight: float32 [16, 3072, 768], P('exp', 'grp')
Inputs may be any that keep to these rules, and one draw needn't show every extreme that they name: `expert_ids`: each token names two different experts. Among the tokens of one device no expert is named by more than 33 routes, a bound that some block reaches. `norm_master`: columns 0 and 2 are gains, columns 1 and 3 biases.
All inputs are finite; a program needn't handle non-finite values. No bound on the sum of `kept_routes` on one device may be relied on, other than what follows from the above.
Results may differ from a plain program's by a relative error of at most 0.015.
Values may be sent and summed in bfloat16 or wider, within the bound.
No kernel may reach another device: no remote copies, remote signals or barrier semaphores. Data moves between devices by JAX's collectives and lax.ppermute only.
A program may use at most 192 MiB of HBM per device.

v0:
```python
import jax
import jax.numpy as jnp
from jax import lax
from jax.sharding import PartitionSpec as P

HEADS = 12
HEAD_DIM = 64
STEP = 10


norm_epsilon = 1e-06
beta_first = 0.9
beta_second = 0.999
adam_epsilon = 1e-08
weight_decay = 0.1


def in_one_piece(arrays, axis, dim, along):
    widths = [a.shape[along] for a in arrays]
    both = jnp.concatenate(arrays, axis=along)
    result = lax.all_gather(both, axis, axis=dim, tiled=True)
    return tuple(jnp.split(result, [sum(widths[:k]) for k in range(1, len(widths))], axis=along))


def rows_first(arrays, axis, dims):
    turned = [jnp.moveaxis(a, dim, 0) for a, dim in zip(arrays, dims)]
    widths = [t[0].size for t in turned]
    both = jnp.concatenate([t.reshape(-1, w) for t, w in zip(turned, widths)], axis=1)
    result = lax.all_gather(both, axis, axis=0, tiled=True)
    blocks = jnp.split(result, [sum(widths[:k]) for k in range(1, len(widths))], axis=1)
    return tuple(
        (
            jnp.moveaxis(b.reshape(-1, *t.shape[1:]), 0, dim)
            for b, t, dim in zip(blocks, turned, dims)
        )
    )


def split_up(value, dim, peers):
    before, after = (value.shape[:dim], value.shape[dim + 1 :])
    return jnp.moveaxis(value.reshape(*before, peers, -1, *after), dim, 0)


def sum_together(arrays, axis, dims):
    peers = lax.axis_size(axis)
    blocks = [split_up(a, dim, peers) for a, dim in zip(arrays, dims)]
    lines = jnp.concatenate([b.reshape(peers, -1) for b in blocks], axis=1)
    extent = max(16, -(-lines.shape[1] // 1024) * 8)
    lines = jnp.pad(lines, ((0, 0), (0, extent * 128 - lines.shape[1]))).reshape(-1, 128)
    flat, at, outs = (lax.psum_scatter(lines, axis, tiled=True).reshape(-1), 0, [])
    for b in blocks:
        part = b[0]
        outs.append(flat[at : at + part.size].reshape(part.shape))
        at += part.size
    return tuple(outs)


def sent_together(arrays, axis, dim, along):
    both = jnp.concatenate(arrays, axis=along)
    result, at, outs = (lax.psum_scatter(both, axis, scatter_dimension=dim, tiled=True), 0, [])
    for a in arrays:
        outs.append(lax.slice_in_dim(result, at, at + a.shape[along], axis=along))
        at += a.shape[along]
    return tuple(outs)


def layer_norm(values, gain, shift):
    centered = values - jnp.mean(values, axis=-1, keepdims=True)
    variance = jnp.mean(centered * centered, axis=-1, keepdims=True)
    return centered * lax.rsqrt(variance + norm_epsilon) * gain + shift


def softmax_rows(logit_rows):
    return jax.nn.softmax(logit_rows, axis=-1)


def adamw(master, first, second, gradient, rate):
    first = beta_first * first + (1.0 - beta_first) * gradient
    second = beta_second * second + (1.0 - beta_second) * gradient * gradient
    corrected = first / (1.0 - beta_first**STEP)
    scaled = jnp.sqrt(second / (1.0 - beta_second**STEP)) + adam_epsilon
    return (first, second, master - rate * (corrected / scaled + weight_decay * master))


def on_device(
    images,
    cotangent,
    expert_ids,
    kept_routes,
    qkv_master,
    qkv_first,
    qkv_second,
    proj_master,
    proj_first,
    proj_second,
    router_master,
    router_first,
    router_second,
    norm_master,
    norm_first,
    norm_second,
    inner_master,
    inner_first,
    inner_second,
    outer_master,
    outer_first,
    outer_second,
):
    low_type = jnp.bfloat16
    image_count, length, model_width = images.shape
    token_count = image_count * length
    experts = lax.axis_size("exp")
    capacity = (2 * token_count + experts - 1) // experts + 8
    slot_total = experts * capacity
    score_scale = HEAD_DIM ** (-0.5)
    qkv_w, proj_w, router_w, norm_w = in_one_piece(
        (
            qkv_master.astype(low_type),
            proj_master.astype(low_type),
            router_master.astype(low_type),
            norm_master.astype(low_type),
        ),
        "grp",
        0,
        1,
    )
    norms = norm_w.astype(jnp.float32)
    inner = inner_master[0].astype(low_type)
    outer = outer_master[0].astype(low_type)
    inner_whole, outer_whole = rows_first((inner, outer), "grp", (1, 0))
    source = images.reshape(token_count, model_width).astype(jnp.float32)
    normed_full, first_back = jax.vjp(layer_norm, source, norms[:, 0], norms[:, 1])
    normed = normed_full.astype(low_type)
    triple = jnp.dot(normed, qkv_w, preferred_element_type=jnp.float32).astype(low_type)
    triple = triple.reshape(image_count, length, 3, HEADS, HEAD_DIM)
    queries = triple[:, :, 0]
    keys_part = triple[:, :, 1]
    values_part = triple[:, :, 2]
    scores = (
        jnp.einsum("bqhd,bkhd->bhqk", queries, keys_part, preferred_element_type=jnp.float32)
        * score_scale
    )
    attn_probs = jax.nn.softmax(scores, axis=-1)
    probs_low = attn_probs.astype(low_type)
    attended = jnp.einsum(
        "bhqk,bkhd->bqhd", probs_low, values_part, preferred_element_type=jnp.float32
    )
    attended = attended.astype(low_type).reshape(token_count, model_width)
    middle = source + jnp.dot(attended, proj_w, preferred_element_type=jnp.float32)
    second_full, second_back = jax.vjp(layer_norm, middle, norms[:, 2], norms[:, 3])
    second = second_full.astype(low_type)
    logit_rows = jnp.dot(second, router_w, preferred_element_type=jnp.float32)
    router_probs, router_back = jax.vjp(softmax_rows, logit_rows)
    id_rows = expert_ids.reshape(token_count, 2)
    keep = kept_routes.reshape(token_count, 2).astype(jnp.float32)
    expert_range = jnp.arange(experts, dtype=jnp.int32)
    chosen = (id_rows[:, :, None] == expert_range[None, None, :]).astype(jnp.float32)
    gates = jnp.sum(router_probs[:, None, :] * chosen, axis=-1) * keep
    flat_ids = id_rows.reshape(-1)
    marks = (flat_ids[:, None] == expert_range[None, :]).astype(jnp.int32)
    slots = jnp.sum((jnp.cumsum(marks, axis=0) - marks) * marks, axis=1)
    target = flat_ids * capacity + slots
    live = kept_routes.reshape(-1) > 0
    slot_range = jnp.arange(slot_total, dtype=jnp.int32)
    dispatch = ((slot_range[:, None] == target[None, :]) & live[None, :]).astype(low_type)
    copies = jnp.repeat(second, 2, axis=0)
    send = jnp.dot(dispatch, copies, preferred_element_type=jnp.float32).astype(low_type)
    send = send.reshape(experts, capacity, model_width)
    arrived = lax.all_to_all(send, "exp", split_axis=0, concat_axis=0, tiled=True)
    gathered = arrived.reshape(-1, model_width)
    hidden = jnp.dot(gathered, inner_whole, preferred_element_type=jnp.float32)
    active_full, gelu_back = jax.vjp(jax.nn.gelu, hidden)
    active = active_full.astype(low_type)
    summed = jnp.dot(active, outer_whole, preferred_element_type=jnp.float32)
    outgoing = summed.astype(low_type).reshape(experts, capacity, model_width)
    returned = lax.all_to_all(outgoing, "exp", split_axis=0, concat_axis=0, tiled=True).reshape(
        slot_total, model_width
    )
    per_route = jnp.einsum("sr,sd->rd", dispatch, returned, preferred_element_type=jnp.float32)
    per_route = per_route.reshape(token_count, 2, model_width)
    output = middle + jnp.sum(gates[:, :, None] * per_route, axis=1)
    result = output.astype(low_type).reshape(images.shape)
    grad_out = cotangent.reshape(token_count, model_width).astype(jnp.float32)
    d_gates = jnp.sum(grad_out[:, None, :] * per_route, axis=-1) * keep
    d_router = jnp.sum(d_gates[:, :, None] * chosen, axis=1)
    d_logits = router_back(d_router)[0].astype(low_type)
    router_grad = jnp.einsum("td,te->de", second, d_logits, preferred_element_type=jnp.float32)
    d_route = (gates[:, :, None] * grad_out[:, None, :]).astype(low_type).reshape(-1, model_width)
    back_send = jnp.dot(dispatch, d_route, preferred_element_type=jnp.float32).astype(low_type)
    back_send = back_send.reshape(experts, capacity, model_width)
    back_arrived = lax.all_to_all(back_send, "exp", split_axis=0, concat_axis=0, tiled=True)
    back_gathered = back_arrived.reshape(-1, model_width)
    outer_part = jnp.einsum("rf,rd->fd", active, back_gathered, preferred_element_type=jnp.float32)
    d_active = jnp.einsum(
        "rd,fd->rf", back_gathered, outer_whole, preferred_element_type=jnp.float32
    )
    d_hidden = gelu_back(d_active)[0].astype(low_type)
    inner_part = jnp.einsum("rd,rf->df", gathered, d_hidden, preferred_element_type=jnp.float32)
    d_inputs = jnp.einsum("rf,df->rd", d_hidden, inner_whole, preferred_element_type=jnp.float32)
    inner_grad, outer_grad = sum_together((inner_part, outer_part), "grp", (1, 0))
    d_inputs = d_inputs.astype(low_type).reshape(experts, capacity, model_width)
    d_back = lax.all_to_all(d_inputs, "exp", split_axis=0, concat_axis=0, tiled=True).reshape(
        slot_total, model_width
    )
    d_copies = jnp.einsum("sr,sd->rd", dispatch, d_back, preferred_element_type=jnp.float32)
    d_copies = d_copies.reshape(token_count, 2, model_width)
    d_second = jnp.einsum(
        "te,de->td", d_logits, router_w, preferred_element_type=jnp.float32
    ) + jnp.sum(d_copies, axis=1)
    d_middle_norm, d_gain_two, d_shift_two = second_back(d_second)
    d_middle = grad_out + d_middle_norm
    d_middle_low = d_middle.astype(low_type)
    proj_grad = jnp.einsum("td,te->de", attended, d_middle_low, preferred_element_type=jnp.float32)
    d_attended = jnp.einsum("te,de->td", d_middle_low, proj_w, preferred_element_type=jnp.float32)
    d_attended = d_attended.astype(low_type).reshape(image_count, length, HEADS, HEAD_DIM)
    d_values = jnp.einsum(
        "bhqk,bqhd->bkhd", probs_low, d_attended, preferred_element_type=jnp.float32
    )
    d_weights = jnp.einsum(
        "bqhd,bkhd->bhqk", d_attended, values_part, preferred_element_type=jnp.float32
    )
    d_scores = attn_probs * (d_weights - jnp.sum(d_weights * attn_probs, axis=-1, keepdims=True))
    d_scores = d_scores.astype(low_type)
    d_queries = (
        jnp.einsum("bhqk,bkhd->bqhd", d_scores, keys_part, preferred_element_type=jnp.float32)
        * score_scale
    )
    d_keys = (
        jnp.einsum("bhqk,bqhd->bkhd", d_scores, queries, preferred_element_type=jnp.float32)
        * score_scale
    )
    d_triple = jnp.stack([d_queries, d_keys, d_values], axis=2).astype(low_type)
    d_triple = d_triple.reshape(token_count, 3 * model_width)
    qkv_grad = jnp.einsum("td,te->de", normed, d_triple, preferred_element_type=jnp.float32)
    d_normed = jnp.einsum("te,de->td", d_triple, qkv_w, preferred_element_type=jnp.float32)
    d_source, d_gain_one, d_shift_one = first_back(d_normed)
    image_grad = (d_middle + d_source).reshape(images.shape)
    norm_grad = jnp.stack([d_gain_one, d_shift_one, d_gain_two, d_shift_two], axis=1)
    shares = sent_together((qkv_grad, proj_grad, router_grad, norm_grad), "grp", 0, 1)
    owned = lax.psum((shares[0], shares[1], shares[2], shares[3]), "exp")
    qkv_moment, qkv_square, qkv_weight = adamw(qkv_master, qkv_first, qkv_second, owned[0], 0.04)
    proj_moment, proj_square, proj_weight = adamw(
        proj_master, proj_first, proj_second, owned[1], 0.2
    )
    router_moment, router_square, router_weight = adamw(
        router_master, router_first, router_second, owned[2], 0.03
    )
    norm_moment, norm_square, norm_weight = adamw(
        norm_master, norm_first, norm_second, owned[3], 0.3
    )
    inner_moment, inner_square, inner_weight = adamw(
        inner_master, inner_first, inner_second, inner_grad[None], 0.04
    )
    outer_moment, outer_square, outer_weight = adamw(
        outer_master, outer_first, outer_second, outer_grad[None], 0.15
    )
    return (
        result,
        image_grad,
        qkv_moment,
        qkv_square,
        qkv_weight,
        proj_moment,
        proj_square,
        proj_weight,
        router_moment,
        router_square,
        router_weight,
        norm_moment,
        norm_square,
        norm_weight,
        inner_moment,
        inner_square,
        inner_weight,
        outer_moment,
        outer_square,
        outer_weight,
    )


def solution(mesh):
    in_specs = (
        P(("grp", "exp"), None, None),
        P(("grp", "exp"), None, None),
        P(("grp", "exp"), None, None),
        P(("grp", "exp"), None, None),
        P("grp", None),
        P("grp", None),
        P("grp", None),
        P("grp", None),
        P("grp", None),
        P("grp", None),
        P("grp", None),
        P("grp", None),
        P("grp", None),
        P("grp", None),
        P("grp", None),
        P("grp", None),
        P("exp", None, "grp"),
        P("exp", None, "grp"),
        P("exp", None, "grp"),
        P("exp", "grp", None),
        P("exp", "grp", None),
        P("exp", "grp", None),
    )
    out_specs = (
        P(("grp", "exp"), None, None),
        P(("grp", "exp"), None, None),
        P("grp", None),
        P("grp", None),
        P("grp", None),
        P("grp", None),
        P("grp", None),
        P("grp", None),
        P("grp", None),
        P("grp", None),
        P("grp", None),
        P("grp", None),
        P("grp", None),
        P("grp", None),
        P("exp", None, "grp"),
        P("exp", None, "grp"),
        P("exp", None, "grp"),
        P("exp", "grp", None),
        P("exp", "grp", None),
        P("exp", "grp", None),
    )
    return jax.shard_map(
        on_device, mesh=mesh, in_specs=in_specs, out_specs=out_specs, check_vma=False
    )
```

profile of v0, /device:TPU:1, one launch (start us, length us, event | category | flops | bytes accessed | tf_op | source)
XLA Modules:
  0.0 492.6 jit_solution(12751401338446250391)
XLA Ops:
  14.3 1.9 mul.626
  20.7 30.4 %all-gather.3.cloned.1.call-done = bf16[768,3092]{1,0:T(8,128)(2,1)} async-done(((bf16[96,3092]{1,0:T(8,128)(2,1)}), bf16[768,3092]{1,0:T(8,128)(2,1)}) %all-gather.3.cloned.1.call-update) | async-done | bytes 4749328 | tf_op jit(solution)/shard_map/all_gather | solution.py:21
  53.0 3.0 convolution_convert_fusion
  58.1 2.1 fusion.132
  61.6 2.0 fusion.133
  68.0 1.6 reduce_sum.251
  70.3 2.9 convolution_convert_fusion.1
  73.2 2.3 reshape.515
  75.6 6.8 %all-to-all-start.2 = ((bf16[16,33,768]{2,1,0:T(8,128)(2,1)}), bf16[16,33,768]{2,1,0:T(8,128)(2,1)}, u32[]{:S(2)}, u32[]{:S(2)}) async-start(bf16[16,33,768]{2,1,0:T(8,128)(2,1)} %reshape.515), calls=%async_computation.2 | async-start | bytes 1966080 | tf_op jit(solution)/shard_map/all_to_all | solution.py:191
  82.3 2.1 broadcast_in_dim.14
  84.4 2.7 reshape.509
  87.1 2.6 convolution_convert_fusion.2
  89.7 2.5 reshape.510
  92.2 5.9 %all-to-all-done.2 = bf16[16,33,768]{2,1,0:T(8,128)(2,1)} async-done(((bf16[16,33,768]{2,1,0:T(8,128)(2,1)}), bf16[16,33,768]{2,1,0:T(8,128)(2,1)}, u32[]{:S(2)}, u32[]{:S(2)}) %all-to-all-start.2) | async-done | bytes 811040 | tf_op jit(solution)/shard_map/all_to_all | solution.py:191
  98.1 4.5 all-to-all-start
  102.7 1.5 reduce_sum.212
  104.1 1.5 multiply_add_fusion.4
  106.7 2.4 reshape.516
  109.1 8.2 %all-to-all-done = bf16[16,33,768]{2,1,0:T(8,128)(2,1)} async-done(((bf16[16,33,768]{2,1,0:T(8,128)(2,1)}), bf16[16,33,768]{2,1,0:T(8,128)(2,1)}, u32[]{:S(2)}, u32[]{:S(2)}) %all-to-all-start) | async-done | bytes 811040 | tf_op jit(solution)/shard_map/all_to_all | solution.py:169
  117.3 2.4 reshape.511
  119.6 5.0 %fusion.18 = f32[528,3072]{1,0:T(8,128)S(1)} fusion(bf16[528,768]{1,0:T(8,128)(2,1)} %reshape.516, bf16[3072,1536]{1,0:T(8,128)(2,1)} %all-gather.5.cloned.1.call-done), kind=kOutput, calls=%fused_computation.26 | convolution fusion | flops 2491416576 | bytes 12017664 | tf_op jit(solution)/shard_map/rd,fd->rf/dot_general | solution.py:194
  125.2 7.4 %fusion.14 = (bf16[3072,528]{0,1:T(8,128)(2,1)}, f32[528,3072]{1,0:T(8,128)S(1)}) fusion(f32[528,3072]{1,0:T(8,128)S(1)} %fusion.18, bf16[528,768]{1,0:T(8,128)(2,1)S(1)} %copy-done.26, bf16[3072,1536]{1,0:T(8,128)(2,1)S(1)} %copy-done.49), kind=kOutput, calls=%fused_computation.19 | convolution fusion | flops 2523856896 | bytes 21749760 | tf_op jit(solution)/shard_map/dot_general | solution.py:171
  132.7 2.8 copy-done.50
  135.4 7.2 %fusion.35 = bf16[528,768]{1,0:T(8,128)(2,1)} fusion(bf16[3072,1536]{1,0:T(8,128)(2,1)S(1)} %copy-done.49, f32[528,3072]{1,0:T(8,128)S(1)} %get-tuple-element.171, f32[528,3072]{1,0:T(8,128)S(1)} %fusion.18), kind=kOutput, calls=%fused_computation.50 | convolution fusion | flops 2524262400 | bytes 18505728 | tf_op jit(solution)/shard_map/rf,df->rd/dot_general | solution.py:199
  142.6 2.3 reshape.517
  144.9 5.1 %all-to-all-start.3 = ((bf16[16,33,768]{2,1,0:T(8,128)(2,1)}), bf16[16,33,768]{2,1,0:T(8,128)(2,1)}, u32[]{:S(2)}, u32[]{:S(2)}) async-start(bf16[16,33,768]{2,1,0:T(8,128)(2,1)} %reshape.517), calls=%async_computation.3 | async-start | bytes 1966080 | tf_op jit(solution)/shard_map/all_to_all | solution.py:202
  150.1 8.9 %fusion.40 = bf16[528,768]{1,0:T(8,128)(2,1)} fusion(bf16[3072,1536]{1,0:T(8,128)(2,1)} %all-gather.5.cloned.1.call-done, f32[528,3072]{1,0:T(8,128)} %copy-done.50), kind=kOutput, calls=%fused_computation.51 | convolution fusion | flops 2506420224 | bytes 12017664 | tf_op jit(solution)/shard_map/dot_general | solution.py:174
  159.0 2.4 reshape.512
  161.3 2.9 all-to-all-done.3
  164.3 4.3 all-to-all-start.1
  168.7 2.4 reshape.526
  171.0 2.7 convolution_reduce_fusion
  173.8 8.0 %all-to-all-done.1 = bf16[16,33,768]{2,1,0:T(8,128)(2,1)} async-done(((bf16[16,33,768]{2,1,0:T(8,128)(2,1)}), bf16[16,33,768]{2,1,0:T(8,128)(2,1)}, u32[]{:S(2)}, u32[]{:S(2)}) %all-to-all-start.1) | async-done | bytes 811040 | tf_op jit(solution)/shard_map/all_to_all | solution.py:176
  181.7 2.4 reshape.525
  184.1 2.3 multiply_reduce_fusion.2
  186.5 1.4 multiply_reduce_fusion.4
  189.9 1.9 convolution_convert_fusion.4
  192.7 1.6 convolution_bitcast_fusion.1
  198.3 4.2 fusion.91
  202.6 1.4 fusion.123
  208.1 11.2 %concatenate.22 = f32[768,3092]{1,0:T(8,128)} concatenate(f32[768,2304]{1,0:T(8,128)} %fusion.91, f32[768,768]{1,0:T(8,128)S(1)} %fusion.135, f32[768,16]{1,0:T(8,128)} %fusion.136, f32[768,1]{1,0:T(8,128)} %stack.32, f32[768,1]{1,0:T(8,128)} %stack.33, f32[768,1]{1,0:T(8,128)} %stack.34, f32[768,1]{1,0:T(8,128)} %stack.35), dimensions={1} | concatenate | bytes 18997248 | tf_op jit(solution)/shard_map/concatenate | solution.py:59
  219.5 1.5 reshape.527
  221.0 11.3 %fusion.122 = f32[3072,768]{1,0:T(8,128)} fusion(bf16[528,768]{1,0:T(8,128)(2,1)S(1)} %copy-done.25, f32[528,3072]{1,0:T(8,128)} %copy-done.50), kind=kOutput, calls=%fused_computation.208 | convolution fusion | flops 2506014720 | bytes 16736256 | tf_op jit(solution)/shard_map/rf,rd->fd/dot_general | solution.py:193
  232.4 9.2 %reshape_reshape.7 = f32[8,294912]{1,0:T(8,128)} reshape(f32[3072,768]{1,0:T(8,128)} %fusion.122) | data formatting | bytes 18874368 | tf_op jit(solution)/shard_map/reshape;reshape | solution.py:47
  241.6 5.9 %convolution_bitcast_fusion = f32[1,8,768,384]{3,2,1,0:T(8,128)S(1)} fusion(bf16[528,768,1]{1,0,2:T(8,128)(2,1)S(1)} %reshape.527, bf16[66,8,8,384]{3,2,1,0:T(8,128)(2,1)} %bitcast.190), kind=kOutput, calls=%fused_computation.35 | convolution fusion | flops 2491416576 | bytes 13492224 | tf_op jit(solution)/shard_map/rd,rf->df/dot_general | solution.py:198
  247.5 9.3 %copy.280 = f32[1,8,768,384]{3,1,2,0:T(8,128)} copy(f32[1,8,768,384]{3,2,1,0:T(8,128)S(1)} %convolution_bitcast_fusion) | data formatting | bytes 18874368
  256.7 21.1 %reduce-scatter.7.cloned.1.call-done = f32[96,3092]{1,0:T(8,128)} async-done(((f32[768,3092]{1,0:T(8,128)}), f32[96,3092]{1,0:T(8,128)}) %reduce-scatter.7.cloned.1.call-update) | async-done | bytes 1187344
  281.6 17.2 %pad_maximum_fusion = f32[8,589824]{1,0:T(8,128)} fusion(f32[8,294912]{1,0:T(8,128)} %reshape_reshape.7, f32[8,294912]{1,0:T(8,128)} %bitcast.174), kind=kLoop, calls=%fused_computation.1 | loop fusion | flops 4718592 | bytes 37748736 | tf_op jit(solution)/shard_map/concatenate | solution.py:47
  298.7 15.8 %reshape.522 = f32[36864,128]{1,0:T(8,128)} reshape(f32[8,589824]{1,0:T(8,128)} %pad_maximum_fusion) | data formatting | bytes 37748736 | tf_op jit(solution)/shard_map/reshape | solution.py:49
  317.0 1.6 copy.248
  318.6 2.6 copy.240
  321.1 1.9 copy.252
  323.1 1.9 copy.251
  325.0 1.5 add_bitcast_fusion
  326.5 1.4 copy.256
  329.0 61.2 %all-reduce.1 = (f32[96,16]{0,1:T(8,128)S(1)}, f32[96,4]{0,1:T(4,128)S(1)}) all-reduce(f32[96,16]{0,1:T(8,128)S(1)} %copy.273, f32[96,4]{0,1:T(4,128)S(1)} %copy.274), channel_id=1, replica_groups=mesh['grp'=8,'exp'=16] {'exp'}, use_global_device_ids=true, to_apply=%region_29.30 | all-reduce | flops 1920 | bytes 15360 | tf_op jit(solution)/shard_map/psum | solution.py:240
  391.4 4.1 multiply_subtract_fusion.2
  395.5 2.6 copy.257
  398.1 2.7 copy.258
  405.1 69.4 %reduce-scatter.5.cloned.1.call-done = f32[4608,128]{1,0:T(8,128)} async-done(((f32[36864,128]{1,0:T(8,128)}), f32[4608,128]{1,0:T(8,128)}) %reduce-scatter.5.cloned.1.call-update) | async-done | bytes 2359312 | tf_op jit(solution)/shard_map/reduce_scatter | solution.py:50
  474.5 2.8 fusion.131
  477.6 1.6 broadcast_in_dim_reshape.8
  479.2 4.1 multiply_subtract_fusion.1
  483.3 2.3 multiply_subtract_fusion
  (215 shorter events, 47.5 us)
Async XLA Ops:
  7.2 5.1 %copy-start.7 = (f32[1,768,384]{2,1,0:T(8,128)S(1)}, f32[1,768,384]{2,1,0:T(8,128)}, u32[]{:S(2)}) copy-start(f32[1,768,384]{2,1,0:T(8,128)} %param.38) | copy-start | bytes 3538948
  7.2 5.3 %copy-start.9 = (f32[1,384,768]{2,1,0:T(8,128)S(1)}, f32[1,384,768]{2,1,0:T(8,128)}, u32[]{:S(2)}) copy-start(f32[1,384,768]{2,1,0:T(8,128)} %param.41) | copy-start | bytes 3538948
  7.2 43.9 %all-gather.3.cloned.1.call-start = ((), (), s32[]{:S(2)}) async-start(), calls=%async_computation.6 | async-start | bytes 5529600 | tf_op jit(solution)/shard_map/all_gather | solution.py:21
  12.2 107.4 %all-gather.5.cloned.1.call-start = ((), (), s32[]{:S(2)}) async-start(), calls=%async_computation.7 | async-start | bytes 10616832 | tf_op jit(solution)/shard_map/all_gather | solution.py:29
  12.5 1.2 copy-start.13
  13.8 2.4 copy-start.46
  13.8 4.9 %copy-start.15 = (f32[197,768]{1,0:T(8,128)}, f32[197,768]{1,0:T(8,128)S(1)}, u32[]{:S(2)}) copy-start(f32[197,768]{1,0:T(8,128)S(1)} %bitcast_convert_fusion) | copy-start | bytes 1815556
  13.8 2.7 copy-start.32
  13.8 5.9 %copy-start = (bf16[1,197,768]{2,1,0:T(8,128)(2,1)S(1)}, bf16[1,197,768]{2,1,0:T(8,128)(2,1)}, u32[]{:S(2)}) copy-start(bf16[1,197,768]{2,1,0:T(8,128)(2,1)} %param.22) | copy-start | bytes 907780
  19.8 36.2 %copy-start.34 = (s32[394]{0:T(512)}, s32[394]{0:T(512)S(1)}, u32[]{:S(2)}) copy-start(s32[394]{0:T(512)S(1)} %fusion.107) | copy-start | bytes 4732
  20.1 35.8 %copy-start.39 = (f32[197]{0:T(256)}, f32[197]{0:T(256)S(1)}, u32[]{:S(2)}) copy-start(f32[197]{0:T(256)S(1)} %fusion.69) | copy-start | bytes 2368
  56.6 1.0 copy-start.1
  61.6 5.0 %copy-start.28 = (bf16[12,64,197]{2,1,0:T(8,128)(2,1)}, bf16[12,64,197]{2,1,0:T(8,128)(2,1)S(1)}, u32[]{:S(2)}) copy-start(bf16[12,64,197]{2,1,0:T(8,128)(2,1)S(1)} %convolution_convert_fusion.3) | copy-start | bytes 907780
  63.8 0.6 copy-start.41
  63.9 0.6 copy-start.35
  64.6 0.7 copy-start.5
  66.6 0.6 copy-start.37
  75.6 22.6 %all-to-all-start.2 = ((bf16[16,33,768]{2,1,0:T(8,128)(2,1)}), bf16[16,33,768]{2,1,0:T(8,128)(2,1)}, u32[]{:S(2)}, u32[]{:S(2)}) async-start(bf16[16,33,768]{2,1,0:T(8,128)(2,1)} %reshape.515), calls=%async_computation.2 | async-start | bytes 1966080 | tf_op jit(solution)/shard_map/all_to_all | solution.py:191
  98.1 19.1 %all-to-all-start = ((bf16[16,33,768]{2,1,0:T(8,128)(2,1)}), bf16[16,33,768]{2,1,0:T(8,128)(2,1)}, u32[]{:S(2)}, u32[]{:S(2)}) async-start(bf16[16,33,768]{2,1,0:T(8,128)(2,1)} %reshape.510), calls=%async_computation | async-start | bytes 1966080 | tf_op jit(solution)/shard_map/all_to_all | solution.py:169
  119.6 5.0 %copy-start.26 = (bf16[528,768]{1,0:T(8,128)(2,1)S(1)}, bf16[528,768]{1,0:T(8,128)(2,1)}, u32[]{:S(2)}) copy-start(bf16[528,768]{1,0:T(8,128)(2,1)} %reshape.511) | copy-start | bytes 2433028
  119.6 5.6 %copy-start.49 = (bf16[3072,1536]{1,0:T(8,128)(2,1)S(1)}, bf16[3072,1536]{1,0:T(8,128)(2,1)}, u32[]{:S(2)}) copy-start(bf16[3072,1536]{1,0:T(8,128)(2,1)} %all-gather.5.cloned.1.call-done) | copy-start | bytes 28311556
  132.7 2.8 copy-start.50
  144.9 19.3 %all-to-all-start.3 = ((bf16[16,33,768]{2,1,0:T(8,128)(2,1)}), bf16[16,33,768]{2,1,0:T(8,128)(2,1)}, u32[]{:S(2)}, u32[]{:S(2)}) async-start(bf16[16,33,768]{2,1,0:T(8,128)(2,1)} %reshape.517), calls=%async_computation.3 | async-start | bytes 1966080 | tf_op jit(solution)/shard_map/all_to_all | solution.py:202
  159.0 9.7 %copy-start.38 = (f32[197]{0:T(256)S(1)}, f32[197]{0:T(256)}, u32[]{:S(2)}) copy-start(f32[197]{0:T(256)} %copy-done.37) | copy-start | bytes 2368
  164.3 17.5 %all-to-all-start.1 = ((bf16[16,33,768]{2,1,0:T(8,128)(2,1)}), bf16[16,33,768]{2,1,0:T(8,128)(2,1)}, u32[]{:S(2)}, u32[]{:S(2)}) async-start(bf16[16,33,768]{2,1,0:T(8,128)(2,1)} %reshape.512), calls=%async_computation.1 | async-start | bytes 1966080 | tf_op jit(solution)/shard_map/all_to_all | solution.py:176
  168.6 109.3 %reduce-scatter.7.cloned.1.call-start = ((), (), s32[]{:S(2)}) async-start(), calls=%async_computation.9 | async-start | bytes 11059200
  173.8 12.7 %copy-start.36 = (f32[197]{0:T(256)S(1)}, f32[197]{0:T(256)}, u32[]{:S(2)}) copy-start(f32[197]{0:T(256)} %copy-done.35) | copy-start | bytes 2368
  184.1 2.4 copy-start.27
  184.1 3.8 copy-start.42
  186.4 3.4 copy-start.14
  188.9 0.8 copy-start.3
  189.9 4.5 copy-start.20
  192.7 1.6 copy-start.2
  192.7 1.7 copy-start.30
  195.4 1.0 copy-start.21
  195.4 1.1 copy-start.29
  195.9 1.0 copy-start.6
  197.0 5.6 %slice-start.2 = ((s8[4915200]{0:T(1024)(128)(4,1)}), s8[720896]{0:T(1024)(128)(4,1)S(1)}, s32[]{:S(2)}) async-start(s8[4915200]{0:T(1024)(128)(4,1)} %bitcast.188), calls=%async_computation.13 | async-start | bytes 1441792
  198.3 4.3 slice-start.3
  202.6 1.4 copy-start.40
  204.0 15.3 %copy-start.16 = (f32[197,768]{1,0:T(8,128)}, f32[197,768]{1,0:T(8,128)S(1)}, u32[]{:S(2)}) copy-start(f32[197,768]{1,0:T(8,128)S(1)} %get-tuple-element.169) | copy-start | bytes 1815556
  219.3 1.7 copy-start.25
  219.3 172.1 %all-reduce.5.cloned.1.call-start = ((), (), s32[]{:S(2)}) async-start(), calls=%async_computation.10 | async-start | bytes 3145728 | tf_op jit(solution)/shard_map/psum | solution.py:240
  277.9 2.7 slice-start
  281.5 193.0 %reduce-scatter.5.cloned.1.call-start = ((), (), s32[]{:S(2)}) async-start(), calls=%async_computation.8 | async-start | bytes 21233664 | tf_op jit(solution)/shard_map/reduce_scatter | solution.py:50
  314.5 1.2 copy-start.12
  314.5 1.5 copy-start.22
  317.0 8.0 %copy-start.4 = (f32[197,768]{1,0:T(8,128)S(1)}, f32[197,768]{1,0:T(8,128)}, u32[]{:S(2)}) copy-start(f32[197,768]{1,0:T(8,128)} %copy-done.3) | copy-start | bytes 1815556
  321.1 6.8 %slice-start.1 = ((f32[96,3092]{1,0:T(8,128)}), f32[96,16]{1,0:T(8,128)S(1)}, s32[]{:S(2)}) async-start(f32[96,3092]{1,0:T(8,128)} %reduce-scatter.7.cloned.1.call-done), calls=%async_computation.12 | async-start | bytes 98304 | tf_op jit(solution)/shard_map/slice | solution.py:62
  323.0 67.1 %copy-start.45 = (f32[96,4]{0,1:T(4,128)S(1)}, f32[96,4]{0,1:T(4,128)}, u32[]{:S(2)}) copy-start(f32[96,4]{0,1:T(4,128)} %param.35) | copy-start | bytes 4612
  323.0 67.1 %copy-start.47 = (f32[96,4]{0,1:T(4,128)S(1)}, f32[96,4]{0,1:T(4,128)}, u32[]{:S(2)}) copy-start(f32[96,4]{0,1:T(4,128)} %param.37) | copy-start | bytes 4612
  323.0 67.1 %copy-start.48 = (f32[96,4]{0,1:T(4,128)S(1)}, f32[96,4]{0,1:T(4,128)}, u32[]{:S(2)}) copy-start(f32[96,4]{0,1:T(4,128)} %param.36) | copy-start | bytes 4612
  323.0 67.7 %copy-start.33 = (f32[96,16]{0,1:T(8,128)S(1)}, f32[96,16]{0,1:T(8,128)}, u32[]{:S(2)}) copy-start(f32[96,16]{0,1:T(8,128)} %param.32) | copy-start | bytes 18436
  323.0 67.7 %copy-start.43 = (f32[96,16]{0,1:T(8,128)S(1)}, f32[96,16]{0,1:T(8,128)}, u32[]{:S(2)}) copy-start(f32[96,16]{0,1:T(8,128)} %param.34) | copy-start | bytes 18436
  323.1 67.7 %copy-start.44 = (f32[96,16]{0,1:T(8,128)S(1)}, f32[96,16]{0,1:T(8,128)}, u32[]{:S(2)}) copy-start(f32[96,16]{0,1:T(8,128)} %param.33) | copy-start | bytes 18436
  395.5 5.4 %copy-start.11 = (f32[96,2304]{0,1:T(8,128)S(1)}, f32[96,2304]{0,1:T(8,128)}, u32[]{:S(2)}) copy-start(f32[96,2304]{0,1:T(8,128)} %get-tuple-element.152) | copy-start | bytes 2654212
  398.1 4.0 copy-start.17
  398.1 4.0 copy-start.18
  398.1 4.0 copy-start.19
  398.1 4.0 copy-start.31
  477.3 1.9 copy-start.8
  479.2 4.2 copy-start.10
  479.2 4.1 copy-start.23
  479.2 4.1 copy-start.24
Sparse Core Ops, SparseCore 0:
  12.4 38.7 all-gather.2
  53.4 54.0 all-gather.4
  219.4 58.4 reduce-scatter.6
  282.7 87.6 all-reduce.4
  372.8 101.6 reduce-scatter.4
where the time goes:
time: 503 us; the launch traced here: 493 us
  waiting for transfers between devices  146 us (29%)
  local copies, waits for them, and re-layouts  125 us (25%)
  matrix products  78 us (16%)
  blocking collectives  61.2 us (12%)
  other arithmetic  46 us (9%)
  starting transfers between devices  21.1 us (4%)
  between operations  15.1 us (3%)
    reduce_scatter x1, waiting for transfers between devices, sum_together(): lax.psum_scatter(lines, axis, tiled=True).reshape(-1)  69.4 us
    psum x1, blocking collectives, on_device(): owned = lax.psum((shares[0], shares[1], shares[2], shares[3]), 'exp')  61.2 us
    unnamed x126, local copies, waits for them, and re-layouts  40.6 us
    all_gather x1, waiting for transfers between devices, in_one_piece(): result = lax.all_gather(both, axis, axis=dim, tiled=True)  30.4 us
    unnamed x6, waiting for transfers between devices  21.2 us
    concatenate x1, other arithmetic, sum_together(): lines = jnp.concatenate([b.reshape(peers, -1) for b in blocks], axis=1)  17.2 us
    reshape x1, local copies, waits for them, and re-layouts, sum_together(): jnp.pad(lines, ((0, 0), (0, extent * 128 - lines.shape[1])))  15.8 us
    sub x6, other arithmetic, adamw(): master - rate * (corrected / scaled + weight_decay * master)  12.1 us
  transfers between devices with their start and end apart: 9, of which 7 were waited for; matrix products, arithmetic and copies ran while one was open for 33% of the time, Pallas kernels for 0%

commit v1 on v0

v1 whole, which is shorter than its diff:
```python
import jax
import jax.numpy as jnp
from jax import lax
from jax.experimental import pallas as pl
from jax.experimental.pallas import tpu as pltpu
from jax.sharding import PartitionSpec as P

HEADS = 12
HEAD_DIM = 64
STEP = 10
D = 768
TOK = 197
ROWS = 208
EXPERTS = 16
CAP = 40
SLOTS = EXPERTS * CAP
DENSE = 3200
GRP = 8
OWN = D // GRP
PIECE = 48
WIDE = 384
HID = 384

norm_epsilon = 1e-06
beta_first = 0.9
beta_second = 0.999
adam_epsilon = 1e-08
weight_decay = 0.1
score_scale = HEAD_DIM ** (-0.5)
low = jnp.bfloat16
full = jnp.float32


def dot(a, b, dims=((1,), (0,))):
    return lax.dot_general(a, b, (dims, ((), ())), preferred_element_type=jnp.float32)


NT = ((1,), (1,))
TN = ((0,), (0,))


def unit_rows(values):
    centered = values - jnp.mean(values, axis=-1, keepdims=True)
    variance = jnp.mean(centered * centered, axis=-1, keepdims=True)
    scale = lax.rsqrt(variance + norm_epsilon)
    return centered * scale, scale


def norm_rows(w_ref):
    return w_ref[:, 3072:3200].astype(full).T[16:24]


def lanes(shape):
    return lax.broadcasted_iota(jnp.int32, shape, 1)


def half_masks():
    lane = lanes((1, 128))
    first = (lane < HEAD_DIM).astype(full)
    return first.astype(low), (1.0 - first).astype(low)


def forward_kernel(
    x_ref, g_ref, w_ref, ids_ref, keep_ref, trow_ref,
    send_ref, m_ref, a_ref, qkv_ref, p_ref, o_ref, c_ref, r_ref,
    x_pad, g_pad,
):
    x_pad[192:ROWS, :] = jnp.zeros((ROWS - 192, D), full)
    x_pad[0:TOK, :] = x_ref[0].astype(full)
    g_pad[192:ROWS, :] = jnp.zeros((ROWS - 192, D), full)
    g_pad[0:TOK, :] = g_ref[0].astype(full)
    norms = norm_rows(w_ref)
    x = x_pad[...]
    a = (unit_rows(x)[0] * norms[0:1] + norms[1:2]).astype(low)
    a_ref[...] = a
    for part in range(3):
        cols = slice(part * D, part * D + D)
        qkv_ref[:, cols] = dot(a, w_ref[:, cols]).astype(low)
    first, second = half_masks()
    seen = lanes((ROWS, ROWS)) < TOK
    low_half = lanes((ROWS, 128)) < HEAD_DIM
    for pair in range(HEADS // 2):
        at = pair * 128
        q = qkv_ref[:, at : at + 128]
        k = qkv_ref[:, D + at : D + at + 128]
        v = qkv_ref[:, 2 * D + at : 2 * D + at + 128]
        mixed = []
        for side, mask in enumerate((first, second)):
            s = dot(q * mask, k, NT) * score_scale
            s = jnp.where(seen, s, -1e30)
            e = jnp.exp(s - jnp.max(s, axis=1, keepdims=True))
            p = (e / jnp.sum(e, axis=1, keepdims=True)).astype(low)
            p_ref[2 * pair + side] = p
            mixed.append(dot(p, v))
        o_ref[:, at : at + 128] = jnp.where(low_half, mixed[0], mixed[1]).astype(low)
    m = x + dot(o_ref[...], w_ref[:, 2304:3072])
    m_ref[...] = m
    c = (unit_rows(m)[0] * norms[2:3] + norms[3:4]).astype(low)
    c_ref[...] = c
    lane = lanes((ROWS, 128))
    logits = jnp.where(lane < EXPERTS, dot(c, w_ref[:, 3072:3200]), -1e30)
    e = jnp.exp(logits - jnp.max(logits, axis=1, keepdims=True))
    r = e / jnp.sum(e, axis=1, keepdims=True)
    r_ref[...] = r
    slot = lax.broadcasted_iota(jnp.int32, (SLOTS, ROWS), 0)
    g = g_pad[...]
    picks, grads = [], []
    for j in range(2):
        chosen = lane == ids_ref[:, j : j + 1]
        gate = jnp.sum(jnp.where(chosen, r, 0.0), axis=1, keepdims=True) * keep_ref[:, j : j + 1]
        picks.append((slot == trow_ref[j : j + 1, :]).astype(full).astype(low))
        grads.append((gate * g).astype(low))
    send_ref[:, 0:D] = dot(picks[0] + picks[1], c).astype(low)
    send_ref[:, D:] = (dot(picks[0], grads[0]) + dot(picks[1], grads[1])).astype(low)


def expert_kernel(got_ref, w_ref, back_ref, grad_ref, z_sum, dx_sum, xt, dzt):
    step = pl.program_id(0)

    @pl.when(step == 0)
    def _():
        xt[...] = got_ref[:, 0:D].T
        dzt[...] = got_ref[:, D:].T
        z_sum[...] = jnp.zeros_like(z_sum)
        dx_sum[...] = jnp.zeros_like(dx_sum)

    wi = jnp.concatenate([w_ref[0:D, 0:HID], w_ref[D:, 0:HID]], axis=1)
    wot = jnp.concatenate([w_ref[0:D, HID:], w_ref[D:, HID:]], axis=1)
    u = dot(got_ref[:, 0:D], wi)
    dh = dot(got_ref[:, D:], wot)
    square = u * u
    inner = u * (0.7978845608028654 + (0.7978845608028654 * 0.044715) * square)
    t = jnp.tanh(inner)
    half = 0.5 * t + 0.5
    h = (u * half).astype(low)
    slope = (0.5 * u) * (1.0 - t * t)
    slope = slope * (0.7978845608028654 + (3 * 0.7978845608028654 * 0.044715) * square) + half
    du = (slope * dh).astype(low)
    z_sum[...] += dot(h, wot, NT)
    dx_sum[...] += dot(du, wi, NT)
    gi = dot(xt[...], du).astype(low)
    got_grad = dot(dzt[...], h).astype(low)
    grad_ref[0:D, 0:HID] = gi[:, 0:HID]
    grad_ref[D:, 0:HID] = gi[:, HID:]
    grad_ref[0:D, HID:] = got_grad[:, 0:HID]
    grad_ref[D:, HID:] = got_grad[:, HID:]

    @pl.when(step == pl.num_programs(0) - 1)
    def _():
        back_ref[:, 0:D] = z_sum[...].astype(low)
        back_ref[:, D:] = dx_sum[...].astype(low)


def spread(grad, first_group, out_ref):
    for g in range(GRP):
        for r in range(2):
            rows = slice(g * OWN + r * PIECE, g * OWN + (r + 1) * PIECE)
            for k in range(grad.shape[1] // WIDE):
                at = ((g * 2 + r) * 8 + first_group + k) * PIECE
                out_ref[at : at + PIECE, :] = grad[rows, k * WIDE : (k + 1) * WIDE]


def backward_kernel(
    back_ref, x_ref, g_ref, w_ref, ids_ref, tcol_ref,
    m_ref, a_ref, qkv_ref, p_ref, o_ref, c_ref, r_ref, keep_ref,
    result_ref, image_ref, grads_ref, extra_ref,
    x_pad, g_pad, dqkv,
):
    x_pad[192:ROWS, :] = jnp.zeros((ROWS - 192, D), full)
    x_pad[0:TOK, :] = x_ref[0].astype(full)
    g_pad[192:ROWS, :] = jnp.zeros((ROWS - 192, D), full)
    g_pad[0:TOK, :] = g_ref[0].astype(full)
    norms = norm_rows(w_ref)
    g = g_pad[...]
    m = m_ref[...]
    r = r_ref[...]
    lane = lanes((ROWS, 128))
    slot = lanes((ROWS, SLOTS))
    z = back_ref[:, 0:D]
    total = m
    dr = jnp.zeros((ROWS, 128), full)
    picks = []
    for j in range(2):
        pick = (slot == tcol_ref[:, j : j + 1]).astype(full).astype(low)
        picks.append(pick)
        keep = keep_ref[:, j : j + 1]
        chosen = lane == ids_ref[:, j : j + 1]
        gate = jnp.sum(jnp.where(chosen, r, 0.0), axis=1, keepdims=True) * keep
        zj = dot(pick, z)
        total = total + gate * zj
        dgate = jnp.sum(g * zj, axis=1, keepdims=True) * keep
        dr = dr + jnp.where(chosen, dgate, 0.0)
    result_ref[0] = total[0:TOK].astype(low)
    dl = (r * (dr - jnp.sum(dr * r, axis=1, keepdims=True))).astype(low)
    c = c_ref[...]
    extra_ref[0:16, :] = dot(dl, c, TN)[0:16]
    dc = dot(dl, w_ref[:, 3072:3200], NT) + dot(picks[0] + picks[1], back_ref[:, D:])
    xh, scale = unit_rows(m)
    dn2 = jnp.sum(dc * xh, axis=0, keepdims=True)
    dn3 = jnp.sum(dc, axis=0, keepdims=True)
    dxh = dc * norms[2:3]
    dm = g + scale * (
        dxh
        - jnp.mean(dxh, axis=1, keepdims=True)
        - xh * jnp.mean(dxh * xh, axis=1, keepdims=True)
    )
    dmb = dm.astype(low)
    spread(dot(o_ref[...].T, dmb).astype(low), 6, grads_ref)
    do = dot(dmb, w_ref[:, 2304:3072], NT).astype(low)
    first, second = half_masks()
    low_half = lane < HEAD_DIM
    for pair in range(HEADS // 2):
        at = pair * 128
        q = qkv_ref[:, at : at + 128]
        k = qkv_ref[:, D + at : D + at + 128]
        v = qkv_ref[:, 2 * D + at : 2 * D + at + 128]
        dop = do[:, at : at + 128]
        parts = []
        for side, mask in enumerate((first, second)):
            p_low = p_ref[2 * pair + side]
            p = p_low.astype(full)
            dp = dot(dop * mask, v, NT)
            ds = (p * (dp - jnp.sum(dp * p, axis=1, keepdims=True))).astype(low)
            parts.append((dot(ds, k), dot(ds, q, TN), dot(p_low, dop, TN)))
        for which, factor in enumerate((score_scale, score_scale, 1.0)):
            both = jnp.where(low_half, parts[0][which], parts[1][which]) * factor
            dqkv[:, which * D + at : which * D + at + 128] = both.astype(low)
    at_rows = a_ref[...].T
    da = jnp.zeros((ROWS, D), full)
    for part in range(3):
        cols = slice(part * D, part * D + D)
        spread(dot(at_rows, dqkv[:, cols]).astype(low), 2 * part, grads_ref)
        da = da + dot(dqkv[:, cols], w_ref[:, cols], NT)
    xh, scale = unit_rows(x_pad[...])
    extra_ref[16:24, :] = jnp.concatenate(
        [
            jnp.sum(da * xh, axis=0, keepdims=True),
            jnp.sum(da, axis=0, keepdims=True),
            dn2,
            dn3,
            jnp.zeros((4, D), full),
        ],
        axis=0,
    )
    dxh = da * norms[0:1]
    dx = dm + scale * (
        dxh
        - jnp.mean(dxh, axis=1, keepdims=True)
        - xh * jnp.mean(dxh * xh, axis=1, keepdims=True)
    )
    image_ref[0] = dx[0:TOK]


def adamw(master, first, second, gradient, rate):
    first = beta_first * first + (1.0 - beta_first) * gradient
    second = beta_second * second + (1.0 - beta_second) * gradient * gradient
    corrected = first / (1.0 - beta_first**STEP)
    scaled = jnp.sqrt(second / (1.0 - beta_second**STEP)) + adam_epsilon
    return (first, second, master - rate * (corrected / scaled + weight_decay * master))


def owner_kernel(*refs):
    pieces, inputs, outputs = refs[0], refs[1:7], refs[7:13]
    for r in range(2):
        rows = slice(r * PIECE, (r + 1) * PIECE)
        for k in range(8):
            piece = pieces[(r * 8 + k) * PIECE : (r * 8 + k + 1) * PIECE, :].astype(full)
            side, group, rate = (0, k, 0.04) if k < 6 else (3, k - 6, 0.2)
            cols = slice(group * WIDE, (group + 1) * WIDE)
            new = adamw(*[inputs[side + i][rows, cols] for i in range(3)], piece, rate)
            for i in range(3):
                outputs[side + i][rows, cols] = new[i]


def shape(*dims, dtype=jnp.float32):
    return jax.ShapeDtypeStruct(dims, dtype)


def in_vmem(count):
    return [pl.BlockSpec(memory_space=pltpu.VMEM)] * count


def params(mib):
    return pltpu.CompilerParams(vmem_limit_bytes=mib * 2**20)


def token_forward(*args):
    return pl.pallas_call(
        forward_kernel,
        out_shape=(
            shape(SLOTS, 2 * D, dtype=low),
            shape(ROWS, D),
            shape(ROWS, D, dtype=low),
            shape(ROWS, 3 * D, dtype=low),
            shape(HEADS, ROWS, ROWS, dtype=low),
            shape(ROWS, D, dtype=low),
            shape(ROWS, D, dtype=low),
            shape(ROWS, 128),
        ),
        in_specs=in_vmem(6),
        out_specs=tuple(in_vmem(8)),
        scratch_shapes=[pltpu.VMEM((ROWS, D), full)] * 2,
        compiler_params=params(40),
        cost_estimate=pl.CostEstimate(
            flops=4 * 10**9, bytes_accessed=12 * 10**6, transcendentals=10**6
        ),
        name="token_forward",
    )(*args)


def experts_both_ways(got, weights):
    return pl.pallas_call(
        expert_kernel,
        grid=(GRP // 2,),
        out_shape=(shape(SLOTS, 2 * D, dtype=low), shape(GRP * D, D, dtype=low)),
        in_specs=[
            pl.BlockSpec((SLOTS, 2 * D), lambda i: (0, 0)),
            pl.BlockSpec((2 * D, D), lambda i: (i, 0)),
        ],
        out_specs=(
            pl.BlockSpec((SLOTS, 2 * D), lambda i: (0, 0)),
            pl.BlockSpec((2 * D, D), lambda i: (i, 0)),
        ),
        scratch_shapes=[
            pltpu.VMEM((SLOTS, D), full),
            pltpu.VMEM((SLOTS, D), full),
            pltpu.VMEM((D, SLOTS), low),
            pltpu.VMEM((D, SLOTS), low),
        ],
        compiler_params=params(52),
        cost_estimate=pl.CostEstimate(
            flops=18 * 10**9, bytes_accessed=23 * 10**6, transcendentals=2 * 10**6
        ),
        name="experts",
    )(got, weights)


def token_backward(*args):
    return pl.pallas_call(
        backward_kernel,
        out_shape=(
            shape(1, TOK, D, dtype=low),
            shape(1, TOK, D),
            shape(GRP * 16 * PIECE, WIDE, dtype=low),
            shape(24, D),
        ),
        in_specs=in_vmem(14),
        out_specs=tuple(in_vmem(4)),
        scratch_shapes=[
            pltpu.VMEM((ROWS, D), full),
            pltpu.VMEM((ROWS, D), full),
            pltpu.VMEM((ROWS, 3 * D), low),
        ],
        compiler_params=params(48),
        cost_estimate=pl.CostEstimate(
            flops=7 * 10**9, bytes_accessed=18 * 10**6, transcendentals=10**4
        ),
        name="token_backward",
    )(*args)


def owner_step(pieces, arrays):
    return pl.pallas_call(
        owner_kernel,
        out_shape=tuple(shape(*a.shape) for a in arrays),
        in_specs=in_vmem(7),
        out_specs=tuple(in_vmem(6)),
        compiler_params=params(24),
        cost_estimate=pl.CostEstimate(
            flops=10**7, bytes_accessed=8 * 10**6, transcendentals=10**6
        ),
        name="owner_step",
    )(pieces, *arrays)


def on_device(
    images,
    cotangent,
    expert_ids,
    kept_routes,
    qkv_master,
    qkv_first,
    qkv_second,
    proj_master,
    proj_first,
    proj_second,
    router_master,
    router_first,
    router_second,
    norm_master,
    norm_first,
    norm_second,
    inner_master,
    inner_first,
    inner_second,
    outer_master,
    outer_first,
    outer_second,
):
    dense = jnp.concatenate(
        [
            qkv_master.astype(low),
            proj_master.astype(low),
            router_master.astype(low),
            norm_master.astype(low),
            jnp.zeros((OWN, DENSE - 3092), low),
        ],
        axis=1,
    )
    dense = lax.all_gather(dense, "grp", axis=0, tiled=True)
    mine = jnp.concatenate([inner_master[0].astype(low), outer_master[0].astype(low).T], axis=1)
    weights = lax.all_gather(mine, "grp", axis=0, tiled=True)

    ids = expert_ids.reshape(TOK, 2)
    kept = kept_routes.reshape(TOK, 2)
    flat = ids.reshape(-1)
    marks = (flat[:, None] == jnp.arange(EXPERTS, dtype=jnp.int32)[None, :]).astype(jnp.int32)
    slots = jnp.sum((jnp.cumsum(marks, axis=0) - marks) * marks, axis=1).reshape(TOK, 2)
    target = jnp.where(kept > 0, ids * CAP + slots, -1)
    padding = ((0, ROWS - TOK), (0, 0))
    target = jnp.pad(target, padding, constant_values=-1)
    ids = jnp.pad(ids, padding, constant_values=-1)
    keep = jnp.pad(kept.astype(full), padding)

    send, m, a, qkv, p, o, c, r = token_forward(images, cotangent, dense, ids, keep, target.T)
    got = lax.all_to_all(
        send.reshape(EXPERTS, CAP, 2 * D), "exp", split_axis=0, concat_axis=0, tiled=True
    )
    back, expert_grads = experts_both_ways(got.reshape(SLOTS, 2 * D), weights)
    expert_grads = lax.psum_scatter(expert_grads, "grp", scatter_dimension=0, tiled=True)
    back = lax.all_to_all(
        back.reshape(EXPERTS, CAP, 2 * D), "exp", split_axis=0, concat_axis=0, tiled=True
    )
    result, image_grad, grads, extra = token_backward(
        back.reshape(SLOTS, 2 * D), images, cotangent, dense, ids, target,
        m, a, qkv, p, o, c, r, keep,
    )
    grads = lax.psum_scatter(grads, "grp", scatter_dimension=0, tiled=True)

    extra = jnp.moveaxis(extra.reshape(24, GRP, OWN), 1, 0)
    extra = lax.all_to_all(extra, "grp", split_axis=0, concat_axis=0, tiled=True)
    extra = jnp.broadcast_to(jnp.sum(extra, axis=0)[None], (EXPERTS, 24, OWN))
    extra = lax.all_to_all(extra, "exp", split_axis=0, concat_axis=0, tiled=True)
    extra = jnp.sum(extra, axis=0).T

    pieces = lax.all_to_all(
        grads.reshape(16, PIECE, WIDE), "exp", split_axis=0, concat_axis=0, tiled=True
    )
    piece = jnp.sum(pieces.astype(full), axis=0).astype(low)
    pieces = lax.all_to_all(
        jnp.broadcast_to(piece[None], (16, PIECE, WIDE)),
        "exp",
        split_axis=0,
        concat_axis=0,
        tiled=True,
    )
    qkv_moment, qkv_square, qkv_weight, proj_moment, proj_square, proj_weight = owner_step(
        pieces.reshape(16 * PIECE, WIDE),
        (qkv_master, qkv_first, qkv_second, proj_master, proj_first, proj_second),
    )
    router_moment, router_square, router_weight = adamw(
        router_master, router_first, router_second, extra[:, 0:16], 0.03
    )
    norm_moment, norm_square, norm_weight = adamw(
        norm_master, norm_first, norm_second, extra[:, 16:20], 0.3
    )
    inner_grad = expert_grads[:, 0:HID].astype(full)
    outer_grad = expert_grads[:, HID:].T.astype(full)
    inner_moment, inner_square, inner_weight = adamw(
        inner_master, inner_first, inner_second, inner_grad[None], 0.04
    )
    outer_moment, outer_square, outer_weight = adamw(
        outer_master, outer_first, outer_second, outer_grad[None], 0.15
    )
    return (
        result,
        image_grad,
        qkv_moment,
        qkv_square,
        qkv_weight,
        proj_moment,
        proj_square,
        proj_weight,
        router_moment,
        router_square,
        router_weight,
        norm_moment,
        norm_square,
        norm_weight,
        inner_moment,
        inner_square,
        inner_weight,
        outer_moment,
        outer_square,
        outer_weight,
    )


def solution(mesh):
    in_specs = (
        P(("grp", "exp"), None, None),
        P(("grp", "exp"), None, None),
        P(("grp", "exp"), None, None),
        P(("grp", "exp"), None, None),
        P("grp", None),
        P("grp", None),
        P("grp", None),
        P("grp", None),
        P("grp", None),
        P("grp", None),
        P("grp", None),
        P("grp", None),
        P("grp", None),
        P("grp", None),
        P("grp", None),
        P("grp", None),
        P("exp", None, "grp"),
        P("exp", None, "grp"),
        P("exp", None, "grp"),
        P("exp", "grp", None),
        P("exp", "grp", None),
        P("exp", "grp", None),
    )
    out_specs = (
        P(("grp", "exp"), None, None),
        P(("grp", "exp"), None, None),
        P("grp", None),
        P("grp", None),
        P("grp", None),
        P("grp", None),
        P("grp", None),
        P("grp", None),
        P("grp", None),
        P("grp", None),
        P("grp", None),
        P("grp", None),
        P("grp", None),
        P("grp", None),
        P("exp", None, "grp"),
        P("exp", None, "grp"),
        P("exp", None, "grp"),
        P("exp", "grp", None),
        P("exp", "grp", None),
        P("exp", "grp", None),
    )
    return jax.shard_map(
        on_device, mesh=mesh, in_specs=in_specs, out_specs=out_specs, check_vma=False
    )
```

time: 503 us -> 295 us (0.59); the launches traced: 493 us -> 294 us
  local copies, waits for them, and re-layouts: 125 us -> 27.4 us
  matrix products: 78 us -> 0 us
  Pallas kernels: 0 us -> 47 us
  waiting for transfers between devices: 146 us -> 99.8 us
  other arithmetic: 46 us -> 15.8 us
  blocking collectives: 61.2 us -> 76.3 us
  starting transfers between devices: 21.1 us -> 13 us
    dot_general x25 -> x0, matrix products: 78 us -> none  [the longest x1 11.3 us: on_device(): jnp.einsum('rf,rd->fd', active, back_gathered, preferred_element_type=jnp...]
    all_to_all x0 -> x3, blocking collectives: none -> 76.3 us  [the longest x1 33 us: on_device(): lax.all_to_all(back.reshape(EXPERTS, CAP, 2 * D), 'exp', split_axis=0, co...]
    psum x1 -> x0, blocking collectives: 61.2 us -> none  [on_device(): owned = lax.psum((shares[0], shares[1], shares[2], shares[3]), 'exp')]
    pallas_call x0 -> x4, Pallas kernels: none -> 47 us  [the longest x1 25.2 us: experts_both_ways(): pl.pallas_call(expert_kernel, grid=(GRP // 2,), out_shape=(shape(SLOTS, 2...]
    reshape x11 -> x3, local copies, waits for them, and re-layouts: 38.9 us -> 0.26 us  [the longest x1 0.14 us: on_device(): jnp.sum((jnp.cumsum(marks, axis=0) - marks) * marks, axis=1).reshape(TOK, 2)]
    reduce_scatter x1 -> x2, waiting for transfers between devices: 69.4 us -> 37.2 us  [the longest x1 23.6 us: on_device(): grads = lax.psum_scatter(grads, 'grp', scatter_dimension=0, tiled=True)]
    unnamed x6 -> x4, waiting for transfers between devices: 21.2 us -> 0.57 us
    concatenate x2 -> x1, other arithmetic: 18.3 us -> 1.11 us  [on_device(): jnp.concatenate([inner_master[0].astype(low), outer_master[0].astype(low)...]
  transfers between devices with their start and end apart: 9 -> 7, of which waited for: 7 -> 6; matrix products, arithmetic and copies ran while one was open for 33% -> 5% of each run, Pallas kernels for 0% -> 3%
where the time goes in v1:
time: 295 us; the launch traced here: 294 us
  waiting for transfers between devices  99.8 us (34%)
  blocking collectives  76.3 us (26%)
  Pallas kernels  47 us (16%)
  local copies, waits for them, and re-layouts  27.4 us (9%)
  other arithmetic  15.8 us (5%)
  between operations  14.2 us (5%)
  starting transfers between devices  13 us (4%)
    all_to_all x1, blocking collectives, on_device(): lax.all_to_all(back.reshape(EXPERTS, CAP, 2 * D), 'exp', split_axis=0, co...  33 us
    all_gather x1, waiting for transfers between devices, on_device(): dense = lax.all_gather(dense, 'grp', axis=0, tiled=True)  32.9 us
    all_to_all x1, blocking collectives, on_device(): lax.all_to_all(send.reshape(EXPERTS, CAP, 2 * D), 'exp', split_axis=0, co...  32.9 us
    pallas_call x1, Pallas kernels, experts_both_ways(): pl.pallas_call(expert_kernel, grid=(GRP // 2,), out_shape=(shape(SLOTS, 2...  25.2 us
    unnamed x69, local copies, waits for them, and re-layouts  23.9 us
    reduce_scatter x1, waiting for transfers between devices, on_device(): grads = lax.psum_scatter(grads, 'grp', scatter_dimension=0, tiled=True)  23.6 us
    pallas_call x1, Pallas kernels, token_backward(): pl.pallas_call(backward_kernel, out_shape=(shape(1, TOK, D, dtype=low), s...  14.1 us
    reduce_scatter x1, waiting for transfers between devices, on_device(): lax.psum_scatter(expert_grads, 'grp', scatter_dimension=0, tiled=True)  13.6 us
  transfers between devices with their start and end apart: 7, of which 6 were waited for; matrix products, arithmetic and copies ran while one was open for 5% of the time, Pallas kernels for 3%

profile of v1, /device:TPU:1, one launch (start us, length us, event | category | flops | bytes accessed | tf_op | source)
XLA Modules:
  0.0 293.6 jit_solution(2695370459862629268)
XLA Ops:
  7.2 0.0 all-gather.3.cloned.1.call-start
  7.3 1.3 convert_element_type.47
  8.6 0.1 copy.94
  8.7 0.1 copy.95
  8.9 1.0 concatenate.6
  9.8 0.0 all-gather.3.cloned.1.call-update
  9.9 0.0 all-gather.5.cloned.1.call-start
  9.9 0.4 copy.103
  10.3 0.1 convert_bitcast_fusion
  10.4 1.6 copy-done.21
  12.0 0.1 convert_bitcast_fusion.1
  12.1 1.1 pad_maximum_fusion
  13.2 0.0 reduce-scatter.3.cloned.1.call-start
  13.3 0.6 copy-done.28
  13.9 0.1 copy.96
  14.0 0.1 eq.22
  14.2 1.2 reduce-window.6
  15.3 0.2 slice_reduce_fusion
  15.6 0.1 bitcast_bitcast_fusion
  15.7 0.1 reshape.96
  15.9 0.1 copy.97
  16.0 0.1 copy.102.trow_ref
  16.2 32.9 %all-gather.3.cloned.1.call-done.w_ref = bf16[768,3200]{1,0:T(8,128)(2,1)} async-done(((bf16[96,3200]{1,0:T(8,128)(2,1)}), bf16[768,3200]{1,0:T(8,128)(2,1)}) %all-gather.3.cloned.1.call-update) | async-done | bytes 4915216 | tf_op jit(solution)/shard_map/all_gather | solution.py:410
  49.1 2.4 copy-done.7
  51.5 4.8 %token_forward.1 = (bf16[640,1536]{1,0:T(8,128)(2,1)S(1)}, f32[208,768]{1,0:T(8,128)S(1)}, bf16[208,768]{1,0:T(8,128)(2,1)S(1)}, bf16[208,2304]{1,0:T(8,128)(2,1...) custom-call(bf16[1,197,768]{2,1,0:T(8,128)(2,1)S(1)} %copy-done.8, ...), custom_call_target="tpu_custom_call" | custom-call | flops 4000000000 | bytes 12000000 | tf_op jit(solution)/shard_map/token_forward/pallas_call | solution.py:288
  56.3 0.8 copy-done.10
  57.1 0.7 copy-done.12
  57.9 0.7 copy-done.14
  58.6 0.7 copy-done.16
  59.3 0.6 copy-done.18
  60.0 32.9 %all_to_all.30 = bf16[16,40,1536]{2,1,0:T(8,128)(2,1)} all-to-all(bf16[16,40,1536]{2,1,0:T(8,128)(2,1)S(1)} %bitcast.62), channel_id=1, replica_groups=mesh['grp'=8,'exp'=16] {'exp'}, dimensions={0} | all-to-all | bytes 3932160 | tf_op jit(solution)/shard_map/all_to_all | solution.py:426
  92.8 12.6 %all-gather.5.cloned.1.call-done.w_ref = bf16[6144,768]{1,0:T(8,128)(2,1)} async-done(((bf16[768,768]{1,0:T(8,128)(2,1)}), bf16[6144,768]{1,0:T(8,128)(2,1)}) %all-gather.5.cloned.1.call-update) | async-done | bytes 9437200 | tf_op jit(solution)/shard_map/all_gather | solution.py:412
  105.5 25.2 %experts.1 = (bf16[640,1536]{1,0:T(8,128)(2,1)S(1)}, bf16[6144,768]{1,0:T(8,128)(2,1)}) custom-call(bf16[640,1536]{1,0:T(8,128)(2,1)} %bitcast.65, bf16[6144,768]{1,0:T(8,128)(2,1)} %all-gather.5.cloned.1.call-done.w_ref), custom_call_target="tpu_custom_call" | custom-call | flops 17999998976 | bytes 23000000 | tf_op jit(solution)/shard_map/experts/pallas_call | solution.py:312
  130.8 33.0 %all_to_all.31 = bf16[16,40,1536]{2,1,0:T(8,128)(2,1)} all-to-all(bf16[16,40,1536]{2,1,0:T(8,128)(2,1)S(1)} %bitcast.63), channel_id=1, replica_groups=mesh['grp'=8,'exp'=16] {'exp'}, dimensions={0} | all-to-all | bytes 3932160 | tf_op jit(solution)/shard_map/all_to_all | solution.py:431
  163.8 14.1 %token_backward.1 = (bf16[1,197,768]{2,1,0:T(8,128)(2,1)}, f32[1,197,768]{2,1,0:T(8,128)S(1)}, bf16[6144,384]{1,0:T(8,128)(2,1)}, f32[24,768]{1,0:T(8,128)S(1)}) custom-call(bf16[640,1536]{1,0:T(8,128)(2,1)} %bitcast.64, bf16[1,197,768]{2,1,0:T(8,128)(2,1)S(1)} %copy-done.8, bf16[1,197,768]{2,1,0:T(8,128)(2,1)S(1)} %copy-done.9, ...), custom_call_target="tpu_custom_call" | custom-call | flops 7000000000 | bytes 18000000 | tf_op jit(solution)/shard_map/token_backward/pallas_call | solution.py:339
  177.9 0.8 copy-done.4
  178.8 0.0 reduce-scatter.5.cloned.1.call-start
  178.8 0.5 reduce-scatter.5.cloned.1.call-update
  179.4 0.1 reshape.103
  179.5 10.4 %all_to_all.32 = f32[8,24,96]{2,1,0:T(8,128)S(1)} all-to-all(f32[8,24,96]{2,1,0:T(8,128)S(1)} %bitcast.68), channel_id=1, replica_groups=mesh['grp'=8,'exp'=16] {'grp'}, dimensions={0} | all-to-all | bytes 147456 | tf_op jit(solution)/shard_map/all_to_all | solution.py:441
  189.9 23.6 %reduce-scatter.3.cloned.1.call-done = bf16[768,384]{1,0:T(8,128)(2,1)} async-done(((bf16[6144,384]{1,0:T(8,128)(2,1)}), bf16[768,384]{1,0:T(8,128)(2,1)}) %reduce-scatter.3.cloned.1.call-update) | async-done | bytes 589840 | tf_op jit(solution)/shard_map/reduce_scatter | solution.py:438
  213.5 5.5 %all-to-all-start.2 = ((bf16[16,48,384]{2,1,0:T(8,128)(2,1)}), bf16[16,48,384]{2,1,0:T(8,128)(2,1)S(1)}, u32[]{:S(2)}, u32[]{:S(2)}) async-start(bf16[16,48,384]{2,1,0:T(8,128)(2,1)} %bitcast.67), calls=%async_computation.3 | async-start | bytes 1179648 | tf_op jit(solution)/shard_map/all_to_all | solution.py:446
  219.0 9.4 %all-to-all-done.2 = bf16[16,48,384]{2,1,0:T(8,128)(2,1)S(1)} async-done(((bf16[16,48,384]{2,1,0:T(8,128)(2,1)}), bf16[16,48,384]{2,1,0:T(8,128)(2,1)S(1)}, u32[]{:S(2)}, u32[]{:S(2)}) %all-to-all-start.2) | async-done | bytes 589856 | tf_op jit(solution)/shard_map/all_to_all | solution.py:446
  228.4 0.7 broadcast_in_dim.13
  229.1 3.5 %all-to-all-start.5 = ((f32[16,24,96]{2,1,0:T(8,128)}), f32[16,24,96]{2,1,0:T(8,128)S(1)}, u32[]{:S(2)}, u32[]{:S(2)}) async-start(f32[16,24,96]{2,1,0:T(8,128)} %broadcast_in_dim.13), calls=%async_computation.6 | async-start | bytes 393216 | tf_op jit(solution)/shard_map/all_to_all | solution.py:443
  232.6 0.1 reduce_sum.40
  232.7 7.0 %all-to-all-done.5 = f32[16,24,96]{2,1,0:T(8,128)S(1)} async-done(((f32[16,24,96]{2,1,0:T(8,128)}), f32[16,24,96]{2,1,0:T(8,128)S(1)}, u32[]{:S(2)}, u32[]{:S(2)}) %all-to-all-start.5) | async-done | bytes 147488 | tf_op jit(solution)/shard_map/all_to_all | solution.py:443
  239.8 0.9 broadcast_in_dim.12
  240.7 3.8 %all-to-all-start.3 = ((bf16[16,48,384]{2,1,0:T(8,128)(2,1)}), bf16[16,48,384]{2,1,0:T(8,128)(2,1)S(1)}, u32[]{:S(2)}, u32[]{:S(2)}) async-start(bf16[16,48,384]{2,1,0:T(8,128)(2,1)} %broadcast_in_dim.12), calls=%async_computation.4 | async-start | bytes 1179648 | tf_op jit(solution)/shard_map/all_to_all | solution.py:450
  244.5 1.4 copy.105
  245.9 2.8 copy.106
  248.7 2.6 copy.109
  251.3 1.0 reduce_sum.42
  252.3 1.3 multiply_subtract_fusion.3
  253.6 1.4 multiply_subtract_fusion.2
  255.0 1.0 copy-done.5
  255.9 1.0 copy-done.6
  256.9 2.8 owner_step.1
  259.7 13.6 %reduce-scatter.5.cloned.1.call-done = bf16[768,768]{1,0:T(8,128)(2,1)} async-done(((bf16[6144,768]{1,0:T(8,128)(2,1)}), bf16[768,768]{1,0:T(8,128)(2,1)}) %reduce-scatter.5.cloned.1.call-update) | async-done | bytes 1179664 | tf_op jit(solution)/shard_map/reduce_scatter | solution.py:430
  273.4 4.1 %multiply_subtract_fusion = (f32[1,384,768]{1,2,0:T(8,128)S(1)}, f32[1,384,768]{1,2,0:T(8,128)S(1)}, f32[1,384,768]{1,2,0:T(8,128)}) fusion(f32[1,384,768]{1,2,0:T(8,128)} %copy-done.20, bf16[768,768]{1,0:T(8,128)(2,1)} %reduce-scatter.5.cloned.1.call-done, f32[1,384,768]{1,2,0:T(8,128)} %copy.106, f32[1,384,768]{1,2,0:T(8,128)} %copy.105), kind=kLoop, calls=%fused_computation.12 | loop fusion | flops 4718592 | bytes 7667712 | tf_op jit(solution)/shard_map/sub | solution.py:259
  277.5 2.7 copy.110
  280.1 1.4 copy.111
  281.5 1.4 copy.112
  282.9 4.2 %multiply_subtract_fusion.1 = (f32[1,768,384]{2,1,0:T(8,128)}, f32[1,768,384]{2,1,0:T(8,128)}, f32[1,768,384]{2,1,0:T(8,128)}) fusion(f32[1,768,384]{2,1,0:T(8,128)S(1)} %copy-done.22, bf16[768,768]{1,0:T(8,128)(2,1)} %reduce-scatter.5.cloned.1.call-done, f32[1,768,384]{2,1,0:T(8,128)} %param.40, f32[1,768,384]{2,1,0:T(8,128)} %param.39), kind=kLoop, calls=%fused_computation.13 | loop fusion | flops 4718592 | bytes 7667712 | tf_op jit(solution)/shard_map/sub | solution.py:259
  (68 shorter events, 0.4 us)
Async XLA Ops:
  7.2 1.3 copy-start.1
  7.2 1.4 copy-start.26
  7.2 1.5 copy-start.27
  7.2 41.9 %all-gather.3.cloned.1.call-start = ((), (), s32[]{:S(2)}) async-start(), calls=%async_computation.8 | async-start | bytes 5529600 | tf_op jit(solution)/shard_map/all_gather | solution.py:410
  8.5 1.4 copy-start.23
  9.9 95.6 %all-gather.5.cloned.1.call-start = ((), (), s32[]{:S(2)}) async-start(), calls=%async_computation.9 | async-start | bytes 10616832 | tf_op jit(solution)/shard_map/all_gather | solution.py:412
  10.3 1.8 copy-start.20
  10.3 1.7 copy-start.21
  13.2 0.7 copy-start.28
  13.2 2.7 copy-start.29
  13.2 35.9 %copy-start.8 = (bf16[1,197,768]{2,1,0:T(8,128)(2,1)S(1)}, bf16[1,197,768]{2,1,0:T(8,128)(2,1)}, u32[]{:S(2)}) copy-start(bf16[1,197,768]{2,1,0:T(8,128)(2,1)} %x_ref.3) | copy-start | bytes 907780
  13.2 35.9 %copy-start.9 = (bf16[1,197,768]{2,1,0:T(8,128)(2,1)S(1)}, bf16[1,197,768]{2,1,0:T(8,128)(2,1)}, u32[]{:S(2)}) copy-start(bf16[1,197,768]{2,1,0:T(8,128)(2,1)} %g_ref.3) | copy-start | bytes 907780
  13.2 200.3 %reduce-scatter.3.cloned.1.call-start = ((), (), s32[]{:S(2)}) async-start(), calls=%async_computation.10 | async-start | bytes 5308416 | tf_op jit(solution)/shard_map/reduce_scatter | solution.py:438
  49.1 2.4 copy-start.7
  56.3 0.8 copy-start.10
  57.1 0.7 copy-start.12
  57.9 0.7 copy-start.14
  58.6 0.7 copy-start.16
  59.3 0.6 copy-start.18
  130.7 33.1 %copy-start.11 = (f32[208,768]{1,0:T(8,128)S(1)}, f32[208,768]{1,0:T(8,128)}, u32[]{:S(2)}) copy-start(f32[208,768]{1,0:T(8,128)} %copy-done.10) | copy-start | bytes 1916932
  130.7 33.1 %copy-start.13 = (bf16[208,768]{1,0:T(8,128)(2,1)S(1)}, bf16[208,768]{1,0:T(8,128)(2,1)}, u32[]{:S(2)}) copy-start(bf16[208,768]{1,0:T(8,128)(2,1)} %copy-done.12) | copy-start | bytes 958468
  130.7 33.1 %copy-start.15 = (bf16[208,768]{1,0:T(8,128)(2,1)S(1)}, bf16[208,768]{1,0:T(8,128)(2,1)}, u32[]{:S(2)}) copy-start(bf16[208,768]{1,0:T(8,128)(2,1)} %copy-done.14) | copy-start | bytes 958468
  130.7 33.1 %copy-start.17 = (bf16[208,768]{1,0:T(8,128)(2,1)S(1)}, bf16[208,768]{1,0:T(8,128)(2,1)}, u32[]{:S(2)}) copy-start(bf16[208,768]{1,0:T(8,128)(2,1)} %copy-done.16) | copy-start | bytes 958468
  130.7 33.1 %copy-start.19 = (f32[208,128]{1,0:T(8,128)S(1)}, f32[208,128]{1,0:T(8,128)}, u32[]{:S(2)}) copy-start(f32[208,128]{1,0:T(8,128)} %copy-done.18) | copy-start | bytes 319492
  177.9 0.8 copy-start.4
  178.8 94.6 %reduce-scatter.5.cloned.1.call-start = ((), (), s32[]{:S(2)}) async-start(), calls=%async_computation.11 | async-start | bytes 10616832 | tf_op jit(solution)/shard_map/reduce_scatter | solution.py:430
  213.5 14.9 %all-to-all-start.2 = ((bf16[16,48,384]{2,1,0:T(8,128)(2,1)}), bf16[16,48,384]{2,1,0:T(8,128)(2,1)S(1)}, u32[]{:S(2)}, u32[]{:S(2)}) async-start(bf16[16,48,384]{2,1,0:T(8,128)(2,1)} %bitcast.67), calls=%async_computation.3 | async-start | bytes 1179648 | tf_op jit(solution)/shard_map/all_to_all | solution.py:446
  229.1 10.7 %all-to-all-start.5 = ((f32[16,24,96]{2,1,0:T(8,128)}), f32[16,24,96]{2,1,0:T(8,128)S(1)}, u32[]{:S(2)}, u32[]{:S(2)}) async-start(f32[16,24,96]{2,1,0:T(8,128)} %broadcast_in_dim.13), calls=%async_computation.6 | async-start | bytes 393216 | tf_op jit(solution)/shard_map/all_to_all | solution.py:443
  232.6 11.9 %copy-start.24 = (f32[1,384,768]{2,1,0:T(8,128)S(1)}, f32[1,384,768]{2,1,0:T(8,128)}, u32[]{:S(2)}) copy-start(f32[1,384,768]{2,1,0:T(8,128)} %param.42) | copy-start | bytes 3538948
  239.8 4.7 %copy-start.25 = (f32[16,24,96]{2,1,0:T(8,128)}, f32[16,24,96]{2,1,0:T(8,128)S(1)}, u32[]{:S(2)}) copy-start(f32[16,24,96]{2,1,0:T(8,128)S(1)} %all-to-all-done.5) | copy-start | bytes 442372
  240.7 14.3 %all-to-all-start.3 = ((bf16[16,48,384]{2,1,0:T(8,128)(2,1)}), bf16[16,48,384]{2,1,0:T(8,128)(2,1)S(1)}, u32[]{:S(2)}, u32[]{:S(2)}) async-start(bf16[16,48,384]{2,1,0:T(8,128)(2,1)} %broadcast_in_dim.12), calls=%async_computation.4 | async-start | bytes 1179648 | tf_op jit(solution)/shard_map/all_to_all | solution.py:450
  245.9 9.1 %copy-start.2 = (f32[96,2304]{1,0:T(8,128)S(1)}, f32[96,2304]{1,0:T(8,128)}, u32[]{:S(2)}) copy-start(f32[96,2304]{1,0:T(8,128)} %refs_2_.1) | copy-start | bytes 2654212
  245.9 9.1 %copy-start.3 = (f32[96,2304]{1,0:T(8,128)S(1)}, f32[96,2304]{1,0:T(8,128)}, u32[]{:S(2)}) copy-start(f32[96,2304]{1,0:T(8,128)} %refs_3_.1) | copy-start | bytes 2654212
  248.7 6.3 %copy-start = (f32[96,2304]{1,0:T(8,128)S(1)}, f32[96,2304]{1,0:T(8,128)}, u32[]{:S(2)}) copy-start(f32[96,2304]{1,0:T(8,128)} %refs_1_.1) | copy-start | bytes 2654212
  255.0 1.0 copy-start.5
  255.9 1.0 copy-start.6
  281.5 1.4 copy-start.22
Sparse Core Ops, SparseCore 0:
  10.3 38.7 all-gather.2
  51.3 54.0 all-gather.4
  178.9 34.5 reduce-scatter.2
  215.8 57.5 reduce-scatter.4

commit v2 on v1

v2 whole, which is shorter than its diff:
```python
import jax
import jax.numpy as jnp
from jax import lax
from jax.experimental import pallas as pl
from jax.experimental.pallas import tpu as pltpu
from jax.sharding import PartitionSpec as P

HEADS = 12
HEAD_DIM = 64
STEP = 10
D = 768
TOK = 197
ROWS = 208
EXPERTS = 16
CAP = 33
SLOTS = EXPERTS * CAP
DENSE = 3200
GRP = 8
OWN = D // GRP
PIECE = 48
WIDE = 384
HID = 384
HALF = D // 2

norm_epsilon = 1e-06
beta_first = 0.9
beta_second = 0.999
adam_epsilon = 1e-08
weight_decay = 0.1
score_scale = HEAD_DIM ** (-0.5)
low = jnp.bfloat16
full = jnp.float32


def dot(a, b, dims=((1,), (0,))):
    return lax.dot_general(a, b, (dims, ((), ())), preferred_element_type=jnp.float32)


NT = ((1,), (1,))
TN = ((0,), (0,))


def unit_rows(values):
    centered = values - jnp.mean(values, axis=-1, keepdims=True)
    variance = jnp.mean(centered * centered, axis=-1, keepdims=True)
    scale = lax.rsqrt(variance + norm_epsilon)
    return centered * scale, scale


def norm_rows(w_ref):
    return w_ref[:, 3072:3200].astype(full).T[16:24]


def pack_kernel(qkv_ref, proj_ref, router_ref, norm_ref, *refs):
    first_out, second_out, qkv_in, proj_in, sem = refs
    loads = [
        pltpu.make_async_copy(source, target, sem.at[i])
        for i, (source, target) in enumerate(((qkv_ref, qkv_in), (proj_ref, proj_in)))
    ]
    for load in loads:
        load.start()
    rest = [router_ref[...], norm_ref[...], jnp.zeros((DENSE - 3092, OWN), full)]
    rest = jnp.concatenate(rest, axis=0).T.astype(low)
    for load in loads:
        load.wait()
    for i, out_ref in enumerate((first_out, second_out)):
        rows = slice(i * PIECE, (i + 1) * PIECE)
        out_ref[:, 0:2304] = qkv_in[rows, :].astype(low)
        out_ref[:, 2304:3072] = proj_in[rows, :].astype(low)
        out_ref[:, 3072:3200] = rest[rows, :]


def dense_pieces(first, second):
    def along(step, value):
        hops = [(2 * x + c, 2 * ((x + step) % 4) + c) for x in range(4) for c in range(2)]
        return lax.ppermute(value, "grp", hops)

    def across(value):
        return lax.ppermute(value, "grp", [(i, i ^ 1) for i in range(GRP)])

    up_first, down_second = along(1, first), along(3, second)
    up_second, down_first = along(1, second), along(3, first)
    far_first, far_second = along(1, up_first), along(3, down_second)
    here = [first, second, up_first, up_second, down_first, down_second, far_first, far_second]
    return here + [across(piece) for piece in here]


def piece_rows(place):
    x, c = place // 2, place % 2
    rows = []
    for core in (c, 1 - c):
        for step in (0, 3, 1, 2):
            near = OWN * (2 * ((x + step) % 4) + core)
            rows += [near, near + PIECE]
    return jnp.stack(rows).astype(jnp.int32)


def dense_copies(rows_ref, pieces, w_ref, sem):
    copies = []
    for i, piece in enumerate(pieces):
        at = pl.multiple_of(rows_ref[i], PIECE)
        copies.append(pltpu.make_async_copy(piece, w_ref.at[pl.ds(at, PIECE), :], sem.at[i]))
        copies[-1].start()
    return copies


class Moves:
    def __init__(self, sem):
        self.sem, self.open = sem, {}

    def start(self, name, source, target):
        self.open[name] = pltpu.make_async_copy(source, target, self.sem.at[len(self.open)])
        self.open[name].start()

    def wait(self, *names):
        for name in names:
            self.open[name].wait()


def padded(ref, pad_ref):
    pad_ref[192:ROWS, :] = jnp.zeros((ROWS - 192, D), full)
    pad_ref[0:TOK, :] = ref[0].astype(full)
    return pad_ref[...]


def lanes(shape):
    return lax.broadcasted_iota(jnp.int32, shape, 1)


def half_masks():
    lane = lanes((1, 128))
    first = (lane < HEAD_DIM).astype(full)
    return first.astype(low), (1.0 - first).astype(low)


def forward_kernel(rows_ref, ids_ref, keep_ref, trow_ref, x_hbm, g_hbm, *refs):
    pieces, refs = refs[:16], refs[16:]
    outs, refs = refs[:8], refs[8:]
    send_ref = outs[0]
    m_ref, a_ref, qkv_ref, p_ref, o_ref, c_ref, r_ref = refs[:7]
    x_ref, g_ref, x_pad, g_pad, w_ref, w_sem, sem, spare = refs[7:]
    moves = Moves(sem)
    moves.start("x", x_hbm, x_ref)
    copies = dense_copies(rows_ref, pieces, w_ref, w_sem)
    moves.start("g", g_hbm, g_ref)
    moves.wait("x")
    x = padded(x_ref, x_pad)
    unit = unit_rows(x)[0]
    moves.wait("g")
    g = padded(g_ref, g_pad)
    for copy in copies:
        copy.wait()
    norms = norm_rows(w_ref)
    a = (unit * norms[0:1] + norms[1:2]).astype(low)
    a_ref[...] = a
    moves.start("a", a_ref, outs[2])
    for part in range(3):
        cols = slice(part * D, part * D + D)
        qkv_ref[:, cols] = dot(a, w_ref[:, cols]).astype(low)
    moves.start("qkv", qkv_ref, outs[3])
    first, second = half_masks()
    seen = lanes((ROWS, ROWS)) < TOK
    low_half = lanes((ROWS, 128)) < HEAD_DIM
    for pair in range(HEADS // 2):
        at = pair * 128
        q = qkv_ref[:, at : at + 128]
        k = qkv_ref[:, D + at : D + at + 128]
        v = qkv_ref[:, 2 * D + at : 2 * D + at + 128]
        mixed = []
        for side, mask in enumerate((first, second)):
            s = dot(q * mask, k, NT) * score_scale
            s = jnp.where(seen, s, -1e30)
            e = jnp.exp(s - jnp.max(s, axis=1, keepdims=True))
            p = (e / jnp.sum(e, axis=1, keepdims=True)).astype(low)
            p_ref[2 * pair + side] = p
            mixed.append(dot(p, v))
        o_ref[:, at : at + 128] = jnp.where(low_half, mixed[0], mixed[1]).astype(low)
    moves.start("p", p_ref, outs[4])
    moves.start("o", o_ref, outs[5])
    m = x + dot(o_ref[...], w_ref[:, 2304:3072])
    m_ref[...] = m
    moves.start("m", m_ref, outs[1])
    c = (unit_rows(m)[0] * norms[2:3] + norms[3:4]).astype(low)
    c_ref[...] = c
    moves.start("c", c_ref, outs[6])
    lane = lanes((ROWS, 128))
    logits = jnp.where(lane < EXPERTS, dot(c, w_ref[:, 3072:3200]), -1e30)
    e = jnp.exp(logits - jnp.max(logits, axis=1, keepdims=True))
    r = e / jnp.sum(e, axis=1, keepdims=True)
    r_ref[...] = r
    moves.start("r", r_ref, outs[7])
    slot = lax.broadcasted_iota(jnp.int32, (SLOTS, ROWS), 0)
    picks, grads = [], []
    for j in range(2):
        chosen = lane == ids_ref[:, j : j + 1]
        gate = jnp.sum(jnp.where(chosen, r, 0.0), axis=1, keepdims=True) * keep_ref[:, j : j + 1]
        picks.append((slot == trow_ref[j : j + 1, :]).astype(full).astype(low))
        grads.append((gate * g).astype(low))
    for part, value in enumerate(
        (dot(picks[0] + picks[1], c), dot(picks[0], grads[0]) + dot(picks[1], grads[1]))
    ):
        spare[...] = value
        for e in range(EXPERTS):
            rows = slice(e * CAP, (e + 1) * CAP)
            send_ref[e, :, part * D : (part + 1) * D] = spare[rows, :].astype(low)
    moves.wait("a", "qkv", "p", "o", "m", "c", "r")


def expert_kernel(
    got_ref, w_ref, back_ref, h_ref, du_ref, xt_ref, dzt_ref, z_sum, dx_sum, xs, dzs
):
    step = pl.program_id(0)

    @pl.when(step == 0)
    def _():
        for e in range(EXPERTS):
            rows = slice(e * CAP, (e + 1) * CAP)
            z_sum[rows, :] = got_ref[e, :, 0:D].astype(full)
            dx_sum[rows, :] = got_ref[e, :, D:].astype(full)
        xs[...] = z_sum[...].astype(low)
        dzs[...] = dx_sum[...].astype(low)
        xt_ref[...] = xs[...].T
        dzt_ref[...] = dzs[...].T
        z_sum[...] = jnp.zeros_like(z_sum)
        dx_sum[...] = jnp.zeros_like(dx_sum)

    wi = jnp.concatenate([w_ref[0:D, 0:HID], w_ref[D:, 0:HID]], axis=1)
    wot = jnp.concatenate([w_ref[0:D, HID:], w_ref[D:, HID:]], axis=1)
    u = dot(xs[...], wi)
    dh = dot(dzs[...], wot)
    square = u * u
    inner = u * (0.7978845608028654 + (0.7978845608028654 * 0.044715) * square)
    t = jnp.tanh(inner)
    half = 0.5 * t + 0.5
    h = (u * half).astype(low)
    slope = (0.5 * u) * (1.0 - t * t)
    slope = slope * (0.7978845608028654 + (3 * 0.7978845608028654 * 0.044715) * square) + half
    du = (slope * dh).astype(low)
    h_ref[...] = h
    du_ref[...] = du
    z_sum[...] += dot(h, wot, NT)
    dx_sum[...] += dot(du, wi, NT)

    @pl.when(step == pl.num_programs(0) - 1)
    def _():
        for e in range(EXPERTS):
            rows = slice(e * CAP, (e + 1) * CAP)
            back_ref[e, :, 0:D] = z_sum[rows, :].astype(low)
            back_ref[e, :, D:] = dx_sum[rows, :].astype(low)


def expert_grad_kernel(xt_ref, dzt_ref, h_ref, du_ref, out_ref):
    gi = dot(xt_ref[...], du_ref[...]).astype(low)
    go = dot(dzt_ref[...], h_ref[...]).astype(low)
    for i in range(2):
        cols = slice(i * HID, (i + 1) * HID)
        out_ref[i * HALF : (i + 1) * HALF, 0:HID] = gi[:, cols]
        out_ref[i * HALF : (i + 1) * HALF, HID:] = go[:, cols]


def spread(grad, part, grads_ref):
    for g in range(GRP):
        for r in range(2):
            rows = slice(g * OWN + r * PIECE, g * OWN + (r + 1) * PIECE)
            for k in range(2):
                cols = slice(k * WIDE, (k + 1) * WIDE)
                grads_ref[g * 2 + r, part * 2 + k] = grad[rows, cols]


def backward_kernel(rows_ref, ids_ref, tcol_ref, keep_ref, back_ref, *refs):
    ins, pieces, refs = refs[:9], refs[9:25], refs[25:]
    outs, refs = refs[:4], refs[4:]
    m_ref, r_ref, g_ref, c_ref, o_ref, qkv_ref, p_ref, a_ref, x_ref = refs[:9]
    result_ref, image_ref, grads_ref, extra_ref = refs[9:13]
    x_pad, g_pad, spare, dqkv, w_ref, w_sem, sem = refs[13:]
    moves = Moves(sem)
    for name in range(1, 5):
        moves.start(name, ins[name - 1], refs[name - 1])
    copies = dense_copies(rows_ref, pieces, w_ref, w_sem)
    for name in range(5, 10):
        moves.start(name, ins[name - 1], refs[name - 1])

    def rows_of(part):
        for e in range(EXPERTS):
            rows = slice(e * CAP, (e + 1) * CAP)
            spare[rows, :] = back_ref[e, :, part * D : (part + 1) * D].astype(full)
        return spare[...].astype(low)

    moves.wait(1, 2, 3)
    g = padded(g_ref, g_pad)
    m = m_ref[...]
    r = r_ref[...]
    lane = lanes((ROWS, 128))
    slot = lanes((ROWS, SLOTS))
    z = rows_of(0)
    total = m
    dr = jnp.zeros((ROWS, 128), full)
    picks = []
    for j in range(2):
        pick = (slot == tcol_ref[:, j : j + 1]).astype(full).astype(low)
        picks.append(pick)
        keep = keep_ref[:, j : j + 1]
        chosen = lane == ids_ref[:, j : j + 1]
        gate = jnp.sum(jnp.where(chosen, r, 0.0), axis=1, keepdims=True) * keep
        zj = dot(pick, z)
        total = total + gate * zj
        dgate = jnp.sum(g * zj, axis=1, keepdims=True) * keep
        dr = dr + jnp.where(chosen, dgate, 0.0)
    result_ref[0] = total[0:TOK].astype(low)
    moves.start("result", result_ref, outs[0])
    for copy in copies:
        copy.wait()
    norms = norm_rows(w_ref)
    moves.wait(4)
    dl = (r * (dr - jnp.sum(dr * r, axis=1, keepdims=True))).astype(low)
    c = c_ref[...]
    extra_ref[0:16, :] = dot(dl, c, TN)[0:16]
    dc = dot(dl, w_ref[:, 3072:3200], NT) + dot(picks[0] + picks[1], rows_of(1))
    xh, scale = unit_rows(m)
    dn2 = jnp.sum(dc * xh, axis=0, keepdims=True)
    dn3 = jnp.sum(dc, axis=0, keepdims=True)
    dxh = dc * norms[2:3]
    dm = g + scale * (
        dxh
        - jnp.mean(dxh, axis=1, keepdims=True)
        - xh * jnp.mean(dxh * xh, axis=1, keepdims=True)
    )
    dmb = dm.astype(low)
    moves.wait(5)
    spread(dot(o_ref[...].T, dmb).astype(low), 3, grads_ref)
    moves.start("proj", grads_ref.at[:, 6:8], outs[2].at[:, 6:8])
    do = dot(dmb, w_ref[:, 2304:3072], NT).astype(low)
    first, second = half_masks()
    low_half = lane < HEAD_DIM
    moves.wait(6, 7)
    for pair in range(HEADS // 2):
        at = pair * 128
        q = qkv_ref[:, at : at + 128]
        k = qkv_ref[:, D + at : D + at + 128]
        v = qkv_ref[:, 2 * D + at : 2 * D + at + 128]
        dop = do[:, at : at + 128]
        parts = []
        for side, mask in enumerate((first, second)):
            p_low = p_ref[2 * pair + side]
            p = p_low.astype(full)
            dp = dot(dop * mask, v, NT)
            ds = (p * (dp - jnp.sum(dp * p, axis=1, keepdims=True))).astype(low)
            parts.append((dot(ds, k), dot(ds, q, TN), dot(p_low, dop, TN)))
        for which, factor in enumerate((score_scale, score_scale, 1.0)):
            both = jnp.where(low_half, parts[0][which], parts[1][which]) * factor
            dqkv[:, which * D + at : which * D + at + 128] = both.astype(low)
    moves.wait(8, 9)
    at_rows = a_ref[...].T
    da = jnp.zeros((ROWS, D), full)
    for part in range(3):
        cols = slice(part * D, part * D + D)
        spread(dot(at_rows, dqkv[:, cols]).astype(low), part, grads_ref)
        groups = slice(2 * part, 2 * part + 2)
        moves.start(("qkv", part), grads_ref.at[:, groups], outs[2].at[:, groups])
        da = da + dot(dqkv[:, cols], w_ref[:, cols], NT)
    xh, scale = unit_rows(padded(x_ref, x_pad))
    extra_ref[16:24, :] = jnp.concatenate(
        [
            jnp.sum(da * xh, axis=0, keepdims=True),
            jnp.sum(da, axis=0, keepdims=True),
            dn2,
            dn3,
            jnp.zeros((4, D), full),
        ],
        axis=0,
    )
    moves.start("extra", extra_ref, outs[3])
    dxh = da * norms[0:1]
    dx = dm + scale * (
        dxh
        - jnp.mean(dxh, axis=1, keepdims=True)
        - xh * jnp.mean(dxh * xh, axis=1, keepdims=True)
    )
    image_ref[0] = dx[0:TOK]
    moves.start("image", image_ref, outs[1])
    moves.wait("result", "proj", ("qkv", 0), ("qkv", 1), ("qkv", 2), "extra", "image")


def adamw(master, first, second, gradient, rate):
    first = beta_first * first + (1.0 - beta_first) * gradient
    second = beta_second * second + (1.0 - beta_second) * gradient * gradient
    corrected = first / (1.0 - beta_first**STEP)
    scaled = jnp.sqrt(second / (1.0 - beta_second**STEP)) + adam_epsilon
    return (first, second, master - rate * (corrected / scaled + weight_decay * master))


def owner_kernel(pieces_ref, *refs):
    inputs, outputs = refs[:6], refs[6:]

    def update(side, rate):
        for r in range(2):
            rows = slice(r * PIECE, (r + 1) * PIECE)
            for k in range(2):
                cols = slice(k * WIDE, (k + 1) * WIDE)
                grad = pieces_ref[r, k].astype(full)
                new = adamw(*[ref[rows, cols] for ref in inputs[side : side + 3]], grad, rate)
                for ref, value in zip(outputs[side : side + 3], new):
                    ref[rows, cols] = value

    last = pl.program_id(0) == 3
    pl.when(jnp.logical_not(last))(lambda: update(0, 0.04))
    pl.when(last)(lambda: update(3, 0.2))


def expert_step_kernel(inner_ref, outer_ref, *refs):
    inputs, outputs = refs[:6], refs[-6:]
    new = adamw(*[ref[0] for ref in inputs[:3]], inner_ref[...].astype(full), 0.04)
    new = new + adamw(*[ref[0] for ref in inputs[3:]], outer_ref[...].astype(full).T, 0.15)
    for ref, value in zip(outputs, new):
        ref[0] = value


def expert_step(half, grad, arrays, partial):
    inner = pl.BlockSpec((1, HALF, 128), lambda i: (0, half, i))
    outer = pl.BlockSpec((1, 128, HALF), lambda i: (0, i, half))
    return pl.pallas_call(
        expert_step_kernel,
        grid=(3,),
        out_shape=tuple(hbm(*a.shape) for a in arrays),
        in_specs=[
            pl.BlockSpec((HALF, 128), lambda i: (0, i)),
            pl.BlockSpec((HALF, 128), lambda i: (0, 3 + i)),
        ]
        + [inner] * 3
        + [outer] * 3
        + in_place(len(partial)),
        out_specs=(inner,) * 3 + (outer,) * 3,
        input_output_aliases={8 + i: i for i in range(len(partial))},
        compiler_params=params(16),
        cost_estimate=pl.CostEstimate(
            flops=10**7, bytes_accessed=8 * 10**6, transcendentals=10**6
        ),
        name="expert_step",
    )(*pinned([grad, grad, *arrays, *partial]))


def shape(*dims, dtype=jnp.float32):
    return jax.ShapeDtypeStruct(dims, dtype)


def in_vmem(count):
    return [pl.BlockSpec(memory_space=pltpu.VMEM)] * count


def pinned(values):
    return [pltpu.with_memory_space_constraint(v, pltpu.HBM) for v in values]


def hbm(*dims, dtype=jnp.float32):
    return pltpu.HBM(dims, dtype)


def in_smem():
    return pl.BlockSpec(memory_space=pltpu.SMEM)


def in_place(count):
    return [pl.BlockSpec(memory_space=pl.ANY)] * count


def params(mib):
    return pltpu.CompilerParams(vmem_limit_bytes=mib * 2**20)


def pack(qkv, proj, router, norm):
    return pl.pallas_call(
        pack_kernel,
        out_shape=(shape(PIECE, DENSE, dtype=low),) * 2,
        in_specs=in_place(2) + in_vmem(2),
        out_specs=tuple(in_vmem(2)),
        scratch_shapes=vmem_like((qkv, proj)) + [pltpu.SemaphoreType.DMA((2,))],
        compiler_params=params(16),
        cost_estimate=pl.CostEstimate(flops=10**5, bytes_accessed=2 * 10**6, transcendentals=0),
        name="pack",
    )(*pinned((qkv, proj)), router.T, norm.T)


def flat_type(value):
    return value.inner_aval if hasattr(value, "inner_aval") else value


def vmem_like(shapes):
    return [pltpu.VMEM(s.shape, s.dtype) for s in map(flat_type, shapes)]


def token_forward(*args):
    outs = (
        pltpu.VMEM((EXPERTS, CAP, 2 * D), low),
        hbm(ROWS, D),
        hbm(ROWS, D, dtype=low),
        hbm(ROWS, 3 * D, dtype=low),
        hbm(HEADS, ROWS, ROWS, dtype=low),
        hbm(ROWS, D, dtype=low),
        hbm(ROWS, D, dtype=low),
        hbm(ROWS, 128),
    )
    return pl.pallas_call(
        forward_kernel,
        out_shape=outs,
        in_specs=[in_smem()] + in_vmem(3) + in_place(18),
        out_specs=tuple(in_vmem(1) + in_place(7)),
        scratch_shapes=vmem_like(outs[1:])
        + [pltpu.VMEM((1, TOK, D), low)] * 2
        + [pltpu.VMEM((ROWS, D), full)] * 2
        + [
            pltpu.VMEM((D, DENSE), low),
            pltpu.SemaphoreType.DMA((16,)),
            pltpu.SemaphoreType.DMA((10,)),
            pltpu.VMEM((SLOTS, D), full),
        ],
        compiler_params=params(40),
        cost_estimate=pl.CostEstimate(
            flops=4 * 10**9, bytes_accessed=12 * 10**6, transcendentals=10**6
        ),
        name="token_forward",
    )(*args[:4], *pinned(args[4:]))


def experts_both_ways(got, weights):
    return pl.pallas_call(
        expert_kernel,
        grid=(GRP // 2,),
        out_shape=(
            pltpu.VMEM((EXPERTS, CAP, 2 * D), low),
            hbm(SLOTS, GRP * HID, dtype=low),
            hbm(SLOTS, GRP * HID, dtype=low),
            hbm(D, SLOTS, dtype=low),
            hbm(D, SLOTS, dtype=low),
        ),
        in_specs=[
            pl.BlockSpec(memory_space=pltpu.VMEM),
            pl.BlockSpec((2 * D, D), lambda i: (i, 0)),
        ],
        out_specs=(
            pl.BlockSpec(memory_space=pltpu.VMEM),
            pl.BlockSpec((SLOTS, 2 * HID), lambda i: (0, i)),
            pl.BlockSpec((SLOTS, 2 * HID), lambda i: (0, i)),
            pl.BlockSpec((D, SLOTS), lambda i: (0, 0)),
            pl.BlockSpec((D, SLOTS), lambda i: (0, 0)),
        ),
        scratch_shapes=[
            pltpu.VMEM((SLOTS, D), full),
            pltpu.VMEM((SLOTS, D), full),
            pltpu.VMEM((SLOTS, D), low),
            pltpu.VMEM((SLOTS, D), low),
        ],
        compiler_params=params(44),
        cost_estimate=pl.CostEstimate(
            flops=10 * 10**9, bytes_accessed=23 * 10**6, transcendentals=2 * 10**6
        ),
        name="experts",
    )(got, *pinned([weights]))


def expert_grads(half, xt, dzt, h, du):
    return pl.pallas_call(
        expert_grad_kernel,
        grid=(GRP // 2,),
        out_shape=hbm(GRP * HALF, D, dtype=low),
        in_specs=[
            pl.BlockSpec((HALF, SLOTS), lambda i: (half, 0)),
            pl.BlockSpec((HALF, SLOTS), lambda i: (half, 0)),
            pl.BlockSpec((SLOTS, 2 * HID), lambda i: (0, i)),
            pl.BlockSpec((SLOTS, 2 * HID), lambda i: (0, i)),
        ],
        out_specs=pl.BlockSpec((2 * HALF, D), lambda i: (i, 0)),
        compiler_params=params(32),
        cost_estimate=pl.CostEstimate(
            flops=3 * 10**9, bytes_accessed=13 * 10**6, transcendentals=0
        ),
        name="expert_grads",
    )(*pinned([xt, dzt, h, du]))


def token_backward(*args):
    outs = (
        hbm(1, TOK, D, dtype=low),
        hbm(1, TOK, D),
        hbm(16, 8, PIECE, WIDE, dtype=low),
        hbm(24, D),
    )
    return pl.pallas_call(
        backward_kernel,
        out_shape=outs,
        in_specs=[in_smem()] + in_vmem(4) + in_place(25),
        out_specs=tuple(in_place(4)),
        scratch_shapes=vmem_like(args[5:14])
        + vmem_like(outs)
        + [
            pltpu.VMEM((ROWS, D), full),
            pltpu.VMEM((ROWS, D), full),
            pltpu.VMEM((SLOTS, D), full),
            pltpu.VMEM((ROWS, 3 * D), low),
            pltpu.VMEM((D, DENSE), low),
            pltpu.SemaphoreType.DMA((16,)),
            pltpu.SemaphoreType.DMA((17,)),
        ],
        compiler_params=params(48),
        cost_estimate=pl.CostEstimate(
            flops=40 * 10**9, bytes_accessed=18 * 10**6, transcendentals=10**4
        ),
        name="token_backward",
    )(*args[:5], *pinned(args[5:]))


def owner_step(pieces, arrays):
    qkv = pl.BlockSpec((OWN, D), lambda i: (0, jnp.minimum(i, 2)))
    proj = pl.BlockSpec((OWN, D), lambda i: (0, 0))
    return pl.pallas_call(
        owner_kernel,
        grid=(4,),
        out_shape=tuple(hbm(*a.shape) for a in arrays),
        in_specs=[pl.BlockSpec((2, 2, PIECE, WIDE), lambda i: (0, i, 0, 0))]
        + [qkv] * 3
        + [proj] * 3,
        out_specs=(qkv,) * 3 + (proj,) * 3,
        compiler_params=params(16),
        cost_estimate=pl.CostEstimate(
            flops=10**7, bytes_accessed=8 * 10**6, transcendentals=10**6
        ),
        name="owner_step",
    )(pieces, *pinned(arrays))


def on_device(
    images,
    cotangent,
    expert_ids,
    kept_routes,
    qkv_master,
    qkv_first,
    qkv_second,
    proj_master,
    proj_first,
    proj_second,
    router_master,
    router_first,
    router_second,
    norm_master,
    norm_first,
    norm_second,
    inner_master,
    inner_first,
    inner_second,
    outer_master,
    outer_first,
    outer_second,
):
    pieces = dense_pieces(*pack(qkv_master, proj_master, router_master, norm_master))
    rows = piece_rows(lax.axis_index("grp"))
    mine = jnp.concatenate([inner_master[0].astype(low), outer_master[0].astype(low).T], axis=1)
    mine, *_ = lax.optimization_barrier((mine, pieces[2], pieces[5]))
    weights = lax.all_gather(mine, "grp", axis=0, tiled=True)

    ids = expert_ids.reshape(TOK, 2)
    kept = kept_routes.reshape(TOK, 2)
    flat = ids.reshape(-1)
    marks = (flat[:, None] == jnp.arange(EXPERTS, dtype=jnp.int32)[None, :]).astype(jnp.int32)
    slots = jnp.sum((jnp.cumsum(marks, axis=0) - marks) * marks, axis=1).reshape(TOK, 2)
    target = jnp.where(kept > 0, ids * CAP + slots, -1)
    padding = ((0, ROWS - TOK), (0, 0))
    target = jnp.pad(target, padding, constant_values=-1)
    ids = jnp.pad(ids, padding, constant_values=-1)
    keep = jnp.pad(kept.astype(full), padding)

    send, m, a, qkv, p, o, c, r = token_forward(
        rows, ids, keep, target.T, images, cotangent, *pieces
    )
    got = lax.all_to_all(send, "exp", split_axis=0, concat_axis=0, tiled=True)
    back, *kept_parts = experts_both_ways(got, weights)
    h, du, xt, dzt = kept_parts
    back = lax.all_to_all(back, "exp", split_axis=0, concat_axis=0, tiled=True)
    head = expert_grads(0, xt, dzt, h, du)
    tail = expert_grads(1, xt, dzt, h, du)
    head = lax.psum_scatter(head, "grp", scatter_dimension=0, tiled=True)
    result, image_grad, grads, extra = token_backward(
        rows, ids, target, keep, back, m, r, cotangent, c, o, qkv, p, a, images, *pieces
    )
    grads, head = lax.optimization_barrier((grads, head))
    grads = lax.psum_scatter(
        grads.reshape(GRP * 16 * PIECE, WIDE), "grp", scatter_dimension=0, tiled=True
    )
    experts = (
        inner_master,
        inner_first,
        inner_second,
        outer_master,
        outer_first,
        outer_second,
    )
    partial = expert_step(0, head, experts, ())

    extra = jnp.moveaxis(extra.reshape(24, GRP, OWN), 1, 0)
    extra = lax.all_to_all(extra, "grp", split_axis=0, concat_axis=0, tiled=True)
    extra = jnp.broadcast_to(jnp.sum(extra, axis=0)[None], (EXPERTS, 24, OWN))
    extra = lax.all_to_all(extra, "exp", split_axis=0, concat_axis=0, tiled=True)
    extra = jnp.sum(extra, axis=0).T
    grads, tail, extra = lax.optimization_barrier((grads, tail, extra))
    tail = lax.psum_scatter(tail, "grp", scatter_dimension=0, tiled=True)

    pieces = lax.all_to_all(
        grads.reshape(16, PIECE, WIDE), "exp", split_axis=0, concat_axis=0, tiled=True
    )
    piece = jnp.sum(pieces.astype(full), axis=0).astype(low)
    pieces = lax.all_to_all(
        jnp.broadcast_to(piece[None], (16, PIECE, WIDE)),
        "exp",
        split_axis=0,
        concat_axis=0,
        tiled=True,
    )
    qkv_moment, qkv_square, qkv_weight, proj_moment, proj_square, proj_weight = owner_step(
        pieces.reshape(2, 8, PIECE, WIDE),
        (qkv_master, qkv_first, qkv_second, proj_master, proj_first, proj_second),
    )
    router_moment, router_square, router_weight = adamw(
        router_master, router_first, router_second, extra[:, 0:16], 0.03
    )
    norm_moment, norm_square, norm_weight = adamw(
        norm_master, norm_first, norm_second, extra[:, 16:20], 0.3
    )
    (
        inner_moment,
        inner_square,
        inner_weight,
        outer_moment,
        outer_square,
        outer_weight,
    ) = expert_step(1, tail, experts, partial)
    return (
        result,
        image_grad,
        qkv_moment,
        qkv_square,
        qkv_weight,
        proj_moment,
        proj_square,
        proj_weight,
        router_moment,
        router_square,
        router_weight,
        norm_moment,
        norm_square,
        norm_weight,
        inner_moment,
        inner_square,
        inner_weight,
        outer_moment,
        outer_square,
        outer_weight,
    )


def solution(mesh):
    in_specs = (
        P(("grp", "exp"), None, None),
        P(("grp", "exp"), None, None),
        P(("grp", "exp"), None, None),
        P(("grp", "exp"), None, None),
        P("grp", None),
        P("grp", None),
        P("grp", None),
        P("grp", None),
        P("grp", None),
        P("grp", None),
        P("grp", None),
        P("grp", None),
        P("grp", None),
        P("grp", None),
        P("grp", None),
        P("grp", None),
        P("exp", None, "grp"),
        P("exp", None, "grp"),
        P("exp", None, "grp"),
        P("exp", "grp", None),
        P("exp", "grp", None),
        P("exp", "grp", None),
    )
    out_specs = (
        P(("grp", "exp"), None, None),
        P(("grp", "exp"), None, None),
        P("grp", None),
        P("grp", None),
        P("grp", None),
        P("grp", None),
        P("grp", None),
        P("grp", None),
        P("grp", None),
        P("grp", None),
        P("grp", None),
        P("grp", None),
        P("grp", None),
        P("grp", None),
        P("exp", None, "grp"),
        P("exp", None, "grp"),
        P("exp", None, "grp"),
        P("exp", "grp", None),
        P("exp", "grp", None),
        P("exp", "grp", None),
    )
    return jax.shard_map(
        on_device, mesh=mesh, in_specs=in_specs, out_specs=out_specs, check_vma=False
    )
```

time: 295 us -> 250 us (0.85)
  waiting for transfers between devices: 99.8 us -> 32.5 us
  Pallas kernels: 47 us -> 71.6 us
  local copies, waits for them, and re-layouts: 27.4 us -> 11 us
  blocking collectives: 76.3 us -> 89.4 us
  other arithmetic: 15.8 us -> 3.88 us
  starting transfers between devices: 13 us -> 23.7 us
    all_gather x1 -> x0, waiting for transfers between devices: 32.9 us -> none  [on_device(): dense = lax.all_gather(dense, 'grp', axis=0, tiled=True)]
    pallas_call x4 -> x9, Pallas kernels: 47 us -> 71.6 us  [the longest x1 16.5 us: experts_both_ways(): pl.pallas_call(expert_kernel, grid=(GRP // 2,), out_shape=(pltpu.VMEM((EX...]
    reduce_scatter x2 -> x3, waiting for transfers between devices: 37.2 us -> 14.7 us  [the longest x1 10.4 us: on_device(): lax.psum_scatter(grads.reshape(GRP * 16 * PIECE, WIDE), 'grp', scatter_di...]
    ppermute x0 -> x14, waiting for transfers between devices: none -> 16.5 us  [the longest x6 15.1 us: along(): return lax.ppermute(value, 'grp', hops)]
    ppermute x0 -> x14, starting transfers between devices: none -> 16.2 us  [the longest x6 8.82 us: along(): return lax.ppermute(value, 'grp', hops)]
    unnamed x69 -> x58, local copies, waits for them, and re-layouts: 23.9 us -> 8.63 us
    all_to_all x2 -> x3, blocking collectives: 65.9 us -> 79.4 us  [the longest x1 35.6 us: on_device(): got = lax.all_to_all(send, 'exp', split_axis=0, concat_axis=0, tiled=True)]
    all_gather x1, waiting for transfers between devices: 12.6 us -> 0.01 us  [on_device(): weights = lax.all_gather(mine, 'grp', axis=0, tiled=True)]
  transfers between devices with their start and end apart: 7 -> 20, of which waited for: 6 -> 10; matrix products, arithmetic and copies ran while one was open for 5% -> 4% of each run, Pallas kernels for 3% -> 16%
where the time goes in v2:
time: 250 us; the launch traced here: 246 us
  blocking collectives  89.4 us (36%)
  Pallas kernels  71.6 us (29%)
  waiting for transfers between devices  32.5 us (13%)
  starting transfers between devices  23.7 us (9%)
  between operations  14.2 us (6%)
  local copies, waits for them, and re-layouts  11 us (4%)
  other arithmetic  3.88 us (2%)
    all_to_all x1, blocking collectives, on_device(): got = lax.all_to_all(send, 'exp', split_axis=0, concat_axis=0, tiled=True)  35.6 us
    all_to_all x1, blocking collectives, on_device(): back = lax.all_to_all(back, 'exp', split_axis=0, concat_axis=0, tiled=True)  28.9 us
    pallas_call x1, Pallas kernels, experts_both_ways(): pl.pallas_call(expert_kernel, grid=(GRP // 2,), out_shape=(pltpu.VMEM((EX...  16.5 us
    pallas_call x2, Pallas kernels, expert_grads(): pl.pallas_call(expert_grad_kernel, grid=(GRP // 2,), out_shape=hbm(GRP *...  16.1 us
    ppermute x6, waiting for transfers between devices, along(): return lax.ppermute(value, 'grp', hops)  15.1 us
    all_to_all x1, blocking collectives, on_device(): lax.all_to_all(grads.reshape(16, PIECE, WIDE), 'exp', split_axis=0, conca...  14.8 us
    pallas_call x1, Pallas kernels, token_backward(): pl.pallas_call(backward_kernel, out_shape=outs, in_specs=[in_smem()] + in...  13.7 us
    reduce_scatter x1, waiting for transfers between devices, on_device(): lax.psum_scatter(grads.reshape(GRP * 16 * PIECE, WIDE), 'grp', scatter_di...  10.4 us
  transfers between devices with their start and end apart: 20, of which 10 were waited for; matrix products, arithmetic and copies ran while one was open for 4% of the time, Pallas kernels for 16%

profile of v2, /device:TPU:1, one launch (start us, length us, event | category | flops | bytes accessed | tf_op | source)
XLA Modules:
  0.0 246.3 jit_solution(12172243255862320896)
XLA Ops:
  7.2 0.7 copy-done.1
  7.9 0.7 copy-done.3
  8.6 1.4 pack.1
  10.1 2.1 collective-permute-start
  12.2 1.3 collective-permute-start.3
  13.5 1.1 copy.80
  14.6 0.1 convert_bitcast_fusion.1
  14.7 1.0 copy-done.9
  15.6 1.1 pad_maximum_fusion
  16.8 3.2 %collective-permute-done.refs_2_.refs_11_ = bf16[48,3200]{1,0:T(8,128)(2,1)S(1)} collective-permute-done((bf16[48,3200]{1,0:T(8,128)(2,1)S(1)}, bf16[48,3200]{1,0:T(8,128)(2,1)S(1)}, u32[]{:S(2)}, u32[]{:S(2)}) %collective-permute-start) | collective-permute-done | bytes 307232 | tf_op jit(solution)/shard_map/ppermute | solution.py:76
  20.0 0.1 collective-permute-done.3.refs_5_.refs_14_
  20.2 1.9 collective-permute-start.6
  22.1 2.6 %collective-permute-start.2 = (bf16[48,3200]{1,0:T(8,128)(2,1)S(1)}, bf16[48,3200]{1,0:T(8,128)(2,1)S(1)}, u32[]{:S(2)}, u32[]{:S(2)}) collective-permute-start(bf16[48,3200]{1,0:T(8,128)(2,1)S(1)} %get-tuple-element.63.refs_0_.refs_9_), channel_id=1, source_target_pairs={{0,96},{16,112},{32,0},{48,16},{64,32},{80,48},{96,64},{112,80},{1... | collective-permute-start | bytes 921608 | tf_op jit(solution)/shard_map/ppermute | solution.py:76
  24.7 0.4 collective-permute-start.7
  25.1 0.1 copy.73
  25.2 0.1 eq.32
  25.4 1.2 reduce-window.6
  26.5 0.2 slice_reduce_fusion
  26.8 0.1 bitcast_bitcast_fusion
  26.9 0.1 collective-permute-start.4
  27.0 2.7 %collective-permute-start.5 = (bf16[48,3200]{1,0:T(8,128)(2,1)}, bf16[48,3200]{1,0:T(8,128)(2,1)S(1)}, u32[]{:S(2)}, u32[]{:S(2)}) collective-permute-start(bf16[48,3200]{1,0:T(8,128)(2,1)} %collective-permute-done.3.refs_5_.refs_14_), channel_id=1, source_target_pairs={{0,96},{16,112},{32,0},{48,16},{64,32},{80,48},{96,64},{112,80},{1... | collective-permute-start | bytes 921608 | tf_op jit(solution)/shard_map/ppermute | solution.py:76
  29.6 1.7 collective-permute-done.2.refs_4_.refs_13_
  31.3 1.3 collective-permute-start.10
  32.7 0.1 reshape.81
  32.8 0.1 copy.74
  33.0 0.1 collective-permute-start.8
  33.1 1.9 collective-permute-done.1.refs_3_.refs_12_
  35.0 1.5 collective-permute-start.11
  36.5 0.1 collective-permute-start.9
  36.6 8.2 %collective-permute-done.4.refs_6_.refs_15_ = bf16[48,3200]{1,0:T(8,128)(2,1)S(1)} collective-permute-done((bf16[48,3200]{1,0:T(8,128)(2,1)S(1)}, bf16[48,3200]{1,0:T(8,128)(2,1)S(1)}, u32[]{:S(2)}, u32[]{:S(2)}) %collective-permute-start.4) | collective-permute-done | bytes 307232 | tf_op jit(solution)/shard_map/ppermute | solution.py:76
  44.8 2.0 collective-permute-start.12
  46.8 0.1 collective-permute-start.13
  46.9 0.1 copy.79.trow_ref
  47.0 0.1 stack.67.rows_ref
  47.1 1.0 collective-permute-done.12.refs_14_.refs_23_
  48.1 0.4 collective-permute-done.13.refs_15_.refs_24_
  48.6 8.2 %token_forward.1 = (bf16[16,33,1536]{2,1,0:T(8,128)(2,1)S(1)}, f32[208,768]{1,0:T(8,128)}, bf16[208,768]{1,0:T(8,128)(2,1)}, bf16[208,2304]{1,0:T(8,128)(2,1)}, ...) custom-call(s32[16]{0:T(128)S(1)} %stack.67.rows_ref, ...), custom_call_target="tpu_custom_call" | custom-call | flops 4000000000 | bytes 12000000 | tf_op jit(solution)/shard_map/token_forward/pallas_call | solution.py:502
  56.8 35.6 %all_to_all.30.got_ref = bf16[16,33,1536]{2,1,0:T(8,128)(2,1)} all-to-all(bf16[16,33,1536]{2,1,0:T(8,128)(2,1)S(1)} %get-tuple-element.65), channel_id=1, replica_groups=mesh['grp'=8,'exp'=16] {'exp'}, dimensions={0} | all-to-all | bytes 3244032 | tf_op jit(solution)/shard_map/all_to_all | solution.py:674
  92.4 1.5 copy-done
  93.9 16.5 %experts.1 = (bf16[16,33,1536]{2,1,0:T(8,128)(2,1)S(1)}, bf16[528,3072]{1,0:T(8,128)(2,1)}, bf16[528,3072]{1,0:T(8,128)(2,1)}, bf16[768,528]{1,0:T(8,128)(2,1)}, bf16[768,528]{1,0:T(8,128)(2,1)}) custom-call(bf16[16,33,1536]{2,1,0:T(8,128)(2,1)S(1)} %copy-done, bf16[6144,768]{1,0:T(8,128)(2,1)} %all-gather.2.cloned.1.call-done.w_ref), custom_call_target="tpu_custom_call" | custom-call | flops 10000000000 | bytes 23000000 | tf_op jit(solution)/shard_map/experts/pallas_call | solution.py:525
  110.4 8.0 %expert_grads.2 = bf16[3072,768]{1,0:T(8,128)(2,1)} custom-call(bf16[768,528]{1,0:T(8,128)(2,1)} %get-tuple-element.78.xt_ref, bf16[768,528]{1,0:T(8,128)(2,1)} %get-tuple-element.79.dzt_ref, bf16[528,3072]{1,0:T(8,128)(2,1)} %get-tuple-element.80.h_ref, bf16[528,3072]{1,0:T(8,128)(2,1)} %get-tuple-element.81.du_ref), custom_call_target="tpu_custom_call" | custom-call | flops 3000000000 | bytes 13000000 | tf_op jit(solution)/shard_map/expert_grads/pallas_call | solution.py:561
  118.5 0.0 reduce-scatter.6.cloned.1.call-start
  118.5 28.9 %all_to_all.31.back_ref = bf16[16,33,1536]{2,1,0:T(8,128)(2,1)S(1)} all-to-all(bf16[16,33,1536]{2,1,0:T(8,128)(2,1)S(1)} %get-tuple-element.67), channel_id=1, replica_groups=mesh['grp'=8,'exp'=16] {'exp'}, dimensions={0} | all-to-all | bytes 3244032 | tf_op jit(solution)/shard_map/all_to_all | solution.py:677
  147.5 13.7 %token_backward.1 = (bf16[1,197,768]{2,1,0:T(8,128)(2,1)}, f32[1,197,768]{2,1,0:T(8,128)}, bf16[16,8,48,384]{3,2,1,0:T(8,128)(2,1)}, f32[24,768]{1,0:T(8,128)}) custom-call(s32[16]{0:T(128)S(1)} %stack.67.rows_ref, s32[208,2]{1,0:T(8,128)S(1)} %pad.15.ids_ref, s32[208,2]{1,0:T(8,128)S(1)} %get-tuple-element.193.tcol_ref, f32[208,2]{1,0:T(8,128)S(1)} %pad.18.keep_ref, ...), custom_call_target="tpu_custom_call" | custom-call | flops 40000000000 | bytes 18000000 | tf_op jit(solution)/shard_map/token_backward/pallas_call | solution.py:587
  161.3 0.9 copy-done.12
  162.1 0.1 reshape.83
  162.3 10.0 %all_to_all.32 = f32[8,24,96]{2,1,0:T(8,128)S(1)} all-to-all(f32[8,24,96]{2,1,0:T(8,128)S(1)} %bitcast.59), channel_id=1, replica_groups=mesh['grp'=8,'exp'=16] {'grp'}, dimensions={0} | all-to-all | bytes 147456 | tf_op jit(solution)/shard_map/all_to_all | solution.py:699
  172.3 0.7 broadcast_in_dim.9
  173.0 3.5 %all-to-all-start.3 = ((f32[16,24,96]{2,1,0:T(8,128)}), f32[16,24,96]{2,1,0:T(8,128)S(1)}, u32[]{:S(2)}, u32[]{:S(2)}) async-start(f32[16,24,96]{2,1,0:T(8,128)} %broadcast_in_dim.9), calls=%async_computation.5 | async-start | bytes 393216 | tf_op jit(solution)/shard_map/all_to_all | solution.py:701
  176.5 8.1 %expert_grads.3 = bf16[3072,768]{1,0:T(8,128)(2,1)} custom-call(bf16[768,528]{1,0:T(8,128)(2,1)} %get-tuple-element.78.xt_ref, bf16[768,528]{1,0:T(8,128)(2,1)} %get-tuple-element.79.dzt_ref, bf16[528,3072]{1,0:T(8,128)(2,1)} %get-tuple-element.80.h_ref, bf16[528,3072]{1,0:T(8,128)(2,1)} %get-tuple-element.81.du_ref), custom_call_target="tpu_custom_call" | custom-call | flops 3000000000 | bytes 13000000 | tf_op jit(solution)/shard_map/expert_grads/pallas_call | solution.py:561
  184.7 10.4 %reduce-scatter.6.cloned.1.call-done = bf16[768,384]{1,0:T(8,128)(2,1)} async-done(((bf16[6144,384]{1,0:T(8,128)(2,1)}), bf16[768,384]{1,0:T(8,128)(2,1)}) %reduce-scatter.6.cloned.1.call-update) | async-done | bytes 589840 | tf_op jit(solution)/shard_map/reduce_scatter | solution.py:685
  195.1 1.0 copy-done.11
  196.1 14.8 %all_to_all.33 = bf16[16,48,384]{2,1,0:T(8,128)(2,1)S(1)} all-to-all(bf16[16,48,384]{2,1,0:T(8,128)(2,1)S(1)} %bitcast.58), channel_id=1, replica_groups=mesh['grp'=8,'exp'=16] {'exp'}, dimensions={0} | all-to-all | bytes 1179648 | tf_op jit(solution)/shard_map/all_to_all | solution.py:706
  211.0 0.1 reduce_sum.42
  211.1 0.9 broadcast_in_dim.10
  211.9 3.8 %all-to-all-start.5 = ((bf16[16,48,384]{2,1,0:T(8,128)(2,1)}), bf16[16,48,384]{2,1,0:T(8,128)(2,1)S(1)}, u32[]{:S(2)}, u32[]{:S(2)}) async-start(bf16[16,48,384]{2,1,0:T(8,128)(2,1)} %broadcast_in_dim.10), calls=%async_computation.7 | async-start | bytes 1179648 | tf_op jit(solution)/shard_map/all_to_all | solution.py:710
  215.8 1.4 copy.82
  217.2 5.2 %expert_step.2 = (f32[1,768,384]{2,1,0:T(8,128)}, f32[1,768,384]{2,1,0:T(8,128)}, f32[1,768,384]{2,1,0:T(8,128)}, f32[1,384,768]{2,1,0:T(8,128)}, f32[1,384,768]{2,1,0:T(8,128)}, /*index=5*/f32[1,384,768]{2,1,0:T(8,128)}) custom-call(bf16[384,768]{1,0:T(8,128)(2,1)} %reduce-scatter.4.cloned.1.call-done.inner_ref.outer_ref, ...), custom_call_target="tpu_custom_call" | custom-call | flops 10000000 | bytes 8000000 | tf_op jit(solution)/shard_map/expert_step/pallas_call | solution.py:421
  222.5 0.6 multiply_subtract_fusion.1
  223.1 0.6 multiply_subtract_fusion
  223.7 1.2 all-to-all-done.5
  224.9 5.4 %owner_step.1 = (f32[96,2304]{1,0:T(8,128)}, f32[96,2304]{1,0:T(8,128)}, f32[96,2304]{1,0:T(8,128)}, f32[96,768]{1,0:T(8,128)}, f32[96,768]{1,0:T(8,128)}, /*index=5*/f32[96,768]{1,0:T(8,128)}) custom-call(bf16[2,8,48,384]{3,2,1,0:T(8,128)(2,1)S(1)} %bitcast.52, f32[96,2304]{1,0:T(8,128)} %refs_0_.3, f32[96,2304]{1,0:T(8,128)} %refs_1_.3, ...), custom_call_target="tpu_custom_call" | custom-call | flops 10000000 | bytes 8000000 | tf_op jit(solution)/shard_map/owner_step/pallas_call | solution.py:614
  230.3 4.3 %reduce-scatter.8.cloned.1.call-done.inner_ref.outer_ref = bf16[384,768]{1,0:T(8,128)(2,1)} async-done(((bf16[3072,768]{1,0:T(8,128)(2,1)}), bf16[384,768]{1,0:T(8,128)(2,1)}) %reduce-scatter.8.cloned.1.call-update) | async-done | bytes 589840 | tf_op jit(solution)/shard_map/reduce_scatter | solution.py:704
  234.6 5.1 %expert_step.3 = (f32[1,768,384]{2,1,0:T(8,128)}, f32[1,768,384]{2,1,0:T(8,128)}, f32[1,768,384]{2,1,0:T(8,128)}, f32[1,384,768]{2,1,0:T(8,128)}, f32[1,384,768]{2,1,0:T(8,128)}, /*index=5*/f32[1,384,768]{2,1,0:T(8,128)}) custom-call(bf16[384,768]{1,0:T(8,128)(2,1)} %reduce-scatter.8.clone, ...), custom_call_target="tpu_custom_call", output_to_operand_aliasing={{0}: (8, {}), {1}: (9, {}), {2}: (10, {}), {3}: (11, {}), {... | custom-call | flops 10000000 | bytes 8000000 | tf_op jit(solution)/shard_map/expert_step/pallas_call | solution.py:421
  (79 shorter events, 0.6 us)
Async XLA Ops:
  7.2 85.2 %all-gather.2.cloned.1.call-start = ((), (), s32[]{:S(2)}) async-start(), calls=%async_computation.9 | async-start | bytes 10616832 | tf_op jit(solution)/shard_map/all_gather | solution.py:658
  7.2 0.7 copy-start.1
  7.9 0.7 copy-start.3
  8.6 4.9 %copy-start.7 = (f32[1,384,768]{2,1,0:T(8,128)S(1)}, f32[1,384,768]{2,1,0:T(8,128)}, u32[]{:S(2)}) copy-start(f32[1,384,768]{2,1,0:T(8,128)} %refs_3_.5) | copy-start | bytes 3538948
  10.0 12.1 %copy-start.5 = (bf16[48,3200]{1,0:T(8,128)(2,1)}, bf16[48,3200]{1,0:T(8,128)(2,1)S(1)}, u32[]{:S(2)}) copy-start(bf16[48,3200]{1,0:T(8,128)(2,1)S(1)} %get-tuple-element.63.refs_0_.refs_9_) | copy-start | bytes 921604
  10.0 15.0 %copy-start.6 = (bf16[48,3200]{1,0:T(8,128)(2,1)}, bf16[48,3200]{1,0:T(8,128)(2,1)S(1)}, u32[]{:S(2)}) copy-start(bf16[48,3200]{1,0:T(8,128)(2,1)S(1)} %get-tuple-element.64.refs_1_.refs_10_) | copy-start | bytes 921604
  10.1 4.5 %copy-start.8 = (f32[1,768,384]{2,1,0:T(8,128)S(1)}, f32[1,768,384]{2,1,0:T(8,128)}, u32[]{:S(2)}) copy-start(f32[1,768,384]{2,1,0:T(8,128)} %refs_0_.5) | copy-start | bytes 3538948
  10.1 9.9 %collective-permute-start = (bf16[48,3200]{1,0:T(8,128)(2,1)S(1)}, bf16[48,3200]{1,0:T(8,128)(2,1)S(1)}, u32[]{:S(2)}, u32[]{:S(2)}) collective-permute-start(bf16[48,3200]{1,0:T(8,128)(2,1)S(1)} %get-tuple-element.63.refs_0_.refs_9_), channel_id=1, source_target_pairs={{0,32},{16,48},{32,64},{48,80},{64,96},{80,112},{96,0},{112,16},{1... | collective-permute-start | bytes 921608 | tf_op jit(solution)/shard_map/ppermute | solution.py:76
  12.2 7.9 %collective-permute-start.3 = (bf16[48,3200]{1,0:T(8,128)(2,1)S(1)}, bf16[48,3200]{1,0:T(8,128)(2,1)}, u32[]{:S(2)}, u32[]{:S(2)}) collective-permute-start(bf16[48,3200]{1,0:T(8,128)(2,1)S(1)} %get-tuple-element.64.refs_1_.refs_10_), channel_id=1, source_target_pairs={{0,96},{16,112},{32,0},{48,16},{64,32},{80,48},{96,64},{112,80},{1... | collective-permute-start | bytes 921608 | tf_op jit(solution)/shard_map/ppermute | solution.py:76
  14.6 1.1 copy-start.9
  16.8 8.3 %copy-start.15 = (s32[1,197,2]{1,2,0:T(2,128)S(1)}, s32[1,197,2]{1,2,0:T(2,128)}, u32[]{:S(2)}) copy-start(s32[1,197,2]{1,2,0:T(2,128)} %param.24) | copy-start | bytes 4732
  16.8 16.1 %copy-start.16 = (s32[1,197,2]{1,2,0:T(2,128)S(1)}, s32[1,197,2]{1,2,0:T(2,128)}, u32[]{:S(2)}) copy-start(s32[1,197,2]{1,2,0:T(2,128)} %param.25) | copy-start | bytes 4732
  20.0 13.0 %copy-start.19 = (bf16[48,3200]{1,0:T(8,128)(2,1)}, bf16[48,3200]{1,0:T(8,128)(2,1)S(1)}, u32[]{:S(2)}) copy-start(bf16[48,3200]{1,0:T(8,128)(2,1)S(1)} %collective-permute-done.refs_2_.refs_11_) | copy-start | bytes 921604
  20.1 141.1 %reduce-scatter.4.cloned.1.call-start = ((), (), s32[]{:S(2)}) async-start(), calls=%async_computation.10 | async-start | bytes 5308416 | tf_op jit(solution)/shard_map/reduce_scatter | solution.py:680
  20.2 6.8 %collective-permute-start.6 = (bf16[48,3200]{1,0:T(8,128)(2,1)S(1)}, bf16[48,3200]{1,0:T(8,128)(2,1)S(1)}, u32[]{:S(2)}, u32[]{:S(2)}) collective-permute-start(bf16[48,3200]{1,0:T(8,128)(2,1)S(1)} %get-tuple-element.63.refs_0_.refs_9_), channel_id=1, source_target_pairs={{0,16},{16,0},{32,48},{48,32},{64,80},{80,64},{96,112},{112,96},{1... | collective-permute-start | bytes 921608 | tf_op jit(solution)/shard_map/ppermute | solution.py:79
  22.1 9.2 %collective-permute-start.2 = (bf16[48,3200]{1,0:T(8,128)(2,1)S(1)}, bf16[48,3200]{1,0:T(8,128)(2,1)S(1)}, u32[]{:S(2)}, u32[]{:S(2)}) collective-permute-start(bf16[48,3200]{1,0:T(8,128)(2,1)S(1)} %get-tuple-element.63.refs_0_.refs_9_), channel_id=1, source_target_pairs={{0,96},{16,112},{32,0},{48,16},{64,32},{80,48},{96,64},{112,80},{1... | collective-permute-start | bytes 921608 | tf_op jit(solution)/shard_map/ppermute | solution.py:76
  24.7 8.3 %collective-permute-start.7 = (bf16[48,3200]{1,0:T(8,128)(2,1)S(1)}, bf16[48,3200]{1,0:T(8,128)(2,1)S(1)}, u32[]{:S(2)}, u32[]{:S(2)}) collective-permute-start(bf16[48,3200]{1,0:T(8,128)(2,1)S(1)} %get-tuple-element.64.refs_1_.refs_10_), channel_id=1, source_target_pairs={{0,16},{16,0},{32,48},{48,32},{64,80},{80,64},{96,112},{112,96},{1... | collective-permute-start | bytes 921608 | tf_op jit(solution)/shard_map/ppermute | solution.py:79
  25.1 9.9 %collective-permute-start.1 = (bf16[48,3200]{1,0:T(8,128)(2,1)S(1)}, bf16[48,3200]{1,0:T(8,128)(2,1)S(1)}, u32[]{:S(2)}, u32[]{:S(2)}) collective-permute-start(bf16[48,3200]{1,0:T(8,128)(2,1)S(1)} %get-tuple-element.64.refs_1_.refs_10_), channel_id=1, source_target_pairs={{0,32},{16,48},{32,64},{48,80},{64,96},{80,112},{96,0},{112,16},{1... | collective-permute-start | bytes 921608 | tf_op jit(solution)/shard_map/ppermute | solution.py:76
  26.9 17.9 %collective-permute-start.4 = (bf16[48,3200]{1,0:T(8,128)(2,1)S(1)}, bf16[48,3200]{1,0:T(8,128)(2,1)S(1)}, u32[]{:S(2)}, u32[]{:S(2)}) collective-permute-start(bf16[48,3200]{1,0:T(8,128)(2,1)S(1)} %collective-permute-done.refs_2_.refs_11_), channel_id=1, source_target_pairs={{0,32},{16,48},{32,64},{48,80},{64,96},{80,112},{96,0},{112,16},{1... | collective-permute-start | bytes 921608 | tf_op jit(solution)/shard_map/ppermute | solution.py:76
  27.0 21.6 %copy-start.20 = (bf16[48,3200]{1,0:T(8,128)(2,1)}, bf16[48,3200]{1,0:T(8,128)(2,1)S(1)}, u32[]{:S(2)}) copy-start(bf16[48,3200]{1,0:T(8,128)(2,1)S(1)} %collective-permute-done.6.refs_8_.refs_17_) | copy-start | bytes 921604
  27.0 19.8 %collective-permute-start.5 = (bf16[48,3200]{1,0:T(8,128)(2,1)}, bf16[48,3200]{1,0:T(8,128)(2,1)S(1)}, u32[]{:S(2)}, u32[]{:S(2)}) collective-permute-start(bf16[48,3200]{1,0:T(8,128)(2,1)} %collective-permute-done.3.refs_5_.refs_14_), channel_id=1, source_target_pairs={{0,96},{16,112},{32,0},{48,16},{64,32},{80,48},{96,64},{112,80},{1... | collective-permute-start | bytes 921608 | tf_op jit(solution)/shard_map/ppermute | solution.py:76
  31.3 17.2 %copy-start.21 = (bf16[48,3200]{1,0:T(8,128)(2,1)}, bf16[48,3200]{1,0:T(8,128)(2,1)S(1)}, u32[]{:S(2)}) copy-start(bf16[48,3200]{1,0:T(8,128)(2,1)S(1)} %collective-permute-done.2.refs_4_.refs_13_) | copy-start | bytes 921604
  31.3 5.2 %collective-permute-start.10 = (bf16[48,3200]{1,0:T(8,128)(2,1)S(1)}, bf16[48,3200]{1,0:T(8,128)(2,1)}, u32[]{:S(2)}, u32[]{:S(2)}) collective-permute-start(bf16[48,3200]{1,0:T(8,128)(2,1)S(1)} %collective-permute-done.2.refs_4_.refs_13_), channel_id=1, source_target_pairs={{0,16},{16,0},{32,48},{48,32},{64,80},{80,64},{96,112},{112,96},{1... | collective-permute-start | bytes 921608 | tf_op jit(solution)/shard_map/ppermute | solution.py:79
  33.0 15.5 %copy-start.22 = (bf16[48,3200]{1,0:T(8,128)(2,1)}, bf16[48,3200]{1,0:T(8,128)(2,1)S(1)}, u32[]{:S(2)}) copy-start(bf16[48,3200]{1,0:T(8,128)(2,1)S(1)} %collective-permute-done.7.refs_9_.refs_18_) | copy-start | bytes 921604
  33.0 14.1 %collective-permute-start.8 = (bf16[48,3200]{1,0:T(8,128)(2,1)S(1)}, bf16[48,3200]{1,0:T(8,128)(2,1)S(1)}, u32[]{:S(2)}, u32[]{:S(2)}) collective-permute-start(bf16[48,3200]{1,0:T(8,128)(2,1)S(1)} %collective-permute-done.refs_2_.refs_11_), channel_id=1, source_target_pairs={{0,16},{16,0},{32,48},{48,32},{64,80},{80,64},{96,112},{112,96},{1... | collective-permute-start | bytes 921608 | tf_op jit(solution)/shard_map/ppermute | solution.py:79
  35.0 13.6 %copy-start.23 = (bf16[48,3200]{1,0:T(8,128)(2,1)}, bf16[48,3200]{1,0:T(8,128)(2,1)S(1)}, u32[]{:S(2)}) copy-start(bf16[48,3200]{1,0:T(8,128)(2,1)S(1)} %collective-permute-done.1.refs_3_.refs_12_) | copy-start | bytes 921604
  35.0 12.1 %collective-permute-start.11 = (bf16[48,3200]{1,0:T(8,128)(2,1)}, bf16[48,3200]{1,0:T(8,128)(2,1)}, u32[]{:S(2)}, u32[]{:S(2)}) collective-permute-start(bf16[48,3200]{1,0:T(8,128)(2,1)} %collective-permute-done.3.refs_5_.refs_14_), channel_id=1, source_target_pairs={{0,16},{16,0},{32,48},{48,32},{64,80},{80,64},{96,112},{112,96},{1... | collective-permute-start | bytes 921608 | tf_op jit(solution)/shard_map/ppermute | solution.py:79
  36.5 10.6 %collective-permute-start.9 = (bf16[48,3200]{1,0:T(8,128)(2,1)S(1)}, bf16[48,3200]{1,0:T(8,128)(2,1)}, u32[]{:S(2)}, u32[]{:S(2)}) collective-permute-start(bf16[48,3200]{1,0:T(8,128)(2,1)S(1)} %collective-permute-done.1.refs_3_.refs_12_), channel_id=1, source_target_pairs={{0,16},{16,0},{32,48},{48,32},{64,80},{80,64},{96,112},{112,96},{1... | collective-permute-start | bytes 921608 | tf_op jit(solution)/shard_map/ppermute | solution.py:79
  44.8 3.8 %copy-start.24 = (bf16[48,3200]{1,0:T(8,128)(2,1)}, bf16[48,3200]{1,0:T(8,128)(2,1)S(1)}, u32[]{:S(2)}) copy-start(bf16[48,3200]{1,0:T(8,128)(2,1)S(1)} %collective-permute-done.4.refs_6_.refs_15_) | copy-start | bytes 921604
  44.8 3.3 %collective-permute-start.12 = (bf16[48,3200]{1,0:T(8,128)(2,1)S(1)}, bf16[48,3200]{1,0:T(8,128)(2,1)}, u32[]{:S(2)}, u32[]{:S(2)}) collective-permute-start(bf16[48,3200]{1,0:T(8,128)(2,1)S(1)} %collective-permute-done.4.refs_6_.refs_15_), channel_id=1, source_target_pairs={{0,16},{16,0},{32,48},{48,32},{64,80},{80,64},{96,112},{112,96},{1... | collective-permute-start | bytes 921608 | tf_op jit(solution)/shard_map/ppermute | solution.py:79
  46.8 1.8 copy-start.25
  46.8 1.8 collective-permute-start.13
  47.1 1.5 copy-start.26
  92.4 1.5 copy-start
  118.5 76.6 %reduce-scatter.6.cloned.1.call-start = ((), (), s32[]{:S(2)}) async-start(), calls=%async_computation.11 | async-start | bytes 5308416 | tf_op jit(solution)/shard_map/reduce_scatter | solution.py:685
  161.2 0.9 copy-start.12
  173.0 11.7 %all-to-all-start.3 = ((f32[16,24,96]{2,1,0:T(8,128)}), f32[16,24,96]{2,1,0:T(8,128)S(1)}, u32[]{:S(2)}, u32[]{:S(2)}) async-start(f32[16,24,96]{2,1,0:T(8,128)} %broadcast_in_dim.9), calls=%async_computation.5 | async-start | bytes 393216 | tf_op jit(solution)/shard_map/all_to_all | solution.py:701
  176.5 58.1 %reduce-scatter.8.cloned.1.call-start = ((), (), s32[]{:S(2)}) async-start(), calls=%async_computation.12 | async-start | bytes 5308416 | tf_op jit(solution)/shard_map/reduce_scatter | solution.py:704
  195.1 1.1 copy-start.11
  211.0 4.8 %copy-start.10 = (f32[1,197,768]{2,1,0:T(8,128)S(1)}, f32[1,197,768]{2,1,0:T(8,128)}, u32[]{:S(2)}) copy-start(f32[1,197,768]{2,1,0:T(8,128)} %get-tuple-element.167) | copy-start | bytes 1815556
  211.9 13.0 %all-to-all-start.5 = ((bf16[16,48,384]{2,1,0:T(8,128)(2,1)}), bf16[16,48,384]{2,1,0:T(8,128)(2,1)S(1)}, u32[]{:S(2)}, u32[]{:S(2)}) async-start(bf16[16,48,384]{2,1,0:T(8,128)(2,1)} %broadcast_in_dim.10), calls=%async_computation.7 | async-start | bytes 1179648 | tf_op jit(solution)/shard_map/all_to_all | solution.py:710
  217.2 5.3 %copy-start.4 = (f32[96,4]{0,1:T(4,128)S(1)}, f32[96,4]{0,1:T(4,128)}, u32[]{:S(2)}) copy-start(f32[96,4]{0,1:T(4,128)} %param.35) | copy-start | bytes 4612
  217.2 5.3 %copy-start.17 = (f32[96,4]{0,1:T(4,128)S(1)}, f32[96,4]{0,1:T(4,128)}, u32[]{:S(2)}) copy-start(f32[96,4]{0,1:T(4,128)} %param.37) | copy-start | bytes 4612
  217.2 5.3 %copy-start.18 = (f32[96,4]{0,1:T(4,128)S(1)}, f32[96,4]{0,1:T(4,128)}, u32[]{:S(2)}) copy-start(f32[96,4]{0,1:T(4,128)} %param.36) | copy-start | bytes 4612
  217.2 5.9 %copy-start.2 = (f32[96,16]{0,1:T(8,128)S(1)}, f32[96,16]{0,1:T(8,128)}, u32[]{:S(2)}) copy-start(f32[96,16]{0,1:T(8,128)} %param.32) | copy-start | bytes 18436
  217.2 5.9 %copy-start.13 = (f32[96,16]{0,1:T(8,128)S(1)}, f32[96,16]{0,1:T(8,128)}, u32[]{:S(2)}) copy-start(f32[96,16]{0,1:T(8,128)} %param.34) | copy-start | bytes 18436
  217.2 5.9 %copy-start.14 = (f32[96,16]{0,1:T(8,128)S(1)}, f32[96,16]{0,1:T(8,128)}, u32[]{:S(2)}) copy-start(f32[96,16]{0,1:T(8,128)} %param.33) | copy-start | bytes 18436
Sparse Core Ops, SparseCore 0:
  20.2 61.8 all-gather.1
  118.6 32.2 reduce-scatter.3
  161.4 33.6 reduce-scatter.5
  197.3 37.2 reduce-scatter.7

commit v3 on v2

--- a/solution.py
+++ b/solution.py
@@ -20,7 +20,7 @@
 PIECE = 48
 WIDE = 384
 HID = 384
-HALF = D // 2
+BLOCK = 4 * PIECE + 16
 
 norm_epsilon = 1e-06
 beta_first = 0.9
@@ -52,16 +52,19 @@
 
 
 def pack_kernel(qkv_ref, proj_ref, router_ref, norm_ref, *refs):
-    first_out, second_out, qkv_in, proj_in, sem = refs
+    first_out, second_out, qkv_in, proj_in, router_in, norm_in, sem = refs
+    sources = (qkv_ref, proj_ref, router_ref, norm_ref)
     loads = [
         pltpu.make_async_copy(source, target, sem.at[i])
-        for i, (source, target) in enumerate(((qkv_ref, qkv_in), (proj_ref, proj_in)))
+        for i, (source, target) in enumerate(zip(sources, refs[2:6]))
     ]
     for load in loads:
         load.start()
-    rest = [router_ref[...], norm_ref[...], jnp.zeros((DENSE - 3092, OWN), full)]
+    for load in loads[2:]:
+        load.wait()
+    rest = [router_in[...], norm_in[...], jnp.zeros((DENSE - 3092, OWN), full)]
     rest = jnp.concatenate(rest, axis=0).T.astype(low)
-    for load in loads:
+    for load in loads[:2]:
         load.wait()
     for i, out_ref in enumerate((first_out, second_out)):
         rows = slice(i * PIECE, (i + 1) * PIECE)
@@ -79,7 +82,10 @@
         return lax.ppermute(value, "grp", [(i, i ^ 1) for i in range(GRP)])
 
     up_first, down_second = along(1, first), along(3, second)
-    up_second, down_first = along(1, second), along(3, first)
+    up_first, down_second, again, other = lax.optimization_barrier(
+        (up_first, down_second, second, first)
+    )
+    up_second, down_first = along(1, again), along(3, other)
     far_first, far_second = along(1, up_first), along(3, down_second)
     here = [first, second, up_first, up_second, down_first, down_second, far_first, far_second]
     return here + [across(piece) for piece in here]
@@ -92,7 +98,7 @@
         for step in (0, 3, 1, 2):
             near = OWN * (2 * ((x + step) % 4) + core)
             rows += [near, near + PIECE]
-    return jnp.stack(rows).astype(jnp.int32)
+    return jnp.stack(rows + [x, c]).astype(jnp.int32)
 
 
 def dense_copies(rows_ref, pieces, w_ref, sem):
@@ -115,6 +121,10 @@
     def wait(self, *names):
         for name in names:
             self.open[name].wait()
+
+
+def slot_rows(e):
+    return slice(e * CAP, (e + 1) * CAP)
 
 
 def padded(ref, pad_ref):
@@ -201,8 +211,7 @@
     ):
         spare[...] = value
         for e in range(EXPERTS):
-            rows = slice(e * CAP, (e + 1) * CAP)
-            send_ref[e, :, part * D : (part + 1) * D] = spare[rows, :].astype(low)
+            send_ref[e, :, part * D : (part + 1) * D] = spare[slot_rows(e), :].astype(low)
     moves.wait("a", "qkv", "p", "o", "m", "c", "r")
 
 
@@ -249,30 +258,51 @@
             back_ref[e, :, D:] = dx_sum[rows, :].astype(low)
 
 
-def expert_grad_kernel(xt_ref, dzt_ref, h_ref, du_ref, out_ref):
+def expert_grad_kernel(h_ref, du_ref, xt_ref, dzt_ref, out_ref):
     gi = dot(xt_ref[...], du_ref[...]).astype(low)
     go = dot(dzt_ref[...], h_ref[...]).astype(low)
     for i in range(2):
         cols = slice(i * HID, (i + 1) * HID)
-        out_ref[i * HALF : (i + 1) * HALF, 0:HID] = gi[:, cols]
-        out_ref[i * HALF : (i + 1) * HALF, HID:] = go[:, cols]
-
-
-def spread(grad, part, grads_ref):
+        out_ref[i * D : (i + 1) * D, 0:HID] = gi[:, cols]
+        out_ref[i * D : (i + 1) * D, HID:] = go[:, cols]
+
+
+def owner_place(rows_ref, g):
+    return (g % 2 + rows_ref[17]) % 2, (g // 2 + 4 - rows_ref[16]) % 4
+
+
+def spread(rows_ref, grad, part, grads_ref):
     for g in range(GRP):
+        side, step = owner_place(rows_ref, g)
+        at = pl.multiple_of(step * PIECE, PIECE)
         for r in range(2):
             rows = slice(g * OWN + r * PIECE, g * OWN + (r + 1) * PIECE)
             for k in range(2):
                 cols = slice(k * WIDE, (k + 1) * WIDE)
-                grads_ref[g * 2 + r, part * 2 + k] = grad[rows, cols]
+                grads_ref[side, r * 8 + part * 2 + k, pl.ds(at, PIECE), :] = grad[rows, cols]
+
+
+def spread_extra(rows_ref, extra, rest_ref, grads_ref):
+    empty = jnp.zeros((16, 128 - OWN), full)
+    for g in range(GRP):
+        side, step = owner_place(rows_ref, g)
+        cols = slice(g * OWN, (g + 1) * OWN)
+        parts = [extra[0:16, cols], empty, extra[16:32, cols], empty, jnp.zeros((16, 128), full)]
+        rest_ref[side, step] = jnp.concatenate(parts, axis=1)
+    unused = jnp.zeros((12, WIDE), full)
+    for side in range(2):
+        for e in range(16):
+            rows = [rest_ref[side, step, e : e + 1, :] for step in range(4)]
+            rows = jnp.concatenate(rows + [unused], axis=0)
+            grads_ref[side, e, 4 * PIECE :, :] = rows.astype(low)
 
 
 def backward_kernel(rows_ref, ids_ref, tcol_ref, keep_ref, back_ref, *refs):
     ins, pieces, refs = refs[:9], refs[9:25], refs[25:]
     outs, refs = refs[:4], refs[4:]
     m_ref, r_ref, g_ref, c_ref, o_ref, qkv_ref, p_ref, a_ref, x_ref = refs[:9]
-    result_ref, image_ref, grads_ref, extra_ref = refs[9:13]
-    x_pad, g_pad, spare, dqkv, w_ref, w_sem, sem = refs[13:]
+    result_ref, image_ref = refs[9:11]
+    x_pad, g_pad, spare, dqkv, w_ref, w_sem, sem, grads_ref, rest_ref = refs[11:]
     moves = Moves(sem)
     for name in range(1, 5):
         moves.start(name, ins[name - 1], refs[name - 1])
@@ -282,9 +312,19 @@
 
     def rows_of(part):
         for e in range(EXPERTS):
-            rows = slice(e * CAP, (e + 1) * CAP)
-            spare[rows, :] = back_ref[e, :, part * D : (part + 1) * D].astype(full)
+            spare[slot_rows(e), :] = back_ref[e, :, part * D : (part + 1) * D].astype(full)
         return spare[...].astype(low)
+
+    def send_grads(part):
+        rows = pl.ds(0, 4 * PIECE)
+        for r in range(2):
+            some = pl.ds(r * 8 + part * 2, 2)
+            for side in (1, 0):
+                moves.start(
+                    (part, r, side),
+                    grads_ref.at[side, some, rows],
+                    outs[2 + side].at[some, rows],
+                )
 
     moves.wait(1, 2, 3)
     g = padded(g_ref, g_pad)
@@ -314,7 +354,7 @@
     moves.wait(4)
     dl = (r * (dr - jnp.sum(dr * r, axis=1, keepdims=True))).astype(low)
     c = c_ref[...]
-    extra_ref[0:16, :] = dot(dl, c, TN)[0:16]
+    gr = dot(dl, c, TN)[0:16]
     dc = dot(dl, w_ref[:, 3072:3200], NT) + dot(picks[0] + picks[1], rows_of(1))
     xh, scale = unit_rows(m)
     dn2 = jnp.sum(dc * xh, axis=0, keepdims=True)
@@ -327,8 +367,8 @@
     )
     dmb = dm.astype(low)
     moves.wait(5)
-    spread(dot(o_ref[...].T, dmb).astype(low), 3, grads_ref)
-    moves.start("proj", grads_ref.at[:, 6:8], outs[2].at[:, 6:8])
+    spread(rows_ref, dot(o_ref[...].T, dmb).astype(low), 3, grads_ref)
+    send_grads(3)
     do = dot(dmb, w_ref[:, 2304:3072], NT).astype(low)
     first, second = half_masks()
     low_half = lane < HEAD_DIM
@@ -354,22 +394,22 @@
     da = jnp.zeros((ROWS, D), full)
     for part in range(3):
         cols = slice(part * D, part * D + D)
-        spread(dot(at_rows, dqkv[:, cols]).astype(low), part, grads_ref)
-        groups = slice(2 * part, 2 * part + 2)
-        moves.start(("qkv", part), grads_ref.at[:, groups], outs[2].at[:, groups])
+        spread(rows_ref, dot(at_rows, dqkv[:, cols]).astype(low), part, grads_ref)
+        send_grads(part)
         da = da + dot(dqkv[:, cols], w_ref[:, cols], NT)
     xh, scale = unit_rows(padded(x_ref, x_pad))
-    extra_ref[16:24, :] = jnp.concatenate(
-        [
-            jnp.sum(da * xh, axis=0, keepdims=True),
-            jnp.sum(da, axis=0, keepdims=True),
-            dn2,
-            dn3,
-            jnp.zeros((4, D), full),
-        ],
-        axis=0,
-    )
-    moves.start("extra", extra_ref, outs[3])
+    extra = [
+        gr,
+        jnp.sum(da * xh, axis=0, keepdims=True),
+        jnp.sum(da, axis=0, keepdims=True),
+        dn2,
+        dn3,
+        jnp.zeros((12, D), full),
+    ]
+    spread_extra(rows_ref, jnp.concatenate(extra, axis=0), rest_ref, grads_ref)
+    for side in (1, 0):
+        rows = pl.ds(4 * PIECE, 16)
+        moves.start(("rest", side), grads_ref.at[side, :, rows], outs[2 + side].at[:, rows])
     dxh = da * norms[0:1]
     dx = dm + scale * (
         dxh
@@ -378,7 +418,7 @@
     )
     image_ref[0] = dx[0:TOK]
     moves.start("image", image_ref, outs[1])
-    moves.wait("result", "proj", ("qkv", 0), ("qkv", 1), ("qkv", 2), "extra", "image")
+    moves.wait(*[name for name in moves.open if name not in range(1, 10)])
 
 
 def adamw(master, first, second, gradient, rate):
@@ -389,15 +429,15 @@
     return (first, second, master - rate * (corrected / scaled + weight_decay * master))
 
 
-def owner_kernel(pieces_ref, *refs):
-    inputs, outputs = refs[:6], refs[6:]
+def owner_kernel(pieces_ref, rest_ref, *refs):
+    inputs, outputs = refs[:12], refs[12:]
 
     def update(side, rate):
         for r in range(2):
             rows = slice(r * PIECE, (r + 1) * PIECE)
             for k in range(2):
                 cols = slice(k * WIDE, (k + 1) * WIDE)
-                grad = pieces_ref[r, k].astype(full)
+                grad = pieces_ref[r, k, 0:PIECE, :].astype(full)
                 new = adamw(*[ref[rows, cols] for ref in inputs[side : side + 3]], grad, rate)
                 for ref, value in zip(outputs[side : side + 3], new):
                     ref[rows, cols] = value
@@ -406,37 +446,46 @@
     pl.when(jnp.logical_not(last))(lambda: update(0, 0.04))
     pl.when(last)(lambda: update(3, 0.2))
 
-
-def expert_step_kernel(inner_ref, outer_ref, *refs):
+    @pl.when(last)
+    def _():
+        rest = jnp.concatenate(
+            [rest_ref[r, k, PIECE :, :] for r in range(2) for k in range(8)], axis=0
+        ).astype(full)
+        for side, grad, rate in (
+            (6, rest[:, 0:OWN], 0.03),
+            (9, rest[0:4, 128 : 128 + OWN], 0.3),
+        ):
+            new = adamw(*[ref[...] for ref in inputs[side : side + 3]], grad, rate)
+            for ref, value in zip(outputs[side : side + 3], new):
+                ref[...] = value
+
+
+def expert_step_kernel(grad_ref, *refs):
     inputs, outputs = refs[:6], refs[-6:]
-    new = adamw(*[ref[0] for ref in inputs[:3]], inner_ref[...].astype(full), 0.04)
-    new = new + adamw(*[ref[0] for ref in inputs[3:]], outer_ref[...].astype(full).T, 0.15)
+    grad = grad_ref[...].astype(full)
+    new = adamw(*[ref[0] for ref in inputs[:3]], grad[:, 0:HID], 0.04)
+    new = new + adamw(*[ref[0] for ref in inputs[3:]], grad[:, HID:].T, 0.15)
     for ref, value in zip(outputs, new):
         ref[0] = value
 
 
-def expert_step(half, grad, arrays, partial):
-    inner = pl.BlockSpec((1, HALF, 128), lambda i: (0, half, i))
-    outer = pl.BlockSpec((1, 128, HALF), lambda i: (0, i, half))
+def expert_step(grad, arrays):
+    inner = pl.BlockSpec((1, 128, HID), lambda i: (0, i, 0))
+    outer = pl.BlockSpec((1, HID, 128), lambda i: (0, 0, i))
     return pl.pallas_call(
         expert_step_kernel,
-        grid=(3,),
+        grid=(D // 128,),
         out_shape=tuple(hbm(*a.shape) for a in arrays),
-        in_specs=[
-            pl.BlockSpec((HALF, 128), lambda i: (0, i)),
-            pl.BlockSpec((HALF, 128), lambda i: (0, 3 + i)),
-        ]
+        in_specs=[pl.BlockSpec((128, D), lambda i: (i, 0))]
         + [inner] * 3
-        + [outer] * 3
-        + in_place(len(partial)),
+        + [outer] * 3,
         out_specs=(inner,) * 3 + (outer,) * 3,
-        input_output_aliases={8 + i: i for i in range(len(partial))},
         compiler_params=params(16),
         cost_estimate=pl.CostEstimate(
             flops=10**7, bytes_accessed=8 * 10**6, transcendentals=10**6
         ),
         name="expert_step",
-    )(*pinned([grad, grad, *arrays, *partial]))
+    )(*pinned([grad, *arrays]))
 
 
 def shape(*dims, dtype=jnp.float32):
@@ -471,13 +520,13 @@
     return pl.pallas_call(
         pack_kernel,
         out_shape=(shape(PIECE, DENSE, dtype=low),) * 2,
-        in_specs=in_place(2) + in_vmem(2),
+        in_specs=in_place(4),
         out_specs=tuple(in_vmem(2)),
-        scratch_shapes=vmem_like((qkv, proj)) + [pltpu.SemaphoreType.DMA((2,))],
+        scratch_shapes=vmem_like((qkv, proj, router.T, norm.T)) + [pltpu.SemaphoreType.DMA((4,))],
         compiler_params=params(16),
         cost_estimate=pl.CostEstimate(flops=10**5, bytes_accessed=2 * 10**6, transcendentals=0),
         name="pack",
-    )(*pinned((qkv, proj)), router.T, norm.T)
+    )(*pinned((qkv, proj, router.T, norm.T)))
 
 
 def flat_type(value):
@@ -521,34 +570,26 @@
     )(*args[:4], *pinned(args[4:]))
 
 
+PAIR = pl.BlockSpec((2 * D, D), lambda i: (i, 0))
+HIDDEN = pl.BlockSpec((SLOTS, 2 * HID), lambda i: (0, i))
+TURNED = pl.BlockSpec((D, SLOTS), lambda i: (0, 0))
+
+
 def experts_both_ways(got, weights):
+    hidden, turned = hbm(SLOTS, GRP * HID, dtype=low), hbm(D, SLOTS, dtype=low)
     return pl.pallas_call(
         expert_kernel,
         grid=(GRP // 2,),
         out_shape=(
             pltpu.VMEM((EXPERTS, CAP, 2 * D), low),
-            hbm(SLOTS, GRP * HID, dtype=low),
-            hbm(SLOTS, GRP * HID, dtype=low),
-            hbm(D, SLOTS, dtype=low),
-            hbm(D, SLOTS, dtype=low),
+            hidden,
+            hidden,
+            turned,
+            turned,
         ),
-        in_specs=[
-            pl.BlockSpec(memory_space=pltpu.VMEM),
-            pl.BlockSpec((2 * D, D), lambda i: (i, 0)),
-        ],
-        out_specs=(
-            pl.BlockSpec(memory_space=pltpu.VMEM),
-            pl.BlockSpec((SLOTS, 2 * HID), lambda i: (0, i)),
-            pl.BlockSpec((SLOTS, 2 * HID), lambda i: (0, i)),
-            pl.BlockSpec((D, SLOTS), lambda i: (0, 0)),
-            pl.BlockSpec((D, SLOTS), lambda i: (0, 0)),
-        ),
-        scratch_shapes=[
-            pltpu.VMEM((SLOTS, D), full),
-            pltpu.VMEM((SLOTS, D), full),
-            pltpu.VMEM((SLOTS, D), low),
-            pltpu.VMEM((SLOTS, D), low),
-        ],
+        in_specs=in_vmem(1) + [PAIR],
+        out_specs=(*in_vmem(1), HIDDEN, HIDDEN, TURNED, TURNED),
+        scratch_shapes=[pltpu.VMEM((SLOTS, D), full)] * 2 + [pltpu.VMEM((SLOTS, D), low)] * 2,
         compiler_params=params(44),
         cost_estimate=pl.CostEstimate(
             flops=10 * 10**9, bytes_accessed=23 * 10**6, transcendentals=2 * 10**6
@@ -557,32 +598,27 @@
     )(got, *pinned([weights]))
 
 
-def expert_grads(half, xt, dzt, h, du):
+def expert_grads(*args):
     return pl.pallas_call(
         expert_grad_kernel,
         grid=(GRP // 2,),
-        out_shape=hbm(GRP * HALF, D, dtype=low),
-        in_specs=[
-            pl.BlockSpec((HALF, SLOTS), lambda i: (half, 0)),
-            pl.BlockSpec((HALF, SLOTS), lambda i: (half, 0)),
-            pl.BlockSpec((SLOTS, 2 * HID), lambda i: (0, i)),
-            pl.BlockSpec((SLOTS, 2 * HID), lambda i: (0, i)),
-        ],
-        out_specs=pl.BlockSpec((2 * HALF, D), lambda i: (i, 0)),
-        compiler_params=params(32),
+        out_shape=hbm(GRP * D, D, dtype=low),
+        in_specs=[HIDDEN, HIDDEN, TURNED, TURNED],
+        out_specs=PAIR,
+        compiler_params=params(28),
         cost_estimate=pl.CostEstimate(
-            flops=3 * 10**9, bytes_accessed=13 * 10**6, transcendentals=0
+            flops=6 * 10**9, bytes_accessed=18 * 10**6, transcendentals=0
         ),
         name="expert_grads",
-    )(*pinned([xt, dzt, h, du]))
+    )(*pinned(args))
 
 
 def token_backward(*args):
     outs = (
         hbm(1, TOK, D, dtype=low),
         hbm(1, TOK, D),
-        hbm(16, 8, PIECE, WIDE, dtype=low),
-        hbm(24, D),
+        hbm(16, BLOCK, WIDE, dtype=low),
+        hbm(16, BLOCK, WIDE, dtype=low),
     )
     return pl.pallas_call(
         backward_kernel,
@@ -590,7 +626,7 @@
         in_specs=[in_smem()] + in_vmem(4) + in_place(25),
         out_specs=tuple(in_place(4)),
         scratch_shapes=vmem_like(args[5:14])
-        + vmem_like(outs)
+        + vmem_like(outs[:2])
         + [
             pltpu.VMEM((ROWS, D), full),
             pltpu.VMEM((ROWS, D), full),
@@ -598,33 +634,58 @@
             pltpu.VMEM((ROWS, 3 * D), low),
             pltpu.VMEM((D, DENSE), low),
             pltpu.SemaphoreType.DMA((16,)),
-            pltpu.SemaphoreType.DMA((17,)),
+            pltpu.SemaphoreType.DMA((29,)),
+            pltpu.VMEM((2, 16, BLOCK, WIDE), low),
+            pltpu.VMEM((2, 4, 16, WIDE), full),
         ],
         compiler_params=params(48),
         cost_estimate=pl.CostEstimate(
-            flops=40 * 10**9, bytes_accessed=18 * 10**6, transcendentals=10**4
+            flops=400 * 10**9, bytes_accessed=18 * 10**6, transcendentals=10**4
         ),
         name="token_backward",
     )(*args[:5], *pinned(args[5:]))
 
 
-def owner_step(pieces, arrays):
+def owner_step(pieces, arrays, small):
     qkv = pl.BlockSpec((OWN, D), lambda i: (0, jnp.minimum(i, 2)))
     proj = pl.BlockSpec((OWN, D), lambda i: (0, 0))
+    whole = [pl.BlockSpec(a.shape, lambda i: (0, 0)) for a in small]
     return pl.pallas_call(
         owner_kernel,
         grid=(4,),
-        out_shape=tuple(hbm(*a.shape) for a in arrays),
-        in_specs=[pl.BlockSpec((2, 2, PIECE, WIDE), lambda i: (0, i, 0, 0))]
+        out_shape=tuple([hbm(*a.shape) for a in arrays] + [shape(*a.shape) for a in small]),
+        in_specs=[
+            pl.BlockSpec((2, 2, PIECE + 1, WIDE), lambda i: (0, i, 0, 0)),
+            pl.BlockSpec((2, 8, PIECE + 1, WIDE), lambda i: (0, 0, 0, 0)),
+        ]
         + [qkv] * 3
-        + [proj] * 3,
-        out_specs=(qkv,) * 3 + (proj,) * 3,
-        compiler_params=params(16),
+        + [proj] * 3
+        + whole,
+        out_specs=tuple([qkv] * 3 + [proj] * 3 + whole),
+        compiler_params=params(24),
         cost_estimate=pl.CostEstimate(
             flops=10**7, bytes_accessed=8 * 10**6, transcendentals=10**6
         ),
         name="owner_step",
-    )(pieces, *pinned(arrays))
+    )(pieces, pieces, *pinned(arrays), *small)
+
+
+def exchange(value):
+    return lax.all_to_all(value, "exp", split_axis=0, concat_axis=0, tiled=True)
+
+
+def dense_sum(keep, give):
+    def along(step, value):
+        hops = [(2 * x + c, 2 * ((x + step) % 4) + c) for x in range(4) for c in range(2)]
+        return lax.ppermute(value, "grp", hops)
+
+    got = lax.ppermute(give, "grp", [(i, i ^ 1) for i in range(GRP)])
+    pieces = exchange((keep.astype(full) + got.astype(full)).astype(low))
+    total = jnp.sum(pieces.astype(full), axis=0)
+    main, rest = total[: 4 * PIECE].reshape(4, PIECE, WIDE), total[4 * PIECE :][:4, None]
+    total = jnp.concatenate([main, rest], axis=1)
+    sent = [along(step, total[step].astype(low)).astype(full) for step in (1, 2, 3)]
+    return total[0] + sent[0] + sent[1] + sent[2]
 
 
 def on_device(
@@ -654,7 +715,7 @@
     pieces = dense_pieces(*pack(qkv_master, proj_master, router_master, norm_master))
     rows = piece_rows(lax.axis_index("grp"))
     mine = jnp.concatenate([inner_master[0].astype(low), outer_master[0].astype(low).T], axis=1)
-    mine, *_ = lax.optimization_barrier((mine, pieces[2], pieces[5]))
+    mine, *_ = lax.optimization_barrier((mine, pieces[3], pieces[4]))
     weights = lax.all_gather(mine, "grp", axis=0, tiled=True)
 
     ids = expert_ids.reshape(TOK, 2)
@@ -671,58 +732,11 @@
     send, m, a, qkv, p, o, c, r = token_forward(
         rows, ids, keep, target.T, images, cotangent, *pieces
     )
-    got = lax.all_to_all(send, "exp", split_axis=0, concat_axis=0, tiled=True)
-    back, *kept_parts = experts_both_ways(got, weights)
-    h, du, xt, dzt = kept_parts
-    back = lax.all_to_all(back, "exp", split_axis=0, concat_axis=0, tiled=True)
-    head = expert_grads(0, xt, dzt, h, du)
-    tail = expert_grads(1, xt, dzt, h, du)
-    head = lax.psum_scatter(head, "grp", scatter_dimension=0, tiled=True)
-    result, image_grad, grads, extra = token_backward(
+    back, *hidden = experts_both_ways(exchange(send), weights)
+    back = exchange(back)
+    grad = lax.psum_scatter(expert_grads(*hidden), "grp", scatter_dimension=0, tiled=True)
+    result, image_grad, keep_grads, give_grads = token_backward(
         rows, ids, target, keep, back, m, r, cotangent, c, o, qkv, p, a, images, *pieces
-    )
-    grads, head = lax.optimization_barrier((grads, head))
-    grads = lax.psum_scatter(
-        grads.reshape(GRP * 16 * PIECE, WIDE), "grp", scatter_dimension=0, tiled=True
-    )
-    experts = (
-        inner_master,
-        inner_first,
-        inner_second,
-        outer_master,
-        outer_first,
-        outer_second,
-    )
-    partial = expert_step(0, head, experts, ())
-
-    extra = jnp.moveaxis(extra.reshape(24, GRP, OWN), 1, 0)
-    extra = lax.all_to_all(extra, "grp", split_axis=0, concat_axis=0, tiled=True)
-    extra = jnp.broadcast_to(jnp.sum(extra, axis=0)[None], (EXPERTS, 24, OWN))
-    extra = lax.all_to_all(extra, "exp", split_axis=0, concat_axis=0, tiled=True)
-    extra = jnp.sum(extra, axis=0).T
-    grads, tail, extra = lax.optimization_barrier((grads, tail, extra))
-    tail = lax.psum_scatter(tail, "grp", scatter_dimension=0, tiled=True)
-
-    pieces = lax.all_to_all(
-        grads.reshape(16, PIECE, WIDE), "exp", split_axis=0, concat_axis=0, tiled=True
-    )
-    piece = jnp.sum(pieces.astype(full), axis=0).astype(low)
-    pieces = lax.all_to_all(
-        jnp.broadcast_to(piece[None], (16, PIECE, WIDE)),
-        "exp",
-        split_axis=0,
-        concat_axis=0,
-        tiled=True,
-    )
-    qkv_moment, qkv_square, qkv_weight, proj_moment, proj_square, proj_weight = owner_step(
-        pieces.reshape(2, 8, PIECE, WIDE),
-        (qkv_master, qkv_first, qkv_second, proj_master, proj_first, proj_second),
-    )
-    router_moment, router_square, router_weight = adamw(
-        router_master, router_first, router_second, extra[:, 0:16], 0.03
-    )
-    norm_moment, norm_square, norm_weight = adamw(
-        norm_master, norm_first, norm_second, extra[:, 16:20], 0.3
     )
     (
         inner_moment,
@@ -731,7 +745,22 @@
         outer_moment,
         outer_square,
         outer_weight,
-    ) = expert_step(1, tail, experts, partial)
+    ) = expert_step(
+        grad,
+        (inner_master, inner_first, inner_second, outer_master, outer_first, outer_second),
+    )
+    block = dense_sum(keep_grads, give_grads).astype(low)
+    block = exchange(jnp.broadcast_to(block[None], (16, PIECE + 1, WIDE)))
+    block, inner_weight = lax.optimization_barrier((block, inner_weight))
+    small = (router_master, router_first, router_second, norm_master, norm_first, norm_second)
+    new = owner_step(
+        block.reshape(2, 8, PIECE + 1, WIDE),
+        (qkv_master, qkv_first, qkv_second, proj_master, proj_first, proj_second),
+        [value.T for value in small],
+    )
+    qkv_moment, qkv_square, qkv_weight, proj_moment, proj_square, proj_weight = new[:6]
+    router_moment, router_square, router_weight = [value.T for value in new[6:9]]
+    norm_moment, norm_square, norm_weight = [value.T for value in new[9:]]
     return (
         result,
         image_grad,

time: 250 us -> 237 us (0.948)
  blocking collectives: 89.4 us -> 69.9 us
  waiting for transfers between devices: 32.5 us -> 43.5 us
  Pallas kernels: 71.6 us -> 65.5 us
  local copies, waits for them, and re-layouts: 11 us -> 6.54 us
  starting transfers between devices: 23.7 us -> 27.6 us
    all_to_all x4 -> x2, blocking collectives: 89.4 us -> 69.9 us  [exchange(): return lax.all_to_all(value, 'exp', split_axis=0, concat_axis=0, tiled=True)]
    all_to_all x2, waiting for transfers between devices: 1.2 us -> 16.9 us  [exchange(): return lax.all_to_all(value, 'exp', split_axis=0, concat_axis=0, tiled=True)]
    reduce_scatter x3 -> x1, waiting for transfers between devices: 14.7 us -> 0.02 us  [on_device(): lax.psum_scatter(expert_grads(*hidden), 'grp', scatter_dimension=0, tiled...]
    ppermute x0 -> x1, waiting for transfers between devices: none -> 4.94 us  [dense_sum(): got = lax.ppermute(give, 'grp', [(i, i ^ 1) for i in range(GRP)])]
    ppermute x6 -> x9, waiting for transfers between devices: 15.1 us -> 19.7 us  [along(): return lax.ppermute(value, 'grp', hops)]
    pallas_call x2 -> x1, Pallas kernels: 16.1 us -> 11.8 us  [expert_grads(): pl.pallas_call(expert_grad_kernel, grid=(GRP // 2,), out_shape=hbm(GRP *...]
    unnamed x58 -> x54, local copies, waits for them, and re-layouts: 8.63 us -> 4.86 us
    ppermute x6 -> x9, starting transfers between devices: 8.82 us -> 11.7 us  [along(): return lax.ppermute(value, 'grp', hops)]
  transfers between devices with their start and end apart: 20 -> 22, of which waited for: 10 -> 11; matrix products, arithmetic and copies ran while one was open for 4% -> 4% of each run, Pallas kernels for 16% -> 18%
where the time goes in v3:
time: 237 us; the launch traced here: 233 us
  blocking collectives  69.9 us (29%)
  Pallas kernels  65.5 us (28%)
  waiting for transfers between devices  43.5 us (18%)
  starting transfers between devices  27.6 us (12%)
  between operations  14.5 us (6%)
  local copies, waits for them, and re-layouts  6.54 us (3%)
  other arithmetic  5.47 us (2%)
    all_to_all x2, blocking collectives, exchange(): return lax.all_to_all(value, 'exp', split_axis=0, concat_axis=0, tiled=True)  69.9 us
    ppermute x9, waiting for transfers between devices, along(): return lax.ppermute(value, 'grp', hops)  19.7 us
    all_to_all x2, waiting for transfers between devices, exchange(): return lax.all_to_all(value, 'exp', split_axis=0, concat_axis=0, tiled=True)  16.9 us
    pallas_call x1, Pallas kernels, experts_both_ways(): pl.pallas_call(expert_kernel, grid=(GRP // 2,), out_shape=(pltpu.VMEM((EX...  16.5 us
    pallas_call x1, Pallas kernels, token_backward(): pl.pallas_call(backward_kernel, out_shape=outs, in_specs=[in_smem()] + in...  14.2 us
    pallas_call x1, Pallas kernels, expert_grads(): pl.pallas_call(expert_grad_kernel, grid=(GRP // 2,), out_shape=hbm(GRP *...  11.8 us
    ppermute x9, starting transfers between devices, along(): return lax.ppermute(value, 'grp', hops)  11.7 us
    pallas_call x1, Pallas kernels, expert_step(): pl.pallas_call(expert_step_kernel, grid=(D // 128,), out_shape=tuple((hbm...  8.04 us
  transfers between devices with their start and end apart: 22, of which 11 were waited for; matrix products, arithmetic and copies ran while one was open for 4% of the time, Pallas kernels for 18%

profile of v3, /device:TPU:1, one launch (start us, length us, event | category | flops | bytes accessed | tf_op | source)
XLA Modules:
  0.0 233.1 jit_solution(8989794495971008189)
XLA Ops:
  7.2 0.0 all-gather.2.cloned.1.call-start
  7.3 1.5 pack.1
  8.7 0.0 copy-start.7
  8.8 2.1 collective-permute-start
  10.9 1.3 collective-permute-start.1
  12.2 1.1 copy.55
  13.3 5.4 %collective-permute-done.refs_2_.refs_11_ = bf16[48,3200]{1,0:T(8,128)(2,1)S(1)} collective-permute-done((bf16[48,3200]{1,0:T(8,128)(2,1)S(1)}, bf16[48,3200]{1,0:T(8,128)(2,1)S(1)}, u32[]{:S(2)}, u32[]{:S(2)}) %collective-permute-start) | collective-permute-done | bytes 307232 | tf_op jit(solution)/shard_map/ppermute | solution.py:79
  18.7 0.1 collective-permute-done.1.refs_5_.refs_14_
  18.8 1.2 collective-permute-start.2
  20.0 1.5 collective-permute-start.3
  21.5 0.1 convert_bitcast_fusion.1
  21.6 1.1 pad_maximum_fusion
  22.7 4.2 %collective-permute-done.2.refs_3_.refs_12_ = bf16[48,3200]{1,0:T(8,128)(2,1)S(1)} collective-permute-done((bf16[48,3200]{1,0:T(8,128)(2,1)S(1)}, bf16[48,3200]{1,0:T(8,128)(2,1)S(1)}, u32[]{:S(2)}, u32[]{:S(2)}) %collective-permute-start.2) | collective-permute-done | bytes 307232 | tf_op jit(solution)/shard_map/ppermute | solution.py:79
  26.9 0.0 all-gather.2.cloned.1.call-update
  27.0 2.9 %collective-permute-start.6 = (bf16[48,3200]{1,0:T(8,128)(2,1)S(1)}, bf16[48,3200]{1,0:T(8,128)(2,1)S(1)}, u32[]{:S(2)}, u32[]{:S(2)}) collective-permute-start(bf16[48,3200]{1,0:T(8,128)(2,1)S(1)} %get-tuple-element.68.refs_0_.refs_9_), channel_id=1, source_target_pairs={{0,16},{16,0},{32,48},{48,32},{64,80},{80,64},{96,112},{112,96},{1... | collective-permute-start | bytes 921608 | tf_op jit(solution)/shard_map/ppermute | solution.py:82
  29.8 0.1 collective-permute-start.7
  29.9 0.1 copy.48
  30.1 0.1 eq.32
  30.2 1.2 reduce-window.6
  31.4 0.2 slice_reduce_fusion
  31.6 0.1 bitcast_bitcast_fusion
  31.7 0.4 collective-permute-start.8
  32.2 0.9 collective-permute-start.4
  33.1 1.8 collective-permute-start.5
  34.9 0.1 reshape.77
  35.0 0.1 copy.49
  35.2 0.7 collective-permute-start.11
  36.0 0.1 collective-permute-start.9
  36.1 0.4 collective-permute-start.10
  36.5 5.7 %collective-permute-done.4.refs_6_.refs_15_ = bf16[48,3200]{1,0:T(8,128)(2,1)S(1)} collective-permute-done((bf16[48,3200]{1,0:T(8,128)(2,1)S(1)}, bf16[48,3200]{1,0:T(8,128)(2,1)S(1)}, u32[]{:S(2)}, u32[]{:S(2)}) %collective-permute-start.4) | collective-permute-done | bytes 307232 | tf_op jit(solution)/shard_map/ppermute | solution.py:79
  42.2 0.9 collective-permute-start.12
  43.1 0.1 collective-permute-start.13
  43.2 0.1 copy.54.trow_ref
  43.3 0.1 stack.75.rows_ref
  43.5 1.2 collective-permute-done.12.refs_14_.refs_23_
  44.7 0.8 collective-permute-done.13.refs_15_.refs_24_
  45.5 0.7 copy-done.24
  46.3 8.0 %token_forward.1 = (bf16[16,33,1536]{2,1,0:T(8,128)(2,1)S(1)}, f32[208,768]{1,0:T(8,128)}, bf16[208,768]{1,0:T(8,128)(2,1)}, bf16[208,2304]{1,0:T(8,128)(2,1)}, ...) custom-call(s32[18]{0:T(128)S(1)} %stack.75.rows_ref, ...), custom_call_target="tpu_custom_call" | custom-call | flops 4000000000 | bytes 12000000 | tf_op jit(solution)/shard_map/token_forward/pallas_call | solution.py:551
  54.3 34.4 %all_to_all.20.got_ref = bf16[16,33,1536]{2,1,0:T(8,128)(2,1)S(1)} all-to-all(bf16[16,33,1536]{2,1,0:T(8,128)(2,1)S(1)} %get-tuple-element.70), channel_id=1, replica_groups=mesh['grp'=8,'exp'=16] {'exp'}, dimensions={0} | all-to-all | bytes 3244032 | tf_op jit(solution)/shard_map/all_to_all | solution.py:674
  88.7 16.5 %experts.1 = (bf16[16,33,1536]{2,1,0:T(8,128)(2,1)S(1)}, bf16[528,3072]{1,0:T(8,128)(2,1)}, bf16[528,3072]{1,0:T(8,128)(2,1)}, bf16[768,528]{1,0:T(8,128)(2,1)}, bf16[768,528]{1,0:T(8,128)(2,1)}) custom-call(bf16[16,33,1536]{2,1,0:T(8,128)(2,1)S(1)} %all_to_all.20.got_ref, bf16[6144,768]{1,0:T(8,128)(2,1)} %all-gather.2.cloned.1.call-done.w_ref), custom_call_target="tpu_custom_call" | custom-call | flops 10000000000 | bytes 23000000 | tf_op jit(solution)/shard_map/experts/pallas_call | solution.py:580
  105.2 1.3 copy-done
  106.5 4.3 %all-to-all-start.1 = ((bf16[16,33,1536]{2,1,0:T(8,128)(2,1)}), bf16[16,33,1536]{2,1,0:T(8,128)(2,1)S(1)}, u32[]{:S(2)}, u32[]{:S(2)}) async-start(bf16[16,33,1536]{2,1,0:T(8,128)(2,1)} %copy-done), calls=%async_computation.1 | async-start | bytes 3932160 | tf_op jit(solution)/shard_map/all_to_all | solution.py:674
  110.8 0.0 reduce-scatter.2.cloned.1.call-start
  110.8 11.8 %expert_grads.1 = bf16[6144,768]{1,0:T(8,128)(2,1)} custom-call(bf16[528,3072]{1,0:T(8,128)(2,1)} %get-tuple-element.84.h_ref, bf16[528,3072]{1,0:T(8,128)(2,1)} %get-tuple-element.85.du_ref, bf16[768,528]{1,0:T(8,128)(2,1)} %get-tuple-element.86.xt_ref, bf16[768,528]{1,0:T(8,128)(2,1)} %get-tuple-element.87.dzt_ref), custom_call_target="tpu_custom_call" | custom-call | flops 6000000000 | bytes 18000000 | tf_op jit(solution)/shard_map/expert_grads/pallas_call | solution.py:602
  122.6 0.0 reduce-scatter.2.cloned.1.call-update
  122.6 16.5 %all-to-all-done.1.back_ref = bf16[16,33,1536]{2,1,0:T(8,128)(2,1)S(1)} async-done(((bf16[16,33,1536]{2,1,0:T(8,128)(2,1)}), bf16[16,33,1536]{2,1,0:T(8,128)(2,1)S(1)}, u32[]{:S(2)}, u32[]{:S(2)}) %all-to-all-start.1) | async-done | bytes 1622048 | tf_op jit(solution)/shard_map/all_to_all | solution.py:674
  139.1 14.2 %token_backward.1 = (bf16[1,197,768]{2,1,0:T(8,128)(2,1)}, f32[1,197,768]{2,1,0:T(8,128)}, bf16[16,208,384]{2,1,0:T(8,128)(2,1)}, bf16[16,208,384]{2,1,0:T(8,128)(2,1)}) custom-call(s32[18]{0:T(128)S(1)} %stack.75.rows_ref, s32[208,2]{1,0:T(8,128)S(1)} %pad.15.ids_ref, s32[208,2]{1,0:T(8,128)S(1)} %get-tuple-element.152.tcol_ref, ...), custom_call_target="tpu_custom_call" | custom-call | flops 399999991808 | bytes 18000000 | tf_op jit(solution)/shard_map/token_backward/pallas_call | solution.py:623
  153.3 2.3 collective-permute-start.14
  155.7 4.9 %collective-permute-done.14 = bf16[16,208,384]{2,1,0:T(8,128)(2,1)S(1)} collective-permute-done((bf16[16,208,384]{2,1,0:T(8,128)(2,1)}, bf16[16,208,384]{2,1,0:T(8,128)(2,1)S(1)}, u32[]{:S(2)}, u32[]{:S(2)}) %collective-permute-start.14) | collective-permute-done | bytes 2555936 | tf_op jit(solution)/shard_map/ppermute | solution.py:682
  160.6 2.5 %add_convert_fusion = bf16[16,208,384]{2,1,0:T(8,128)(2,1)S(1)} fusion(bf16[16,208,384]{2,1,0:T(8,128)(2,1)S(1)} %collective-permute-done.14, bf16[16,208,384]{2,1,0:T(8,128)(2,1)} %get-tuple-element.82), kind=kLoop, calls=%fused_computation.1 | loop fusion | flops 5111808 | bytes 7667712 | tf_op jit(solution)/shard_map/convert_element_type | solution.py:683
  163.1 35.5 %all_to_all.21 = bf16[16,208,384]{2,1,0:T(8,128)(2,1)S(1)} all-to-all(bf16[16,208,384]{2,1,0:T(8,128)(2,1)S(1)} %add_convert_fusion), channel_id=1, replica_groups=mesh['grp'=8,'exp'=16] {'exp'}, dimensions={0} | all-to-all | bytes 5111808 | tf_op jit(solution)/shard_map/all_to_all | solution.py:674
  198.6 0.4 convert_reduce_fusion
  199.1 0.3 collective-permute-start.15
  199.4 2.4 %collective-permute-start.17 = (bf16[49,384]{1,0:T(8,128)(2,1)S(1)}, bf16[49,384]{1,0:T(8,128)(2,1)S(1)}, u32[]{:S(2)}, u32[]{:S(2)}) collective-permute-start(bf16[49,384]{1,0:T(8,128)(2,1)S(1)} %get-tuple-element.149), channel_id=1, source_target_pairs={{0,96},{16,112},{32,0},{48,16},{64,32},{80,48},{96,64},{112,80},{1... | collective-permute-start | bytes 112904 | tf_op jit(solution)/shard_map/ppermute | solution.py:680
  201.9 0.2 collective-permute-start.16
  202.0 1.2 collective-permute-done.15
  203.3 3.0 %collective-permute-done.16 = bf16[49,384]{1,0:T(8,128)(2,1)S(1)} collective-permute-done((bf16[49,384]{1,0:T(8,128)(2,1)S(1)}, bf16[49,384]{1,0:T(8,128)(2,1)S(1)}, u32[]{:S(2)}, u32[]{:S(2)}) %collective-permute-start.16) | collective-permute-done | bytes 37664 | tf_op jit(solution)/shard_map/ppermute | solution.py:680
  206.3 0.9 broadcast_in_dim.16
  207.2 3.6 %all-to-all-start.3 = ((bf16[16,49,384]{2,1,0:T(8,128)(2,1)}), bf16[16,49,384]{2,1,0:T(8,128)(2,1)S(1)}, u32[]{:S(2)}, u32[]{:S(2)}) async-start(bf16[16,49,384]{2,1,0:T(8,128)(2,1)} %broadcast_in_dim.16), calls=%async_computation.3 | async-start | bytes 1376256 | tf_op jit(solution)/shard_map/all_to_all | solution.py:674
  210.8 1.4 copy.56
  212.3 0.0 reduce-scatter.2.cloned.1.call-done.grad_ref
  212.3 8.0 %expert_step.1 = (f32[1,768,384]{2,1,0:T(8,128)}, f32[1,768,384]{2,1,0:T(8,128)}, f32[1,768,384]{2,1,0:T(8,128)}, f32[1,384,768]{2,1,0:T(8,128)}, f32[1,384,768]{2,1,0:T(8,128)}, /*index=5*/f32[1,384,768]{2,1,0:T(8,128)}) custom-call(bf16[768,768]{1,0:T(8,128)(2,1)} %reduce-scatter.2.cloned.1.call-done.grad_ref, f32[1,768,384]{2,1,0:T(8,128)} %refs_0_.2, ...), custom_call_target="tpu_custom_call" | custom-call | flops 10000000 | bytes 8000000 | tf_op jit(solution)/shard_map/expert_step/pallas_call | solution.py:475
  220.4 0.4 all-to-all-done.3
  220.8 5.5 %owner_step.1 = (f32[96,2304]{1,0:T(8,128)}, f32[96,2304]{1,0:T(8,128)}, f32[96,2304]{1,0:T(8,128)}, f32[96,768]{1,0:T(8,128)}, f32[96,768]{1,0:T(8,128)}, /*ind...) custom-call(bf16[2,8,49,384]{3,2,1,0:T(8,128)(2,1)S(1)} %bitcast.75,, ...), custom_call_target="tpu_custom_call" | custom-call | flops 10000000 | bytes 8000000 | tf_op jit(solution)/shard_map/owner_step/pallas_call | solution.py:653
  (73 shorter events, 0.4 us)
Async XLA Ops:
  7.2 5.0 %copy-start.9 = (f32[1,384,768]{2,1,0:T(8,128)S(1)}, f32[1,384,768]{2,1,0:T(8,128)}, u32[]{:S(2)}) copy-start(f32[1,384,768]{2,1,0:T(8,128)} %refs_3_.2) | copy-start | bytes 3538948
  7.2 14.3 %copy-start.10 = (f32[1,768,384]{2,1,0:T(8,128)S(1)}, f32[1,768,384]{2,1,0:T(8,128)}, u32[]{:S(2)}) copy-start(f32[1,768,384]{2,1,0:T(8,128)} %refs_0_.2) | copy-start | bytes 3538948
  7.2 81.5 %all-gather.2.cloned.1.call-start = ((), (), s32[]{:S(2)}) async-start(), calls=%async_computation.5 | async-start | bytes 10616832 | tf_op jit(solution)/shard_map/all_gather | solution.py:719
  8.7 18.2 %copy-start.7 = (bf16[48,3200]{1,0:T(8,128)(2,1)}, bf16[48,3200]{1,0:T(8,128)(2,1)S(1)}, u32[]{:S(2)}) copy-start(bf16[48,3200]{1,0:T(8,128)(2,1)S(1)} %get-tuple-element.68.refs_0_.refs_9_) | copy-start | bytes 921604
  8.8 21.1 %copy-start.8 = (bf16[48,3200]{1,0:T(8,128)(2,1)}, bf16[48,3200]{1,0:T(8,128)(2,1)S(1)}, u32[]{:S(2)}) copy-start(bf16[48,3200]{1,0:T(8,128)(2,1)S(1)} %get-tuple-element.67.refs_1_.refs_10_) | copy-start | bytes 921604
  8.8 9.9 %collective-permute-start = (bf16[48,3200]{1,0:T(8,128)(2,1)S(1)}, bf16[48,3200]{1,0:T(8,128)(2,1)S(1)}, u32[]{:S(2)}, u32[]{:S(2)}) collective-permute-start(bf16[48,3200]{1,0:T(8,128)(2,1)S(1)} %get-tuple-element.68.refs_0_.refs_9_), channel_id=1, source_target_pairs={{0,32},{16,48},{32,64},{48,80},{64,96},{80,112},{96,0},{112,16},{1... | collective-permute-start | bytes 921608 | tf_op jit(solution)/shard_map/ppermute | solution.py:79
  10.9 7.9 %collective-permute-start.1 = (bf16[48,3200]{1,0:T(8,128)(2,1)S(1)}, bf16[48,3200]{1,0:T(8,128)(2,1)}, u32[]{:S(2)}, u32[]{:S(2)}) collective-permute-start(bf16[48,3200]{1,0:T(8,128)(2,1)S(1)} %get-tuple-element.67.refs_1_.refs_10_), channel_id=1, source_target_pairs={{0,96},{16,112},{32,0},{48,16},{64,32},{80,48},{96,64},{112,80},{1... | collective-permute-start | bytes 921608 | tf_op jit(solution)/shard_map/ppermute | solution.py:79
  13.3 8.3 %copy-start.11 = (bf16[1,384,768]{1,2,0:T(8,128)(2,1)S(1)}, bf16[1,384,768]{1,2,0:T(8,128)(2,1)}, u32[]{:S(2)}) copy-start(bf16[1,384,768]{1,2,0:T(8,128)(2,1)} %copy.55) | copy-start | bytes 1769476
  18.7 13.5 %copy-start.15 = (bf16[48,3200]{1,0:T(8,128)(2,1)}, bf16[48,3200]{1,0:T(8,128)(2,1)S(1)}, u32[]{:S(2)}) copy-start(bf16[48,3200]{1,0:T(8,128)(2,1)S(1)} %collective-permute-done.refs_2_.refs_11_) | copy-start | bytes 921604
  18.8 8.1 %collective-permute-start.2 = (bf16[48,3200]{1,0:T(8,128)(2,1)S(1)}, bf16[48,3200]{1,0:T(8,128)(2,1)S(1)}, u32[]{:S(2)}, u32[]{:S(2)}) collective-permute-start(bf16[48,3200]{1,0:T(8,128)(2,1)S(1)} %get-tuple-element.67.refs_1_.refs_10_), channel_id=1, source_target_pairs={{0,32},{16,48},{32,64},{48,80},{64,96},{80,112},{96,0},{112,16},{1... | collective-permute-start | bytes 921608 | tf_op jit(solution)/shard_map/ppermute | solution.py:79
  20.0 6.9 %collective-permute-start.3 = (bf16[48,3200]{1,0:T(8,128)(2,1)S(1)}, bf16[48,3200]{1,0:T(8,128)(2,1)S(1)}, u32[]{:S(2)}, u32[]{:S(2)}) collective-permute-start(bf16[48,3200]{1,0:T(8,128)(2,1)S(1)} %get-tuple-element.68.refs_0_.refs_9_), channel_id=1, source_target_pairs={{0,96},{16,112},{32,0},{48,16},{64,32},{80,48},{96,64},{112,80},{1... | collective-permute-start | bytes 921608 | tf_op jit(solution)/shard_map/ppermute | solution.py:79
  21.6 8.4 %copy-start.13 = (s32[1,197,2]{1,2,0:T(2,128)S(1)}, s32[1,197,2]{1,2,0:T(2,128)}, u32[]{:S(2)}) copy-start(s32[1,197,2]{1,2,0:T(2,128)} %param.24) | copy-start | bytes 4732
  21.6 13.5 %copy-start.14 = (s32[1,197,2]{1,2,0:T(2,128)S(1)}, s32[1,197,2]{1,2,0:T(2,128)}, u32[]{:S(2)}) copy-start(s32[1,197,2]{1,2,0:T(2,128)} %param.25) | copy-start | bytes 4732
  26.9 18.6 %copy-start.16 = (bf16[48,3200]{1,0:T(8,128)(2,1)}, bf16[48,3200]{1,0:T(8,128)(2,1)S(1)}, u32[]{:S(2)}) copy-start(bf16[48,3200]{1,0:T(8,128)(2,1)S(1)} %collective-permute-done.2.refs_3_.refs_12_) | copy-start | bytes 921604
  26.9 18.6 %copy-start.17 = (bf16[48,3200]{1,0:T(8,128)(2,1)}, bf16[48,3200]{1,0:T(8,128)(2,1)S(1)}, u32[]{:S(2)}) copy-start(bf16[48,3200]{1,0:T(8,128)(2,1)S(1)} %collective-permute-done.3.refs_4_.refs_13_) | copy-start | bytes 921604
  27.0 8.3 %collective-permute-start.6 = (bf16[48,3200]{1,0:T(8,128)(2,1)S(1)}, bf16[48,3200]{1,0:T(8,128)(2,1)S(1)}, u32[]{:S(2)}, u32[]{:S(2)}) collective-permute-start(bf16[48,3200]{1,0:T(8,128)(2,1)S(1)} %get-tuple-element.68.refs_0_.refs_9_), channel_id=1, source_target_pairs={{0,16},{16,0},{32,48},{48,32},{64,80},{80,64},{96,112},{112,96},{1... | collective-permute-start | bytes 921608 | tf_op jit(solution)/shard_map/ppermute | solution.py:82
  29.8 6.1 %collective-permute-start.7 = (bf16[48,3200]{1,0:T(8,128)(2,1)S(1)}, bf16[48,3200]{1,0:T(8,128)(2,1)S(1)}, u32[]{:S(2)}, u32[]{:S(2)}) collective-permute-start(bf16[48,3200]{1,0:T(8,128)(2,1)S(1)} %get-tuple-element.67.refs_1_.refs_10_), channel_id=1, source_target_pairs={{0,16},{16,0},{32,48},{48,32},{64,80},{80,64},{96,112},{112,96},{1... | collective-permute-start | bytes 921608 | tf_op jit(solution)/shard_map/ppermute | solution.py:82
  31.7 4.4 %collective-permute-start.8 = (bf16[48,3200]{1,0:T(8,128)(2,1)S(1)}, bf16[48,3200]{1,0:T(8,128)(2,1)S(1)}, u32[]{:S(2)}, u32[]{:S(2)}) collective-permute-start(bf16[48,3200]{1,0:T(8,128)(2,1)S(1)} %collective-permute-done.refs_2_.refs_11_), channel_id=1, source_target_pairs={{0,16},{16,0},{32,48},{48,32},{64,80},{80,64},{96,112},{112,96},{1... | collective-permute-start | bytes 921608 | tf_op jit(solution)/shard_map/ppermute | solution.py:82
  32.2 10.0 %collective-permute-start.4 = (bf16[48,3200]{1,0:T(8,128)(2,1)S(1)}, bf16[48,3200]{1,0:T(8,128)(2,1)S(1)}, u32[]{:S(2)}, u32[]{:S(2)}) collective-permute-start(bf16[48,3200]{1,0:T(8,128)(2,1)S(1)} %collective-permute-done.refs_2_.refs_11_), channel_id=1, source_target_pairs={{0,32},{16,48},{32,64},{48,80},{64,96},{80,112},{96,0},{112,16},{1... | collective-permute-start | bytes 921608 | tf_op jit(solution)/shard_map/ppermute | solution.py:79
  33.1 10.0 %collective-permute-start.5 = (bf16[48,3200]{1,0:T(8,128)(2,1)}, bf16[48,3200]{1,0:T(8,128)(2,1)}, u32[]{:S(2)}, u32[]{:S(2)}) collective-permute-start(bf16[48,3200]{1,0:T(8,128)(2,1)} %collective-permute-done.1.refs_5_.refs_14_), channel_id=1, source_target_pairs={{0,96},{16,112},{32,0},{48,16},{64,32},{80,48},{96,64},{112,80},{1... | collective-permute-start | bytes 921608 | tf_op jit(solution)/shard_map/ppermute | solution.py:79
  35.2 10.2 %copy-start.18 = (bf16[48,3200]{1,0:T(8,128)(2,1)}, bf16[48,3200]{1,0:T(8,128)(2,1)S(1)}, u32[]{:S(2)}) copy-start(bf16[48,3200]{1,0:T(8,128)(2,1)S(1)} %collective-permute-done.6.refs_8_.refs_17_) | copy-start | bytes 921604
  35.2 8.2 %collective-permute-start.11 = (bf16[48,3200]{1,0:T(8,128)(2,1)}, bf16[48,3200]{1,0:T(8,128)(2,1)S(1)}, u32[]{:S(2)}, u32[]{:S(2)}) collective-permute-start(bf16[48,3200]{1,0:T(8,128)(2,1)} %collective-permute-done.1.refs_5_.refs_14_), channel_id=1, source_target_pairs={{0,16},{16,0},{32,48},{48,32},{64,80},{80,64},{96,112},{112,96},{1... | collective-permute-start | bytes 921608 | tf_op jit(solution)/shard_map/ppermute | solution.py:82
  36.0 9.5 %copy-start.19 = (bf16[48,3200]{1,0:T(8,128)(2,1)}, bf16[48,3200]{1,0:T(8,128)(2,1)S(1)}, u32[]{:S(2)}) copy-start(bf16[48,3200]{1,0:T(8,128)(2,1)S(1)} %collective-permute-done.7.refs_9_.refs_18_) | copy-start | bytes 921604
  36.0 7.5 %collective-permute-start.9 = (bf16[48,3200]{1,0:T(8,128)(2,1)S(1)}, bf16[48,3200]{1,0:T(8,128)(2,1)}, u32[]{:S(2)}, u32[]{:S(2)}) collective-permute-start(bf16[48,3200]{1,0:T(8,128)(2,1)S(1)} %collective-permute-done.2.refs_3_.refs_12_), channel_id=1, source_target_pairs={{0,16},{16,0},{32,48},{48,32},{64,80},{80,64},{96,112},{112,96},{1... | collective-permute-start | bytes 921608 | tf_op jit(solution)/shard_map/ppermute | solution.py:82
  36.1 9.4 %copy-start.20 = (bf16[48,3200]{1,0:T(8,128)(2,1)}, bf16[48,3200]{1,0:T(8,128)(2,1)S(1)}, u32[]{:S(2)}) copy-start(bf16[48,3200]{1,0:T(8,128)(2,1)S(1)} %collective-permute-done.8.refs_10_.refs_19_) | copy-start | bytes 921604
  36.1 7.4 %collective-permute-start.10 = (bf16[48,3200]{1,0:T(8,128)(2,1)S(1)}, bf16[48,3200]{1,0:T(8,128)(2,1)}, u32[]{:S(2)}, u32[]{:S(2)}) collective-permute-start(bf16[48,3200]{1,0:T(8,128)(2,1)S(1)} %collective-permute-done.3.refs_4_.refs_13_), channel_id=1, source_target_pairs={{0,16},{16,0},{32,48},{48,32},{64,80},{80,64},{96,112},{112,96},{1... | collective-permute-start | bytes 921608 | tf_op jit(solution)/shard_map/ppermute | solution.py:82
  42.2 3.3 %copy-start.21 = (bf16[48,3200]{1,0:T(8,128)(2,1)}, bf16[48,3200]{1,0:T(8,128)(2,1)S(1)}, u32[]{:S(2)}) copy-start(bf16[48,3200]{1,0:T(8,128)(2,1)S(1)} %collective-permute-done.4.refs_6_.refs_15_) | copy-start | bytes 921604
  42.2 2.5 %collective-permute-start.12 = (bf16[48,3200]{1,0:T(8,128)(2,1)S(1)}, bf16[48,3200]{1,0:T(8,128)(2,1)S(1)}, u32[]{:S(2)}, u32[]{:S(2)}) collective-permute-start(bf16[48,3200]{1,0:T(8,128)(2,1)S(1)} %collective-permute-done.4.refs_6_.refs_15_), channel_id=1, source_target_pairs={{0,16},{16,0},{32,48},{48,32},{64,80},{80,64},{96,112},{112,96},{1... | collective-permute-start | bytes 921608 | tf_op jit(solution)/shard_map/ppermute | solution.py:82
  43.1 2.4 %collective-permute-start.13 = (bf16[48,3200]{1,0:T(8,128)(2,1)}, bf16[48,3200]{1,0:T(8,128)(2,1)S(1)}, u32[]{:S(2)}, u32[]{:S(2)}) collective-permute-start(bf16[48,3200]{1,0:T(8,128)(2,1)} %collective-permute-done.5.refs_7_.refs_16_), channel_id=1, source_target_pairs={{0,16},{16,0},{32,48},{48,32},{64,80},{80,64},{96,112},{112,96},{1... | collective-permute-start | bytes 921608 | tf_op jit(solution)/shard_map/ppermute | solution.py:82
  43.4 2.1 copy-start.22
  44.7 0.8 copy-start.23
  45.5 0.7 copy-start.24
  105.2 1.3 copy-start
  106.5 32.6 %all-to-all-start.1 = ((bf16[16,33,1536]{2,1,0:T(8,128)(2,1)}), bf16[16,33,1536]{2,1,0:T(8,128)(2,1)S(1)}, u32[]{:S(2)}, u32[]{:S(2)}) async-start(bf16[16,33,1536]{2,1,0:T(8,128)(2,1)} %copy-done), calls=%async_computation.1 | async-start | bytes 3932160 | tf_op jit(solution)/shard_map/all_to_all | solution.py:674
  110.8 101.6 %reduce-scatter.2.cloned.1.call-start = ((), (), s32[]{:S(2)}) async-start(), calls=%async_computation.6 | async-start | bytes 10616832 | tf_op jit(solution)/shard_map/reduce_scatter | solution.py:737
  153.3 7.3 %collective-permute-start.14 = (bf16[16,208,384]{2,1,0:T(8,128)(2,1)}, bf16[16,208,384]{2,1,0:T(8,128)(2,1)S(1)}, u32[]{:S(2)}, u32[]{:S(2)}) collective-permute-start(bf16[16,208,384]{2,1,0:T(8,128)(2,1)} %get-tuple-element.83), channel_id=1, source_target_pairs={{0,16},{16,0},{32,48},{48,32},{64,80},{80,64},{96,112},{112,96},{1... | collective-permute-start | bytes 7667720 | tf_op jit(solution)/shard_map/ppermute | solution.py:682
  199.0 11.8 %copy-start.12 = (f32[1,197,768]{2,1,0:T(8,128)S(1)}, f32[1,197,768]{2,1,0:T(8,128)}, u32[]{:S(2)}) copy-start(f32[1,197,768]{2,1,0:T(8,128)} %get-tuple-element.129) | copy-start | bytes 1815556
  199.1 4.2 %collective-permute-start.15 = (bf16[49,384]{1,0:T(8,128)(2,1)S(1)}, bf16[49,384]{1,0:T(8,128)(2,1)S(1)}, u32[]{:S(2)}, u32[]{:S(2)}) collective-permute-start(bf16[49,384]{1,0:T(8,128)(2,1)S(1)} %get-tuple-element.148), channel_id=1, source_target_pairs={{0,32},{16,48},{32,64},{48,80},{64,96},{80,112},{96,0},{112,16},{1... | collective-permute-start | bytes 112904 | tf_op jit(solution)/shard_map/ppermute | solution.py:680
  199.4 3.8 %collective-permute-start.17 = (bf16[49,384]{1,0:T(8,128)(2,1)S(1)}, bf16[49,384]{1,0:T(8,128)(2,1)S(1)}, u32[]{:S(2)}, u32[]{:S(2)}) collective-permute-start(bf16[49,384]{1,0:T(8,128)(2,1)S(1)} %get-tuple-element.149), channel_id=1, source_target_pairs={{0,96},{16,112},{32,0},{48,16},{64,32},{80,48},{96,64},{112,80},{1... | collective-permute-start | bytes 112904 | tf_op jit(solution)/shard_map/ppermute | solution.py:680
  201.9 4.4 %collective-permute-start.16 = (bf16[49,384]{1,0:T(8,128)(2,1)S(1)}, bf16[49,384]{1,0:T(8,128)(2,1)S(1)}, u32[]{:S(2)}, u32[]{:S(2)}) collective-permute-start(bf16[49,384]{1,0:T(8,128)(2,1)S(1)} %get-tuple-element.150), channel_id=1, source_target_pairs={{0,64},{16,80},{32,96},{48,112},{64,0},{80,16},{96,32},{112,48},{1... | collective-permute-start | bytes 112904 | tf_op jit(solution)/shard_map/ppermute | solution.py:680
  207.2 13.6 %all-to-all-start.3 = ((bf16[16,49,384]{2,1,0:T(8,128)(2,1)}), bf16[16,49,384]{2,1,0:T(8,128)(2,1)S(1)}, u32[]{:S(2)}, u32[]{:S(2)}) async-start(bf16[16,49,384]{2,1,0:T(8,128)(2,1)} %broadcast_in_dim.16), calls=%async_computation.3 | async-start | bytes 1376256 | tf_op jit(solution)/shard_map/all_to_all | solution.py:674
  212.2 8.5 %copy-start.1 = (f32[96,16]{0,1:T(8,128)S(1)}, f32[96,16]{0,1:T(8,128)}, u32[]{:S(2)}) copy-start(f32[96,16]{0,1:T(8,128)} %param.32) | copy-start | bytes 18436
  212.2 8.5 %copy-start.2 = (f32[96,16]{0,1:T(8,128)S(1)}, f32[96,16]{0,1:T(8,128)}, u32[]{:S(2)}) copy-start(f32[96,16]{0,1:T(8,128)} %param.33) | copy-start | bytes 18436
  212.3 8.5 %copy-start.3 = (f32[96,16]{0,1:T(8,128)S(1)}, f32[96,16]{0,1:T(8,128)}, u32[]{:S(2)}) copy-start(f32[96,16]{0,1:T(8,128)} %param.34) | copy-start | bytes 18436
  212.3 8.5 %copy-start.4 = (f32[96,4]{0,1:T(4,128)S(1)}, f32[96,4]{0,1:T(4,128)}, u32[]{:S(2)}) copy-start(f32[96,4]{0,1:T(4,128)} %param.35) | copy-start | bytes 4612
  212.3 8.5 %copy-start.5 = (f32[96,4]{0,1:T(4,128)S(1)}, f32[96,4]{0,1:T(4,128)}, u32[]{:S(2)}) copy-start(f32[96,4]{0,1:T(4,128)} %param.36) | copy-start | bytes 4612
  212.3 8.5 %copy-start.6 = (f32[96,4]{0,1:T(4,128)S(1)}, f32[96,4]{0,1:T(4,128)}, u32[]{:S(2)}) copy-start(f32[96,4]{0,1:T(4,128)} %param.37) | copy-start | bytes 4612
Sparse Core Ops, SparseCore 0:
  27.1 59.1 all-gather.1
  122.7 58.0 reduce-scatter.1

commit v4 on v3

--- a/solution.py
+++ b/solution.py
@@ -20,6 +20,7 @@
 PIECE = 48
 WIDE = 384
 HID = 384
+LAST = EXPERTS * 32
 BLOCK = 4 * PIECE + 16
 
 norm_epsilon = 1e-06
@@ -123,8 +124,28 @@
             self.open[name].wait()
 
 
-def slot_rows(e):
-    return slice(e * CAP, (e + 1) * CAP)
+def pack_slots(totals, out_ref):
+    unused = jnp.zeros((4, 128), full)
+    for e in range(EXPERTS):
+        last = []
+        for part, total in enumerate(totals):
+            for j in range(6):
+                cols, at = slice(j * 128, (j + 1) * 128), (part * 6 + j) * 32
+                out_ref[e, at : at + 32, :] = total[e * 32 : (e + 1) * 32, cols].astype(low)
+                last.append(total[LAST + e : LAST + e + 1, cols])
+        out_ref[e, 384:400, :] = jnp.concatenate(last + [unused], axis=0).astype(low)
+
+
+def unpack_slots(got_ref, part, rows_ref):
+    last = []
+    for e in range(EXPERTS):
+        for j in range(6):
+            cols, at = slice(j * 128, (j + 1) * 128), (part * 6 + j) * 32
+            rows_ref[e * 32 : (e + 1) * 32, cols] = got_ref[e, at : at + 32, :]
+        block = got_ref[e, 384:400, :].astype(full)
+        rows = [block[part * 6 + j : part * 6 + j + 1] for j in range(6)]
+        last.append(jnp.concatenate(rows, axis=1))
+    rows_ref[LAST:SLOTS, :] = jnp.concatenate(last, axis=0).astype(low)
 
 
 def padded(ref, pad_ref):
@@ -148,7 +169,7 @@
     outs, refs = refs[:8], refs[8:]
     send_ref = outs[0]
     m_ref, a_ref, qkv_ref, p_ref, o_ref, c_ref, r_ref = refs[:7]
-    x_ref, g_ref, x_pad, g_pad, w_ref, w_sem, sem, spare = refs[7:]
+    x_ref, g_ref, x_pad, g_pad, w_ref, w_sem, sem, spare, spare2 = refs[7:]
     moves = Moves(sem)
     moves.start("x", x_hbm, x_ref)
     copies = dense_copies(rows_ref, pieces, w_ref, w_sem)
@@ -206,12 +227,9 @@
         gate = jnp.sum(jnp.where(chosen, r, 0.0), axis=1, keepdims=True) * keep_ref[:, j : j + 1]
         picks.append((slot == trow_ref[j : j + 1, :]).astype(full).astype(low))
         grads.append((gate * g).astype(low))
-    for part, value in enumerate(
-        (dot(picks[0] + picks[1], c), dot(picks[0], grads[0]) + dot(picks[1], grads[1]))
-    ):
-        spare[...] = value
-        for e in range(EXPERTS):
-            send_ref[e, :, part * D : (part + 1) * D] = spare[slot_rows(e), :].astype(low)
+    spare[...] = dot(picks[0] + picks[1], c)
+    spare2[...] = dot(picks[0], grads[0]) + dot(picks[1], grads[1])
+    pack_slots((spare, spare2), send_ref)
     moves.wait("a", "qkv", "p", "o", "m", "c", "r")
 
 
@@ -222,12 +240,8 @@
 
     @pl.when(step == 0)
     def _():
-        for e in range(EXPERTS):
-            rows = slice(e * CAP, (e + 1) * CAP)
-            z_sum[rows, :] = got_ref[e, :, 0:D].astype(full)
-            dx_sum[rows, :] = got_ref[e, :, D:].astype(full)
-        xs[...] = z_sum[...].astype(low)
-        dzs[...] = dx_sum[...].astype(low)
+        unpack_slots(got_ref, 0, xs)
+        unpack_slots(got_ref, 1, dzs)
         xt_ref[...] = xs[...].T
         dzt_ref[...] = dzs[...].T
         z_sum[...] = jnp.zeros_like(z_sum)
@@ -252,10 +266,7 @@
 
     @pl.when(step == pl.num_programs(0) - 1)
     def _():
-        for e in range(EXPERTS):
-            rows = slice(e * CAP, (e + 1) * CAP)
-            back_ref[e, :, 0:D] = z_sum[rows, :].astype(low)
-            back_ref[e, :, D:] = dx_sum[rows, :].astype(low)
+        pack_slots((z_sum, dx_sum), back_ref)
 
 
 def expert_grad_kernel(h_ref, du_ref, xt_ref, dzt_ref, out_ref):
@@ -311,9 +322,8 @@
         moves.start(name, ins[name - 1], refs[name - 1])
 
     def rows_of(part):
-        for e in range(EXPERTS):
-            spare[slot_rows(e), :] = back_ref[e, :, part * D : (part + 1) * D].astype(full)
-        return spare[...].astype(low)
+        unpack_slots(back_ref, part, spare)
+        return spare[...]
 
     def send_grads(part):
         rows = pl.ds(0, 4 * PIECE)
@@ -539,7 +549,7 @@
 
 def token_forward(*args):
     outs = (
-        pltpu.VMEM((EXPERTS, CAP, 2 * D), low),
+        pltpu.VMEM((EXPERTS, 400, 128), low),
         hbm(ROWS, D),
         hbm(ROWS, D, dtype=low),
         hbm(ROWS, 3 * D, dtype=low),
@@ -561,6 +571,7 @@
             pltpu.SemaphoreType.DMA((16,)),
             pltpu.SemaphoreType.DMA((10,)),
             pltpu.VMEM((SLOTS, D), full),
+            pltpu.VMEM((SLOTS, D), full),
         ],
         compiler_params=params(40),
         cost_estimate=pl.CostEstimate(
@@ -581,7 +592,7 @@
         expert_kernel,
         grid=(GRP // 2,),
         out_shape=(
-            pltpu.VMEM((EXPERTS, CAP, 2 * D), low),
+            pltpu.VMEM((EXPERTS, 400, 128), low),
             hidden,
             hidden,
             turned,
@@ -630,7 +641,7 @@
         + [
             pltpu.VMEM((ROWS, D), full),
             pltpu.VMEM((ROWS, D), full),
-            pltpu.VMEM((SLOTS, D), full),
+            pltpu.VMEM((SLOTS, D), low),
             pltpu.VMEM((ROWS, 3 * D), low),
             pltpu.VMEM((D, DENSE), low),
             pltpu.SemaphoreType.DMA((16,)),
@@ -723,7 +734,8 @@
     flat = ids.reshape(-1)
     marks = (flat[:, None] == jnp.arange(EXPERTS, dtype=jnp.int32)[None, :]).astype(jnp.int32)
     slots = jnp.sum((jnp.cumsum(marks, axis=0) - marks) * marks, axis=1).reshape(TOK, 2)
-    target = jnp.where(kept > 0, ids * CAP + slots, -1)
+    places = jnp.where(slots < CAP - 1, ids * 32 + slots, LAST + ids)
+    target = jnp.where(kept > 0, places, -1)
     padding = ((0, ROWS - TOK), (0, 0))
     target = jnp.pad(target, padding, constant_values=-1)
     ids = jnp.pad(ids, padding, constant_values=-1)

time: 237 us -> 232 us (0.979)
  blocking collectives: 69.9 us -> 66 us
    all_to_all x2, blocking collectives: 69.9 us -> 66 us  [exchange(): return lax.all_to_all(value, 'exp', split_axis=0, concat_axis=0, tiled=True)]
    all_to_all x2, waiting for transfers between devices: 16.9 us -> 14.1 us  [exchange(): return lax.all_to_all(value, 'exp', split_axis=0, concat_axis=0, tiled=True)]
    all_to_all x2, starting transfers between devices: 7.86 us -> 10.3 us  [exchange(): return lax.all_to_all(value, 'exp', split_axis=0, concat_axis=0, tiled=True)]
    unnamed x54 -> x50, local copies, waits for them, and re-layouts: 4.86 us -> 2.84 us
  transfers between devices with their start and end apart: 22 -> 22, of which waited for: 11 -> 12; matrix products, arithmetic and copies ran while one was open for 4% -> 4% of each run, Pallas kernels for 18% -> 18%
where the time goes in v4:
time: 232 us; the launch traced here: 229 us
  blocking collectives  66 us (28%)
  Pallas kernels  65.8 us (28%)
  waiting for transfers between devices  43.3 us (19%)
  starting transfers between devices  29 us (12%)
  between operations  14.5 us (6%)
  other arithmetic  5.53 us (2%)
  local copies, waits for them, and re-layouts  4.51 us (2%)
    all_to_all x2, blocking collectives, exchange(): return lax.all_to_all(value, 'exp', split_axis=0, concat_axis=0, tiled=True)  66 us
    ppermute x9, waiting for transfers between devices, along(): return lax.ppermute(value, 'grp', hops)  19.8 us
    pallas_call x1, Pallas kernels, experts_both_ways(): pl.pallas_call(expert_kernel, grid=(GRP // 2,), out_shape=(pltpu.VMEM((EX...  16.7 us
    pallas_call x1, Pallas kernels, token_backward(): pl.pallas_call(backward_kernel, out_shape=outs, in_specs=[in_smem()] + in...  14.2 us
    all_to_all x2, waiting for transfers between devices, exchange(): return lax.all_to_all(value, 'exp', split_axis=0, concat_axis=0, tiled=True)  14.1 us
    pallas_call x1, Pallas kernels, expert_grads(): pl.pallas_call(expert_grad_kernel, grid=(GRP // 2,), out_shape=hbm(GRP *...  11.8 us
    ppermute x9, starting transfers between devices, along(): return lax.ppermute(value, 'grp', hops)  11.6 us
    all_to_all x2, starting transfers between devices, exchange(): return lax.all_to_all(value, 'exp', split_axis=0, concat_axis=0, tiled=True)  10.3 us
  transfers between devices with their start and end apart: 22, of which 12 were waited for; matrix products, arithmetic and copies ran while one was open for 4% of the time, Pallas kernels for 18%

profile of v4, /device:TPU:1, one launch (start us, length us, event | category | flops | bytes accessed | tf_op | source)
XLA Modules:
  0.0 228.7 jit_solution(17138543533865218324)
XLA Ops:
  7.2 0.0 copy-start.8
  7.2 0.0 all-gather.2.cloned.1.call-start
  7.3 1.5 pack.1
  8.8 0.0 copy-start.7
  8.8 2.1 collective-permute-start
  10.9 1.3 collective-permute-start.1
  12.2 1.1 copy.55
  13.3 5.4 %collective-permute-done.refs_2_.refs_11_ = bf16[48,3200]{1,0:T(8,128)(2,1)S(1)} collective-permute-done((bf16[48,3200]{1,0:T(8,128)(2,1)S(1)}, bf16[48,3200]{1,0:T(8,128)(2,1)S(1)}, u32[]{:S(2)}, u32[]{:S(2)}) %collective-permute-start) | collective-permute-done | bytes 307232 | tf_op jit(solution)/shard_map/ppermute | solution.py:80
  18.7 0.1 collective-permute-done.1.refs_5_.refs_14_
  18.8 1.2 collective-permute-start.2
  20.0 1.5 collective-permute-start.3
  21.5 0.1 convert_bitcast_fusion.1
  21.6 1.1 pad_maximum_fusion
  22.7 4.2 %collective-permute-done.2.refs_3_.refs_12_ = bf16[48,3200]{1,0:T(8,128)(2,1)S(1)} collective-permute-done((bf16[48,3200]{1,0:T(8,128)(2,1)S(1)}, bf16[48,3200]{1,0:T(8,128)(2,1)S(1)}, u32[]{:S(2)}, u32[]{:S(2)}) %collective-permute-start.2) | collective-permute-done | bytes 307232 | tf_op jit(solution)/shard_map/ppermute | solution.py:80
  26.9 0.0 all-gather.2.cloned.1.call-update
  27.0 2.9 %collective-permute-start.6 = (bf16[48,3200]{1,0:T(8,128)(2,1)S(1)}, bf16[48,3200]{1,0:T(8,128)(2,1)S(1)}, u32[]{:S(2)}, u32[]{:S(2)}) collective-permute-start(bf16[48,3200]{1,0:T(8,128)(2,1)S(1)} %get-tuple-element.68.refs_0_.refs_9_), channel_id=1, source_target_pairs={{0,16},{16,0},{32,48},{48,32},{64,80},{80,64},{96,112},{112,96},{1... | collective-permute-start | bytes 921608 | tf_op jit(solution)/shard_map/ppermute | solution.py:83
  29.8 0.1 collective-permute-start.7
  29.9 0.1 copy.48
  30.1 0.1 eq.32
  30.2 1.2 reduce-window.6
  31.4 0.2 slice_reduce_fusion
  31.6 0.1 bitcast_bitcast_fusion
  31.7 0.4 collective-permute-start.8
  32.2 0.9 collective-permute-start.4
  33.1 1.8 collective-permute-start.5
  34.9 0.1 reshape.77
  35.0 0.1 copy.49
  35.3 0.7 collective-permute-start.11
  36.0 0.1 collective-permute-start.9
  36.1 0.4 collective-permute-start.10
  36.5 5.7 %collective-permute-done.4.refs_6_.refs_15_ = bf16[48,3200]{1,0:T(8,128)(2,1)S(1)} collective-permute-done((bf16[48,3200]{1,0:T(8,128)(2,1)S(1)}, bf16[48,3200]{1,0:T(8,128)(2,1)S(1)}, u32[]{:S(2)}, u32[]{:S(2)}) %collective-permute-start.4) | collective-permute-done | bytes 307232 | tf_op jit(solution)/shard_map/ppermute | solution.py:80
  42.2 0.9 collective-permute-start.12
  43.1 0.1 collective-permute-start.13
  43.2 0.1 copy.54.trow_ref
  43.3 0.1 stack.75.rows_ref
  43.5 1.2 collective-permute-done.12.refs_14_.refs_23_
  44.7 0.9 collective-permute-done.13.refs_15_.refs_24_
  45.6 8.0 %token_forward.1 = (bf16[16,400,128]{2,1,0:T(8,128)(2,1)S(1)}, f32[208,768]{1,0:T(8,128)}, bf16[208,768]{1,0:T(8,128)(2,1)}, bf16[208,2304]{1,0:T(8,128)(2,1)}, ...) custom-call(s32[18]{0:T(128)S(1)} %stack.75.rows_ref, ...), custom_call_target="tpu_custom_call" | custom-call | flops 4000000000 | bytes 12000000 | tf_op jit(solution)/shard_map/token_forward/pallas_call | solution.py:561
  53.7 30.4 %all_to_all.20.got_ref = bf16[16,400,128]{2,1,0:T(8,128)(2,1)S(1)} all-to-all(bf16[16,400,128]{2,1,0:T(8,128)(2,1)S(1)} %get-tuple-element.70), channel_id=1, replica_groups=mesh['grp'=8,'exp'=16] {'exp'}, dimensions={0} | all-to-all | bytes 3276800 | tf_op jit(solution)/shard_map/all_to_all | solution.py:685
  84.1 2.1 all-gather.2.cloned.1.call-done.w_ref
  86.3 16.7 %experts.1 = (bf16[16,400,128]{2,1,0:T(8,128)(2,1)}, bf16[528,3072]{1,0:T(8,128)(2,1)}, bf16[528,3072]{1,0:T(8,128)(2,1)}, bf16[768,528]{1,0:T(8,128)(2,1)}, bf16[768,528]{1,0:T(8,128)(2,1)}) custom-call(bf16[16,400,128]{2,1,0:T(8,128)(2,1)S(1)} %all_to_all.20.got_ref, bf16[6144,768]{1,0:T(8,128)(2,1)} %all-gather.2.cloned.1.call-done.w_ref), custom_call_target="tpu_custom_call" | custom-call | flops 10000000000 | bytes 23000000 | tf_op jit(solution)/shard_map/experts/pallas_call | solution.py:591
  103.0 6.7 %all-to-all-start.1 = ((bf16[16,400,128]{2,1,0:T(8,128)(2,1)}), bf16[16,400,128]{2,1,0:T(8,128)(2,1)S(1)}, u32[]{:S(2)}, u32[]{:S(2)}) async-start(bf16[16,400,128]{2,1,0:T(8,128)(2,1)} %get-tuple-element.72), calls=%async_computation.1 | async-start | bytes 3276800 | tf_op jit(solution)/shard_map/all_to_all | solution.py:685
  109.7 0.0 reduce-scatter.2.cloned.1.call-start
  109.7 11.8 %expert_grads.1 = bf16[6144,768]{1,0:T(8,128)(2,1)} custom-call(bf16[528,3072]{1,0:T(8,128)(2,1)} %get-tuple-element.84.h_ref, bf16[528,3072]{1,0:T(8,128)(2,1)} %get-tuple-element.85.du_ref, bf16[768,528]{1,0:T(8,128)(2,1)} %get-tuple-element.86.xt_ref, bf16[768,528]{1,0:T(8,128)(2,1)} %get-tuple-element.87.dzt_ref), custom_call_target="tpu_custom_call" | custom-call | flops 6000000000 | bytes 18000000 | tf_op jit(solution)/shard_map/expert_grads/pallas_call | solution.py:613
  121.5 0.0 reduce-scatter.2.cloned.1.call-update
  121.5 13.6 %all-to-all-done.1.back_ref = bf16[16,400,128]{2,1,0:T(8,128)(2,1)S(1)} async-done(((bf16[16,400,128]{2,1,0:T(8,128)(2,1)}), bf16[16,400,128]{2,1,0:T(8,128)(2,1)S(1)}, u32[]{:S(2)}, u32[]{:S(2)}) %all-to-all-start.1) | async-done | bytes 1638432 | tf_op jit(solution)/shard_map/all_to_all | solution.py:685
  135.2 14.2 %token_backward.1 = (bf16[1,197,768]{2,1,0:T(8,128)(2,1)}, f32[1,197,768]{2,1,0:T(8,128)}, bf16[16,208,384]{2,1,0:T(8,128)(2,1)}, bf16[16,208,384]{2,1,0:T(8,128)(2,1)}) custom-call(s32[18]{0:T(128)S(1)} %stack.75.rows_ref, s32[208,2]{1,0:T(8,128)S(1)} %pad.15.ids_ref, s32[208,2]{1,0:T(8,128)S(1)} %get-tuple-element.152.tcol_ref, ...), custom_call_target="tpu_custom_call" | custom-call | flops 399999991808 | bytes 18000000 | tf_op jit(solution)/shard_map/token_backward/pallas_call | solution.py:634
  149.4 1.4 collective-permute-start.14
  150.9 5.1 %collective-permute-done.14 = bf16[16,208,384]{2,1,0:T(8,128)(2,1)S(1)} collective-permute-done((bf16[16,208,384]{2,1,0:T(8,128)(2,1)}, bf16[16,208,384]{2,1,0:T(8,128)(2,1)S(1)}, u32[]{:S(2)}, u32[]{:S(2)}) %collective-permute-start.14) | collective-permute-done | bytes 2555936 | tf_op jit(solution)/shard_map/ppermute | solution.py:693
  155.9 2.6 %add_convert_fusion = bf16[16,208,384]{2,1,0:T(8,128)(2,1)S(1)} fusion(bf16[16,208,384]{2,1,0:T(8,128)(2,1)S(1)} %collective-permute-done.14, bf16[16,208,384]{2,1,0:T(8,128)(2,1)} %get-tuple-element.82), kind=kLoop, calls=%fused_computation.1 | loop fusion | flops 5111808 | bytes 7667712 | tf_op jit(solution)/shard_map/convert_element_type | solution.py:694
  158.5 35.6 %all_to_all.21 = bf16[16,208,384]{2,1,0:T(8,128)(2,1)S(1)} all-to-all(bf16[16,208,384]{2,1,0:T(8,128)(2,1)S(1)} %add_convert_fusion), channel_id=1, replica_groups=mesh['grp'=8,'exp'=16] {'exp'}, dimensions={0} | all-to-all | bytes 5111808 | tf_op jit(solution)/shard_map/all_to_all | solution.py:685
  194.1 0.4 convert_reduce_fusion
  194.6 0.1 collective-permute-start.15
  194.7 2.7 %collective-permute-start.17 = (bf16[49,384]{1,0:T(8,128)(2,1)S(1)}, bf16[49,384]{1,0:T(8,128)(2,1)S(1)}, u32[]{:S(2)}, u32[]{:S(2)}) collective-permute-start(bf16[49,384]{1,0:T(8,128)(2,1)S(1)} %get-tuple-element.149), channel_id=1, source_target_pairs={{0,96},{16,112},{32,0},{48,16},{64,32},{80,48},{96,64},{112,80},{1... | collective-permute-start | bytes 112904 | tf_op jit(solution)/shard_map/ppermute | solution.py:691
  197.4 0.1 collective-permute-start.16
  197.4 1.4 collective-permute-done.15
  198.8 3.0 %collective-permute-done.16 = bf16[49,384]{1,0:T(8,128)(2,1)S(1)} collective-permute-done((bf16[49,384]{1,0:T(8,128)(2,1)S(1)}, bf16[49,384]{1,0:T(8,128)(2,1)S(1)}, u32[]{:S(2)}, u32[]{:S(2)}) %collective-permute-start.16) | collective-permute-done | bytes 37664 | tf_op jit(solution)/shard_map/ppermute | solution.py:691
  201.8 0.9 broadcast_in_dim.16
  202.7 3.6 %all-to-all-start.3 = ((bf16[16,49,384]{2,1,0:T(8,128)(2,1)}), bf16[16,49,384]{2,1,0:T(8,128)(2,1)S(1)}, u32[]{:S(2)}, u32[]{:S(2)}) async-start(bf16[16,49,384]{2,1,0:T(8,128)(2,1)} %broadcast_in_dim.16), calls=%async_computation.3 | async-start | bytes 1376256 | tf_op jit(solution)/shard_map/all_to_all | solution.py:685
  206.3 1.4 copy.56
  207.8 0.0 reduce-scatter.2.cloned.1.call-done.grad_ref
  207.8 8.0 %expert_step.1 = (f32[1,768,384]{2,1,0:T(8,128)}, f32[1,768,384]{2,1,0:T(8,128)}, f32[1,768,384]{2,1,0:T(8,128)}, f32[1,384,768]{2,1,0:T(8,128)}, f32[1,384,768]{2,1,0:T(8,128)}, /*index=5*/f32[1,384,768]{2,1,0:T(8,128)}) custom-call(bf16[768,768]{1,0:T(8,128)(2,1)} %reduce-scatter.2.cloned.1.call-done.grad_ref, f32[1,768,384]{2,1,0:T(8,128)} %refs_0_.2, ...), custom_call_target="tpu_custom_call" | custom-call | flops 10000000 | bytes 8000000 | tf_op jit(solution)/shard_map/expert_step/pallas_call | solution.py:485
  215.9 0.5 all-to-all-done.3
  216.3 5.5 %owner_step.1 = (f32[96,2304]{1,0:T(8,128)}, f32[96,2304]{1,0:T(8,128)}, f32[96,2304]{1,0:T(8,128)}, f32[96,768]{1,0:T(8,128)}, f32[96,768]{1,0:T(8,128)}, /*ind...) custom-call(bf16[2,8,49,384]{3,2,1,0:T(8,128)(2,1)S(1)} %bitcast.75,, ...), custom_call_target="tpu_custom_call" | custom-call | flops 10000000 | bytes 8000000 | tf_op jit(solution)/shard_map/owner_step/pallas_call | solution.py:664
  (69 shorter events, 0.4 us)
Async XLA Ops:
  7.2 5.0 %copy-start.8 = (f32[1,384,768]{2,1,0:T(8,128)S(1)}, f32[1,384,768]{2,1,0:T(8,128)}, u32[]{:S(2)}) copy-start(f32[1,384,768]{2,1,0:T(8,128)} %refs_3_.2) | copy-start | bytes 3538948
  7.2 14.3 %copy-start.9 = (f32[1,768,384]{2,1,0:T(8,128)S(1)}, f32[1,768,384]{2,1,0:T(8,128)}, u32[]{:S(2)}) copy-start(f32[1,768,384]{2,1,0:T(8,128)} %refs_0_.2) | copy-start | bytes 3538948
  7.2 79.0 %all-gather.2.cloned.1.call-start = ((), (), s32[]{:S(2)}) async-start(), calls=%async_computation.5 | async-start | bytes 10616832 | tf_op jit(solution)/shard_map/all_gather | solution.py:730
  8.7 18.2 %copy-start.6 = (bf16[48,3200]{1,0:T(8,128)(2,1)}, bf16[48,3200]{1,0:T(8,128)(2,1)S(1)}, u32[]{:S(2)}) copy-start(bf16[48,3200]{1,0:T(8,128)(2,1)S(1)} %get-tuple-element.68.refs_0_.refs_9_) | copy-start | bytes 921604
  8.8 21.1 %copy-start.7 = (bf16[48,3200]{1,0:T(8,128)(2,1)}, bf16[48,3200]{1,0:T(8,128)(2,1)S(1)}, u32[]{:S(2)}) copy-start(bf16[48,3200]{1,0:T(8,128)(2,1)S(1)} %get-tuple-element.67.refs_1_.refs_10_) | copy-start | bytes 921604
  8.8 9.9 %collective-permute-start = (bf16[48,3200]{1,0:T(8,128)(2,1)S(1)}, bf16[48,3200]{1,0:T(8,128)(2,1)S(1)}, u32[]{:S(2)}, u32[]{:S(2)}) collective-permute-start(bf16[48,3200]{1,0:T(8,128)(2,1)S(1)} %get-tuple-element.68.refs_0_.refs_9_), channel_id=1, source_target_pairs={{0,32},{16,48},{32,64},{48,80},{64,96},{80,112},{96,0},{112,16},{1... | collective-permute-start | bytes 921608 | tf_op jit(solution)/shard_map/ppermute | solution.py:80
  10.9 7.9 %collective-permute-start.1 = (bf16[48,3200]{1,0:T(8,128)(2,1)S(1)}, bf16[48,3200]{1,0:T(8,128)(2,1)}, u32[]{:S(2)}, u32[]{:S(2)}) collective-permute-start(bf16[48,3200]{1,0:T(8,128)(2,1)S(1)} %get-tuple-element.67.refs_1_.refs_10_), channel_id=1, source_target_pairs={{0,96},{16,112},{32,0},{48,16},{64,32},{80,48},{96,64},{112,80},{1... | collective-permute-start | bytes 921608 | tf_op jit(solution)/shard_map/ppermute | solution.py:80
  13.3 8.3 %copy-start.10 = (bf16[1,384,768]{1,2,0:T(8,128)(2,1)S(1)}, bf16[1,384,768]{1,2,0:T(8,128)(2,1)}, u32[]{:S(2)}) copy-start(bf16[1,384,768]{1,2,0:T(8,128)(2,1)} %copy.55) | copy-start | bytes 1769476
  18.7 13.5 %copy-start.14 = (bf16[48,3200]{1,0:T(8,128)(2,1)}, bf16[48,3200]{1,0:T(8,128)(2,1)S(1)}, u32[]{:S(2)}) copy-start(bf16[48,3200]{1,0:T(8,128)(2,1)S(1)} %collective-permute-done.refs_2_.refs_11_) | copy-start | bytes 921604
  18.8 8.1 %collective-permute-start.2 = (bf16[48,3200]{1,0:T(8,128)(2,1)S(1)}, bf16[48,3200]{1,0:T(8,128)(2,1)S(1)}, u32[]{:S(2)}, u32[]{:S(2)}) collective-permute-start(bf16[48,3200]{1,0:T(8,128)(2,1)S(1)} %get-tuple-element.67.refs_1_.refs_10_), channel_id=1, source_target_pairs={{0,32},{16,48},{32,64},{48,80},{64,96},{80,112},{96,0},{112,16},{1... | collective-permute-start | bytes 921608 | tf_op jit(solution)/shard_map/ppermute | solution.py:80
  20.0 6.9 %collective-permute-start.3 = (bf16[48,3200]{1,0:T(8,128)(2,1)S(1)}, bf16[48,3200]{1,0:T(8,128)(2,1)S(1)}, u32[]{:S(2)}, u32[]{:S(2)}) collective-permute-start(bf16[48,3200]{1,0:T(8,128)(2,1)S(1)} %get-tuple-element.68.refs_0_.refs_9_), channel_id=1, source_target_pairs={{0,96},{16,112},{32,0},{48,16},{64,32},{80,48},{96,64},{112,80},{1... | collective-permute-start | bytes 921608 | tf_op jit(solution)/shard_map/ppermute | solution.py:80
  21.6 8.4 %copy-start.12 = (s32[1,197,2]{1,2,0:T(2,128)S(1)}, s32[1,197,2]{1,2,0:T(2,128)}, u32[]{:S(2)}) copy-start(s32[1,197,2]{1,2,0:T(2,128)} %param.24) | copy-start | bytes 4732
  21.6 13.5 %copy-start.13 = (s32[1,197,2]{1,2,0:T(2,128)S(1)}, s32[1,197,2]{1,2,0:T(2,128)}, u32[]{:S(2)}) copy-start(s32[1,197,2]{1,2,0:T(2,128)} %param.25) | copy-start | bytes 4732
  26.9 16.4 %copy-start.15 = (bf16[48,3200]{1,0:T(8,128)(2,1)}, bf16[48,3200]{1,0:T(8,128)(2,1)S(1)}, u32[]{:S(2)}) copy-start(bf16[48,3200]{1,0:T(8,128)(2,1)S(1)} %collective-permute-done.2.refs_3_.refs_12_) | copy-start | bytes 921604
  26.9 16.4 %copy-start.16 = (bf16[48,3200]{1,0:T(8,128)(2,1)}, bf16[48,3200]{1,0:T(8,128)(2,1)S(1)}, u32[]{:S(2)}) copy-start(bf16[48,3200]{1,0:T(8,128)(2,1)S(1)} %collective-permute-done.3.refs_4_.refs_13_) | copy-start | bytes 921604
  27.0 8.3 %collective-permute-start.6 = (bf16[48,3200]{1,0:T(8,128)(2,1)S(1)}, bf16[48,3200]{1,0:T(8,128)(2,1)S(1)}, u32[]{:S(2)}, u32[]{:S(2)}) collective-permute-start(bf16[48,3200]{1,0:T(8,128)(2,1)S(1)} %get-tuple-element.68.refs_0_.refs_9_), channel_id=1, source_target_pairs={{0,16},{16,0},{32,48},{48,32},{64,80},{80,64},{96,112},{112,96},{1... | collective-permute-start | bytes 921608 | tf_op jit(solution)/shard_map/ppermute | solution.py:83
  29.8 6.1 %collective-permute-start.7 = (bf16[48,3200]{1,0:T(8,128)(2,1)S(1)}, bf16[48,3200]{1,0:T(8,128)(2,1)S(1)}, u32[]{:S(2)}, u32[]{:S(2)}) collective-permute-start(bf16[48,3200]{1,0:T(8,128)(2,1)S(1)} %get-tuple-element.67.refs_1_.refs_10_), channel_id=1, source_target_pairs={{0,16},{16,0},{32,48},{48,32},{64,80},{80,64},{96,112},{112,96},{1... | collective-permute-start | bytes 921608 | tf_op jit(solution)/shard_map/ppermute | solution.py:83
  31.7 4.4 %collective-permute-start.8 = (bf16[48,3200]{1,0:T(8,128)(2,1)S(1)}, bf16[48,3200]{1,0:T(8,128)(2,1)S(1)}, u32[]{:S(2)}, u32[]{:S(2)}) collective-permute-start(bf16[48,3200]{1,0:T(8,128)(2,1)S(1)} %collective-permute-done.refs_2_.refs_11_), channel_id=1, source_target_pairs={{0,16},{16,0},{32,48},{48,32},{64,80},{80,64},{96,112},{112,96},{1... | collective-permute-start | bytes 921608 | tf_op jit(solution)/shard_map/ppermute | solution.py:83
  32.2 10.0 %collective-permute-start.4 = (bf16[48,3200]{1,0:T(8,128)(2,1)S(1)}, bf16[48,3200]{1,0:T(8,128)(2,1)S(1)}, u32[]{:S(2)}, u32[]{:S(2)}) collective-permute-start(bf16[48,3200]{1,0:T(8,128)(2,1)S(1)} %collective-permute-done.refs_2_.refs_11_), channel_id=1, source_target_pairs={{0,32},{16,48},{32,64},{48,80},{64,96},{80,112},{96,0},{112,16},{1... | collective-permute-start | bytes 921608 | tf_op jit(solution)/shard_map/ppermute | solution.py:80
  33.1 10.0 %collective-permute-start.5 = (bf16[48,3200]{1,0:T(8,128)(2,1)}, bf16[48,3200]{1,0:T(8,128)(2,1)}, u32[]{:S(2)}, u32[]{:S(2)}) collective-permute-start(bf16[48,3200]{1,0:T(8,128)(2,1)} %collective-permute-done.1.refs_5_.refs_14_), channel_id=1, source_target_pairs={{0,96},{16,112},{32,0},{48,16},{64,32},{80,48},{96,64},{112,80},{1... | collective-permute-start | bytes 921608 | tf_op jit(solution)/shard_map/ppermute | solution.py:80
  35.2 10.4 %copy-start.17 = (bf16[48,3200]{1,0:T(8,128)(2,1)}, bf16[48,3200]{1,0:T(8,128)(2,1)S(1)}, u32[]{:S(2)}) copy-start(bf16[48,3200]{1,0:T(8,128)(2,1)S(1)} %collective-permute-done.6.refs_8_.refs_17_) | copy-start | bytes 921604
  35.3 8.2 %collective-permute-start.11 = (bf16[48,3200]{1,0:T(8,128)(2,1)}, bf16[48,3200]{1,0:T(8,128)(2,1)S(1)}, u32[]{:S(2)}, u32[]{:S(2)}) collective-permute-start(bf16[48,3200]{1,0:T(8,128)(2,1)} %collective-permute-done.1.refs_5_.refs_14_), channel_id=1, source_target_pairs={{0,16},{16,0},{32,48},{48,32},{64,80},{80,64},{96,112},{112,96},{1... | collective-permute-start | bytes 921608 | tf_op jit(solution)/shard_map/ppermute | solution.py:83
  36.0 9.6 %copy-start.18 = (bf16[48,3200]{1,0:T(8,128)(2,1)}, bf16[48,3200]{1,0:T(8,128)(2,1)S(1)}, u32[]{:S(2)}) copy-start(bf16[48,3200]{1,0:T(8,128)(2,1)S(1)} %collective-permute-done.7.refs_9_.refs_18_) | copy-start | bytes 921604
  36.0 7.5 %collective-permute-start.9 = (bf16[48,3200]{1,0:T(8,128)(2,1)S(1)}, bf16[48,3200]{1,0:T(8,128)(2,1)}, u32[]{:S(2)}, u32[]{:S(2)}) collective-permute-start(bf16[48,3200]{1,0:T(8,128)(2,1)S(1)} %collective-permute-done.2.refs_3_.refs_12_), channel_id=1, source_target_pairs={{0,16},{16,0},{32,48},{48,32},{64,80},{80,64},{96,112},{112,96},{1... | collective-permute-start | bytes 921608 | tf_op jit(solution)/shard_map/ppermute | solution.py:83
  36.1 9.5 %copy-start.19 = (bf16[48,3200]{1,0:T(8,128)(2,1)}, bf16[48,3200]{1,0:T(8,128)(2,1)S(1)}, u32[]{:S(2)}) copy-start(bf16[48,3200]{1,0:T(8,128)(2,1)S(1)} %collective-permute-done.8.refs_10_.refs_19_) | copy-start | bytes 921604
  36.1 7.4 %collective-permute-start.10 = (bf16[48,3200]{1,0:T(8,128)(2,1)S(1)}, bf16[48,3200]{1,0:T(8,128)(2,1)}, u32[]{:S(2)}, u32[]{:S(2)}) collective-permute-start(bf16[48,3200]{1,0:T(8,128)(2,1)S(1)} %collective-permute-done.3.refs_4_.refs_13_), channel_id=1, source_target_pairs={{0,16},{16,0},{32,48},{48,32},{64,80},{80,64},{96,112},{112,96},{1... | collective-permute-start | bytes 921608 | tf_op jit(solution)/shard_map/ppermute | solution.py:83
  42.2 3.4 %copy-start.20 = (bf16[48,3200]{1,0:T(8,128)(2,1)}, bf16[48,3200]{1,0:T(8,128)(2,1)S(1)}, u32[]{:S(2)}) copy-start(bf16[48,3200]{1,0:T(8,128)(2,1)S(1)} %collective-permute-done.4.refs_6_.refs_15_) | copy-start | bytes 921604
  42.2 2.5 %collective-permute-start.12 = (bf16[48,3200]{1,0:T(8,128)(2,1)S(1)}, bf16[48,3200]{1,0:T(8,128)(2,1)S(1)}, u32[]{:S(2)}, u32[]{:S(2)}) collective-permute-start(bf16[48,3200]{1,0:T(8,128)(2,1)S(1)} %collective-permute-done.4.refs_6_.refs_15_), channel_id=1, source_target_pairs={{0,16},{16,0},{32,48},{48,32},{64,80},{80,64},{96,112},{112,96},{1... | collective-permute-start | bytes 921608 | tf_op jit(solution)/shard_map/ppermute | solution.py:83
  43.1 2.5 %collective-permute-start.13 = (bf16[48,3200]{1,0:T(8,128)(2,1)}, bf16[48,3200]{1,0:T(8,128)(2,1)}, u32[]{:S(2)}, u32[]{:S(2)}) collective-permute-start(bf16[48,3200]{1,0:T(8,128)(2,1)} %collective-permute-done.5.refs_7_.refs_16_), channel_id=1, source_target_pairs={{0,16},{16,0},{32,48},{48,32},{64,80},{80,64},{96,112},{112,96},{1... | collective-permute-start | bytes 921608 | tf_op jit(solution)/shard_map/ppermute | solution.py:83
  43.4 2.2 copy-start.21
  44.7 1.0 copy-start.22
  103.0 32.2 %all-to-all-start.1 = ((bf16[16,400,128]{2,1,0:T(8,128)(2,1)}), bf16[16,400,128]{2,1,0:T(8,128)(2,1)S(1)}, u32[]{:S(2)}, u32[]{:S(2)}) async-start(bf16[16,400,128]{2,1,0:T(8,128)(2,1)} %get-tuple-element.72), calls=%async_computation.1 | async-start | bytes 3276800 | tf_op jit(solution)/shard_map/all_to_all | solution.py:685
  109.7 98.1 %reduce-scatter.2.cloned.1.call-start = ((), (), s32[]{:S(2)}) async-start(), calls=%async_computation.6 | async-start | bytes 10616832 | tf_op jit(solution)/shard_map/reduce_scatter | solution.py:749
  149.4 6.5 %collective-permute-start.14 = (bf16[16,208,384]{2,1,0:T(8,128)(2,1)}, bf16[16,208,384]{2,1,0:T(8,128)(2,1)S(1)}, u32[]{:S(2)}, u32[]{:S(2)}) collective-permute-start(bf16[16,208,384]{2,1,0:T(8,128)(2,1)} %get-tuple-element.83), channel_id=1, source_target_pairs={{0,16},{16,0},{32,48},{48,32},{64,80},{80,64},{96,112},{112,96},{1... | collective-permute-start | bytes 7667720 | tf_op jit(solution)/shard_map/ppermute | solution.py:693
  194.5 11.7 %copy-start.11 = (f32[1,197,768]{2,1,0:T(8,128)S(1)}, f32[1,197,768]{2,1,0:T(8,128)}, u32[]{:S(2)}) copy-start(f32[1,197,768]{2,1,0:T(8,128)} %get-tuple-element.129) | copy-start | bytes 1815556
  194.6 4.2 %collective-permute-start.15 = (bf16[49,384]{1,0:T(8,128)(2,1)S(1)}, bf16[49,384]{1,0:T(8,128)(2,1)S(1)}, u32[]{:S(2)}, u32[]{:S(2)}) collective-permute-start(bf16[49,384]{1,0:T(8,128)(2,1)S(1)} %get-tuple-element.148), channel_id=1, source_target_pairs={{0,32},{16,48},{32,64},{48,80},{64,96},{80,112},{96,0},{112,16},{1... | collective-permute-start | bytes 112904 | tf_op jit(solution)/shard_map/ppermute | solution.py:691
  194.7 4.1 %collective-permute-start.17 = (bf16[49,384]{1,0:T(8,128)(2,1)S(1)}, bf16[49,384]{1,0:T(8,128)(2,1)S(1)}, u32[]{:S(2)}, u32[]{:S(2)}) collective-permute-start(bf16[49,384]{1,0:T(8,128)(2,1)S(1)} %get-tuple-element.149), channel_id=1, source_target_pairs={{0,96},{16,112},{32,0},{48,16},{64,32},{80,48},{96,64},{112,80},{1... | collective-permute-start | bytes 112904 | tf_op jit(solution)/shard_map/ppermute | solution.py:691
  197.4 4.4 %collective-permute-start.16 = (bf16[49,384]{1,0:T(8,128)(2,1)S(1)}, bf16[49,384]{1,0:T(8,128)(2,1)S(1)}, u32[]{:S(2)}, u32[]{:S(2)}) collective-permute-start(bf16[49,384]{1,0:T(8,128)(2,1)S(1)} %get-tuple-element.150), channel_id=1, source_target_pairs={{0,64},{16,80},{32,96},{48,112},{64,0},{80,16},{96,32},{112,48},{1... | collective-permute-start | bytes 112904 | tf_op jit(solution)/shard_map/ppermute | solution.py:691
  202.7 13.6 %all-to-all-start.3 = ((bf16[16,49,384]{2,1,0:T(8,128)(2,1)}), bf16[16,49,384]{2,1,0:T(8,128)(2,1)S(1)}, u32[]{:S(2)}, u32[]{:S(2)}) async-start(bf16[16,49,384]{2,1,0:T(8,128)(2,1)} %broadcast_in_dim.16), calls=%async_computation.3 | async-start | bytes 1376256 | tf_op jit(solution)/shard_map/all_to_all | solution.py:685
  207.7 8.6 %copy-start = (f32[96,16]{0,1:T(8,128)S(1)}, f32[96,16]{0,1:T(8,128)}, u32[]{:S(2)}) copy-start(f32[96,16]{0,1:T(8,128)} %param.32) | copy-start | bytes 18436
  207.7 8.6 %copy-start.1 = (f32[96,16]{0,1:T(8,128)S(1)}, f32[96,16]{0,1:T(8,128)}, u32[]{:S(2)}) copy-start(f32[96,16]{0,1:T(8,128)} %param.33) | copy-start | bytes 18436
  207.7 8.6 %copy-start.2 = (f32[96,16]{0,1:T(8,128)S(1)}, f32[96,16]{0,1:T(8,128)}, u32[]{:S(2)}) copy-start(f32[96,16]{0,1:T(8,128)} %param.34) | copy-start | bytes 18436
  207.8 8.6 %copy-start.3 = (f32[96,4]{0,1:T(4,128)S(1)}, f32[96,4]{0,1:T(4,128)}, u32[]{:S(2)}) copy-start(f32[96,4]{0,1:T(4,128)} %param.35) | copy-start | bytes 4612
  207.8 8.6 %copy-start.4 = (f32[96,4]{0,1:T(4,128)S(1)}, f32[96,4]{0,1:T(4,128)}, u32[]{:S(2)}) copy-start(f32[96,4]{0,1:T(4,128)} %param.36) | copy-start | bytes 4612
  207.8 8.6 %copy-start.5 = (f32[96,4]{0,1:T(4,128)S(1)}, f32[96,4]{0,1:T(4,128)}, u32[]{:S(2)}) copy-start(f32[96,4]{0,1:T(4,128)} %param.37) | copy-start | bytes 4612
Sparse Core Ops, SparseCore 0:
  27.1 59.1 all-gather.1
  121.7 57.1 reduce-scatter.1

commit v5 on v4

--- a/solution.py
+++ b/solution.py
@@ -434,40 +434,51 @@
 def adamw(master, first, second, gradient, rate):
     first = beta_first * first + (1.0 - beta_first) * gradient
     second = beta_second * second + (1.0 - beta_second) * gradient * gradient
-    corrected = first / (1.0 - beta_first**STEP)
-    scaled = jnp.sqrt(second / (1.0 - beta_second**STEP)) + adam_epsilon
+    corrected = first * (1.0 / (1.0 - beta_first**STEP))
+    scaled = jnp.sqrt(second * (1.0 / (1.0 - beta_second**STEP))) + adam_epsilon
     return (first, second, master - rate * (corrected / scaled + weight_decay * master))
 
 
-def owner_kernel(pieces_ref, rest_ref, *refs):
-    inputs, outputs = refs[:12], refs[12:]
-
-    def update(side, rate):
+def owner_kernel(pieces_ref, *refs):
+    arrays, small, outputs = refs[:6], refs[6:12], refs[12:18]
+    small_out, loaded, made, sem = refs[18:24], refs[24:30], refs[30:36], refs[36]
+    chunks = [(0, part, 0.04) for part in range(3)] + [(3, 0, 0.2)]
+    loads, stores = [], []
+    for n, (side, part, _) in enumerate(chunks):
+        cols = pl.ds(part * D, D)
+        for i in range(side, side + 3):
+            slot = n * 3 + i - side
+            loads.append(
+                pltpu.make_async_copy(
+                    arrays[i].at[:, cols], loaded[i].at[:, cols], sem.at[slot]
+                )
+            )
+            loads[-1].start()
+            stores.append(
+                pltpu.make_async_copy(
+                    made[i].at[:, cols], outputs[i].at[:, cols], sem.at[12 + slot]
+                )
+            )
+    rest = jnp.concatenate([pieces_ref[e, PIECE:, :] for e in range(16)], axis=0).astype(full)
+    for side, grad, rate in ((0, rest[:, 0:OWN], 0.03), (3, rest[0:4, 128 : 128 + OWN], 0.3)):
+        new = adamw(*[ref[...] for ref in small[side : side + 3]], grad, rate)
+        for ref, value in zip(small_out[side : side + 3], new):
+            ref[...] = value
+    for n, (side, part, rate) in enumerate(chunks):
+        for load in loads[n * 3 : n * 3 + 3]:
+            load.wait()
         for r in range(2):
             rows = slice(r * PIECE, (r + 1) * PIECE)
             for k in range(2):
-                cols = slice(k * WIDE, (k + 1) * WIDE)
-                grad = pieces_ref[r, k, 0:PIECE, :].astype(full)
-                new = adamw(*[ref[rows, cols] for ref in inputs[side : side + 3]], grad, rate)
-                for ref, value in zip(outputs[side : side + 3], new):
+                cols = slice(part * D + k * WIDE, part * D + (k + 1) * WIDE)
+                grad = pieces_ref[r * 8 + n * 2 + k, 0:PIECE, :].astype(full)
+                new = adamw(*[ref[rows, cols] for ref in loaded[side : side + 3]], grad, rate)
+                for ref, value in zip(made[side : side + 3], new):
                     ref[rows, cols] = value
-
-    last = pl.program_id(0) == 3
-    pl.when(jnp.logical_not(last))(lambda: update(0, 0.04))
-    pl.when(last)(lambda: update(3, 0.2))
-
-    @pl.when(last)
-    def _():
-        rest = jnp.concatenate(
-            [rest_ref[r, k, PIECE :, :] for r in range(2) for k in range(8)], axis=0
-        ).astype(full)
-        for side, grad, rate in (
-            (6, rest[:, 0:OWN], 0.03),
-            (9, rest[0:4, 128 : 128 + OWN], 0.3),
-        ):
-            new = adamw(*[ref[...] for ref in inputs[side : side + 3]], grad, rate)
-            for ref, value in zip(outputs[side : side + 3], new):
-                ref[...] = value
+        for store in stores[n * 3 : n * 3 + 3]:
+            store.start()
+    for store in stores:
+        store.wait()
 
 
 def expert_step_kernel(grad_ref, *refs):
@@ -480,17 +491,17 @@
 
 
 def expert_step(grad, arrays):
-    inner = pl.BlockSpec((1, 128, HID), lambda i: (0, i, 0))
-    outer = pl.BlockSpec((1, HID, 128), lambda i: (0, 0, i))
+    inner = pl.BlockSpec((1, 256, HID), lambda i: (0, i, 0))
+    outer = pl.BlockSpec((1, HID, 256), lambda i: (0, 0, i))
     return pl.pallas_call(
         expert_step_kernel,
-        grid=(D // 128,),
+        grid=(D // 256,),
         out_shape=tuple(hbm(*a.shape) for a in arrays),
-        in_specs=[pl.BlockSpec((128, D), lambda i: (i, 0))]
+        in_specs=[pl.BlockSpec((256, D), lambda i: (i, 0))]
         + [inner] * 3
         + [outer] * 3,
         out_specs=(inner,) * 3 + (outer,) * 3,
-        compiler_params=params(16),
+        compiler_params=params(32),
         cost_estimate=pl.CostEstimate(
             flops=10**7, bytes_accessed=8 * 10**6, transcendentals=10**6
         ),
@@ -658,27 +669,18 @@
 
 
 def owner_step(pieces, arrays, small):
-    qkv = pl.BlockSpec((OWN, D), lambda i: (0, jnp.minimum(i, 2)))
-    proj = pl.BlockSpec((OWN, D), lambda i: (0, 0))
-    whole = [pl.BlockSpec(a.shape, lambda i: (0, 0)) for a in small]
     return pl.pallas_call(
         owner_kernel,
-        grid=(4,),
         out_shape=tuple([hbm(*a.shape) for a in arrays] + [shape(*a.shape) for a in small]),
-        in_specs=[
-            pl.BlockSpec((2, 2, PIECE + 1, WIDE), lambda i: (0, i, 0, 0)),
-            pl.BlockSpec((2, 8, PIECE + 1, WIDE), lambda i: (0, 0, 0, 0)),
-        ]
-        + [qkv] * 3
-        + [proj] * 3
-        + whole,
-        out_specs=tuple([qkv] * 3 + [proj] * 3 + whole),
+        in_specs=in_vmem(1) + in_place(6) + in_vmem(6),
+        out_specs=tuple(in_place(6) + in_vmem(6)),
+        scratch_shapes=vmem_like(arrays) * 2 + [pltpu.SemaphoreType.DMA((24,))],
         compiler_params=params(24),
         cost_estimate=pl.CostEstimate(
             flops=10**7, bytes_accessed=8 * 10**6, transcendentals=10**6
         ),
         name="owner_step",
-    )(pieces, pieces, *pinned(arrays), *small)
+    )(pieces, *pinned(arrays), *small)
 
 
 def exchange(value):
@@ -766,7 +768,7 @@
     block, inner_weight = lax.optimization_barrier((block, inner_weight))
     small = (router_master, router_first, router_second, norm_master, norm_first, norm_second)
     new = owner_step(
-        block.reshape(2, 8, PIECE + 1, WIDE),
+        block,
         (qkv_master, qkv_first, qkv_second, proj_master, proj_first, proj_second),
         [value.T for value in small],
     )

time: 232 us -> 231 us (level)
  no operation moved by 1% of the time
where the time goes in v5:
time: 231 us; the launch traced here: 227 us
  blocking collectives  66.1 us (29%)
  Pallas kernels  63.7 us (28%)
  waiting for transfers between devices  43.7 us (19%)
  starting transfers between devices  29.2 us (13%)
  between operations  14.5 us (6%)
  other arithmetic  5.53 us (2%)
  local copies, waits for them, and re-layouts  4.51 us (2%)
    all_to_all x2, blocking collectives, exchange(): return lax.all_to_all(value, 'exp', split_axis=0, concat_axis=0, tiled=True)  66.1 us
    ppermute x9, waiting for transfers between devices, along(): return lax.ppermute(value, 'grp', hops)  19.6 us
    pallas_call x1, Pallas kernels, experts_both_ways(): pl.pallas_call(expert_kernel, grid=(GRP // 2,), out_shape=(pltpu.VMEM((EX...  16.7 us
    all_to_all x2, waiting for transfers between devices, exchange(): return lax.all_to_all(value, 'exp', split_axis=0, concat_axis=0, tiled=True)  14.7 us
    pallas_call x1, Pallas kernels, token_backward(): pl.pallas_call(backward_kernel, out_shape=outs, in_specs=[in_smem()] + in...  14.2 us
    pallas_call x1, Pallas kernels, expert_grads(): pl.pallas_call(expert_grad_kernel, grid=(GRP // 2,), out_shape=hbm(GRP *...  11.8 us
    ppermute x9, starting transfers between devices, along(): return lax.ppermute(value, 'grp', hops)  11.8 us
    all_to_all x2, starting transfers between devices, exchange(): return lax.all_to_all(value, 'exp', split_axis=0, concat_axis=0, tiled=True)  10.3 us
  transfers between devices with their start and end apart: 22, of which 12 were waited for; matrix products, arithmetic and copies ran while one was open for 4% of the time, Pallas kernels for 18%

profile of v5, /device:TPU:1, one launch (start us, length us, event | category | flops | bytes accessed | tf_op | source)
XLA Modules:
  0.0 227.2 jit_solution(11050043521899727139)
XLA Ops:
  7.2 0.0 copy-start.9
  7.2 0.0 all-gather.2.cloned.1.call-start
  7.3 1.5 pack.1
  8.7 0.0 copy-start.6
  8.8 2.1 collective-permute-start
  10.9 1.3 collective-permute-start.1
  12.2 1.1 copy.55
  13.3 5.4 %collective-permute-done.refs_2_.refs_11_ = bf16[48,3200]{1,0:T(8,128)(2,1)S(1)} collective-permute-done((bf16[48,3200]{1,0:T(8,128)(2,1)S(1)}, bf16[48,3200]{1,0:T(8,128)(2,1)S(1)}, u32[]{:S(2)}, u32[]{:S(2)}) %collective-permute-start) | collective-permute-done | bytes 307232 | tf_op jit(solution)/shard_map/ppermute | solution.py:80
  18.7 0.1 collective-permute-done.1.refs_5_.refs_14_
  18.8 1.2 collective-permute-start.2
  20.0 1.5 collective-permute-start.3
  21.5 0.1 convert_bitcast_fusion.1
  21.6 1.1 pad_maximum_fusion
  22.7 4.2 %collective-permute-done.2.refs_3_.refs_12_ = bf16[48,3200]{1,0:T(8,128)(2,1)S(1)} collective-permute-done((bf16[48,3200]{1,0:T(8,128)(2,1)S(1)}, bf16[48,3200]{1,0:T(8,128)(2,1)S(1)}, u32[]{:S(2)}, u32[]{:S(2)}) %collective-permute-start.2) | collective-permute-done | bytes 307232 | tf_op jit(solution)/shard_map/ppermute | solution.py:80
  26.9 0.0 all-gather.2.cloned.1.call-update
  27.0 2.9 %collective-permute-start.6 = (bf16[48,3200]{1,0:T(8,128)(2,1)S(1)}, bf16[48,3200]{1,0:T(8,128)(2,1)S(1)}, u32[]{:S(2)}, u32[]{:S(2)}) collective-permute-start(bf16[48,3200]{1,0:T(8,128)(2,1)S(1)} %get-tuple-element.68.refs_0_.refs_9_), channel_id=1, source_target_pairs={{0,16},{16,0},{32,48},{48,32},{64,80},{80,64},{96,112},{112,96},{1... | collective-permute-start | bytes 921608 | tf_op jit(solution)/shard_map/ppermute | solution.py:83
  29.8 0.1 collective-permute-start.7
  29.9 0.1 copy.48
  30.1 0.1 eq.32
  30.2 1.2 reduce-window.6
  31.4 0.2 slice_reduce_fusion
  31.6 0.1 bitcast_bitcast_fusion
  31.7 0.4 collective-permute-start.8
  32.2 0.9 collective-permute-start.4
  33.1 1.8 collective-permute-start.5
  34.9 0.1 reshape.74
  35.0 0.1 copy.49
  35.2 0.7 collective-permute-start.11
  36.0 0.1 collective-permute-start.9
  36.1 0.4 collective-permute-start.10
  36.5 5.7 %collective-permute-done.4.refs_6_.refs_15_ = bf16[48,3200]{1,0:T(8,128)(2,1)S(1)} collective-permute-done((bf16[48,3200]{1,0:T(8,128)(2,1)S(1)}, bf16[48,3200]{1,0:T(8,128)(2,1)S(1)}, u32[]{:S(2)}, u32[]{:S(2)}) %collective-permute-start.4) | collective-permute-done | bytes 307232 | tf_op jit(solution)/shard_map/ppermute | solution.py:80
  42.2 0.9 collective-permute-start.12
  43.1 0.1 collective-permute-start.13
  43.2 0.1 copy.54.trow_ref
  43.3 0.1 stack.75.rows_ref
  43.5 1.2 collective-permute-done.12.refs_14_.refs_23_
  44.7 0.9 collective-permute-done.13.refs_15_.refs_24_
  45.6 8.0 %token_forward.1 = (bf16[16,400,128]{2,1,0:T(8,128)(2,1)S(1)}, f32[208,768]{1,0:T(8,128)}, bf16[208,768]{1,0:T(8,128)(2,1)}, bf16[208,2304]{1,0:T(8,128)(2,1)}, ...) custom-call(s32[18]{0:T(128)S(1)} %stack.75.rows_ref, ...), custom_call_target="tpu_custom_call" | custom-call | flops 4000000000 | bytes 12000000 | tf_op jit(solution)/shard_map/token_forward/pallas_call | solution.py:572
  53.7 30.5 %all_to_all.20.got_ref = bf16[16,400,128]{2,1,0:T(8,128)(2,1)S(1)} all-to-all(bf16[16,400,128]{2,1,0:T(8,128)(2,1)S(1)} %get-tuple-element.70), channel_id=1, replica_groups=mesh['grp'=8,'exp'=16] {'exp'}, dimensions={0} | all-to-all | bytes 3276800 | tf_op jit(solution)/shard_map/all_to_all | solution.py:687
  84.1 2.1 all-gather.2.cloned.1.call-done.w_ref
  86.3 16.7 %experts.1 = (bf16[16,400,128]{2,1,0:T(8,128)(2,1)}, bf16[528,3072]{1,0:T(8,128)(2,1)}, bf16[528,3072]{1,0:T(8,128)(2,1)}, bf16[768,528]{1,0:T(8,128)(2,1)}, bf16[768,528]{1,0:T(8,128)(2,1)}) custom-call(bf16[16,400,128]{2,1,0:T(8,128)(2,1)S(1)} %all_to_all.20.got_ref, bf16[6144,768]{1,0:T(8,128)(2,1)} %all-gather.2.cloned.1.call-done.w_ref), custom_call_target="tpu_custom_call" | custom-call | flops 10000000000 | bytes 23000000 | tf_op jit(solution)/shard_map/experts/pallas_call | solution.py:602
  103.0 6.7 %all-to-all-start.1 = ((bf16[16,400,128]{2,1,0:T(8,128)(2,1)}), bf16[16,400,128]{2,1,0:T(8,128)(2,1)S(1)}, u32[]{:S(2)}, u32[]{:S(2)}) async-start(bf16[16,400,128]{2,1,0:T(8,128)(2,1)} %get-tuple-element.72), calls=%async_computation.1 | async-start | bytes 3276800 | tf_op jit(solution)/shard_map/all_to_all | solution.py:687
  109.7 0.0 reduce-scatter.2.cloned.1.call-start
  109.7 11.8 %expert_grads.1 = bf16[6144,768]{1,0:T(8,128)(2,1)} custom-call(bf16[528,3072]{1,0:T(8,128)(2,1)} %get-tuple-element.84.h_ref, bf16[528,3072]{1,0:T(8,128)(2,1)} %get-tuple-element.85.du_ref, bf16[768,528]{1,0:T(8,128)(2,1)} %get-tuple-element.86.xt_ref, bf16[768,528]{1,0:T(8,128)(2,1)} %get-tuple-element.87.dzt_ref), custom_call_target="tpu_custom_call" | custom-call | flops 6000000000 | bytes 18000000 | tf_op jit(solution)/shard_map/expert_grads/pallas_call | solution.py:624
  121.5 0.0 reduce-scatter.2.cloned.1.call-update
  121.6 13.7 %all-to-all-done.1.back_ref = bf16[16,400,128]{2,1,0:T(8,128)(2,1)S(1)} async-done(((bf16[16,400,128]{2,1,0:T(8,128)(2,1)}), bf16[16,400,128]{2,1,0:T(8,128)(2,1)S(1)}, u32[]{:S(2)}, u32[]{:S(2)}) %all-to-all-start.1) | async-done | bytes 1638432 | tf_op jit(solution)/shard_map/all_to_all | solution.py:687
  135.2 14.2 %token_backward.1 = (bf16[1,197,768]{2,1,0:T(8,128)(2,1)}, f32[1,197,768]{2,1,0:T(8,128)}, bf16[16,208,384]{2,1,0:T(8,128)(2,1)}, bf16[16,208,384]{2,1,0:T(8,128)(2,1)}) custom-call(s32[18]{0:T(128)S(1)} %stack.75.rows_ref, s32[208,2]{1,0:T(8,128)S(1)} %pad.15.ids_ref, s32[208,2]{1,0:T(8,128)S(1)} %get-tuple-element.152.tcol_ref, ...), custom_call_target="tpu_custom_call" | custom-call | flops 399999991808 | bytes 18000000 | tf_op jit(solution)/shard_map/token_backward/pallas_call | solution.py:645
  149.4 1.4 collective-permute-start.14
  150.9 5.1 %collective-permute-done.14 = bf16[16,208,384]{2,1,0:T(8,128)(2,1)S(1)} collective-permute-done((bf16[16,208,384]{2,1,0:T(8,128)(2,1)}, bf16[16,208,384]{2,1,0:T(8,128)(2,1)S(1)}, u32[]{:S(2)}, u32[]{:S(2)}) %collective-permute-start.14) | collective-permute-done | bytes 2555936 | tf_op jit(solution)/shard_map/ppermute | solution.py:695
  155.9 2.6 %add_convert_fusion = bf16[16,208,384]{2,1,0:T(8,128)(2,1)S(1)} fusion(bf16[16,208,384]{2,1,0:T(8,128)(2,1)S(1)} %collective-permute-done.14, bf16[16,208,384]{2,1,0:T(8,128)(2,1)} %get-tuple-element.82), kind=kLoop, calls=%fused_computation.1 | loop fusion | flops 5111808 | bytes 7667712 | tf_op jit(solution)/shard_map/convert_element_type | solution.py:696
  158.5 35.6 %all_to_all.21 = bf16[16,208,384]{2,1,0:T(8,128)(2,1)S(1)} all-to-all(bf16[16,208,384]{2,1,0:T(8,128)(2,1)S(1)} %add_convert_fusion), channel_id=1, replica_groups=mesh['grp'=8,'exp'=16] {'exp'}, dimensions={0} | all-to-all | bytes 5111808 | tf_op jit(solution)/shard_map/all_to_all | solution.py:687
  194.1 0.4 convert_reduce_fusion
  194.6 0.1 collective-permute-start.15
  194.7 2.7 %collective-permute-start.17 = (bf16[49,384]{1,0:T(8,128)(2,1)S(1)}, bf16[49,384]{1,0:T(8,128)(2,1)S(1)}, u32[]{:S(2)}, u32[]{:S(2)}) collective-permute-start(bf16[49,384]{1,0:T(8,128)(2,1)S(1)} %get-tuple-element.149), channel_id=1, source_target_pairs={{0,96},{16,112},{32,0},{48,16},{64,32},{80,48},{96,64},{112,80},{1... | collective-permute-start | bytes 112904 | tf_op jit(solution)/shard_map/ppermute | solution.py:693
  197.4 0.2 collective-permute-start.16
  197.6 1.2 collective-permute-done.15
  198.8 3.0 %collective-permute-done.16 = bf16[49,384]{1,0:T(8,128)(2,1)S(1)} collective-permute-done((bf16[49,384]{1,0:T(8,128)(2,1)S(1)}, bf16[49,384]{1,0:T(8,128)(2,1)S(1)}, u32[]{:S(2)}, u32[]{:S(2)}) %collective-permute-start.16) | collective-permute-done | bytes 37664 | tf_op jit(solution)/shard_map/ppermute | solution.py:693
  201.8 0.9 broadcast_in_dim.16
  202.7 3.6 %all-to-all-start.3 = ((bf16[16,49,384]{2,1,0:T(8,128)(2,1)}), bf16[16,49,384]{2,1,0:T(8,128)(2,1)S(1)}, u32[]{:S(2)}, u32[]{:S(2)}) async-start(bf16[16,49,384]{2,1,0:T(8,128)(2,1)} %broadcast_in_dim.16), calls=%async_computation.3 | async-start | bytes 1376256 | tf_op jit(solution)/shard_map/all_to_all | solution.py:687
  206.3 1.4 copy.56
  207.8 0.0 reduce-scatter.2.cloned.1.call-done.grad_ref
  207.8 7.5 %expert_step.1 = (f32[1,768,384]{2,1,0:T(8,128)}, f32[1,768,384]{2,1,0:T(8,128)}, f32[1,768,384]{2,1,0:T(8,128)}, f32[1,384,768]{2,1,0:T(8,128)}, f32[1,384,768]{2,1,0:T(8,128)}, /*index=5*/f32[1,384,768]{2,1,0:T(8,128)}) custom-call(bf16[768,768]{1,0:T(8,128)(2,1)} %reduce-scatter.2.cloned.1.call-done.grad_ref, f32[1,768,384]{2,1,0:T(8,128)} %refs_0_.2, ...), custom_call_target="tpu_custom_call" | custom-call | flops 10000000 | bytes 8000000 | tf_op jit(solution)/shard_map/expert_step/pallas_call | solution.py:496
  215.3 1.0 all-to-all-done.3.pieces_ref
  216.4 4.0 %owner_step.1 = (f32[96,2304]{1,0:T(8,128)}, f32[96,2304]{1,0:T(8,128)}, f32[96,2304]{1,0:T(8,128)}, f32[96,768]{1,0:T(8,128)}, f32[96,768]{1,0:T(8,128)}, /*ind...) custom-call(bf16[16,49,384]{2,1,0:T(8,128)(2,1)S(1)} %all-to-all-don, ...), custom_call_target="tpu_custom_call" | custom-call | flops 10000000 | bytes 8000000 | tf_op jit(solution)/shard_map/owner_step/pallas_call | solution.py:672
  (69 shorter events, 0.4 us)
Async XLA Ops:
  7.2 5.0 %copy-start.8 = (f32[1,384,768]{2,1,0:T(8,128)S(1)}, f32[1,384,768]{2,1,0:T(8,128)}, u32[]{:S(2)}) copy-start(f32[1,384,768]{2,1,0:T(8,128)} %refs_3_.2) | copy-start | bytes 3538948
  7.2 14.3 %copy-start.9 = (f32[1,768,384]{2,1,0:T(8,128)S(1)}, f32[1,768,384]{2,1,0:T(8,128)}, u32[]{:S(2)}) copy-start(f32[1,768,384]{2,1,0:T(8,128)} %refs_0_.2) | copy-start | bytes 3538948
  7.2 79.0 %all-gather.2.cloned.1.call-start = ((), (), s32[]{:S(2)}) async-start(), calls=%async_computation.5 | async-start | bytes 10616832 | tf_op jit(solution)/shard_map/all_gather | solution.py:732
  8.7 18.2 %copy-start.6 = (bf16[48,3200]{1,0:T(8,128)(2,1)}, bf16[48,3200]{1,0:T(8,128)(2,1)S(1)}, u32[]{:S(2)}) copy-start(bf16[48,3200]{1,0:T(8,128)(2,1)S(1)} %get-tuple-element.68.refs_0_.refs_9_) | copy-start | bytes 921604
  8.8 21.1 %copy-start.7 = (bf16[48,3200]{1,0:T(8,128)(2,1)}, bf16[48,3200]{1,0:T(8,128)(2,1)S(1)}, u32[]{:S(2)}) copy-start(bf16[48,3200]{1,0:T(8,128)(2,1)S(1)} %get-tuple-element.67.refs_1_.refs_10_) | copy-start | bytes 921604
  8.8 9.9 %collective-permute-start = (bf16[48,3200]{1,0:T(8,128)(2,1)S(1)}, bf16[48,3200]{1,0:T(8,128)(2,1)S(1)}, u32[]{:S(2)}, u32[]{:S(2)}) collective-permute-start(bf16[48,3200]{1,0:T(8,128)(2,1)S(1)} %get-tuple-element.68.refs_0_.refs_9_), channel_id=1, source_target_pairs={{0,32},{16,48},{32,64},{48,80},{64,96},{80,112},{96,0},{112,16},{1... | collective-permute-start | bytes 921608 | tf_op jit(solution)/shard_map/ppermute | solution.py:80
  10.9 7.9 %collective-permute-start.1 = (bf16[48,3200]{1,0:T(8,128)(2,1)S(1)}, bf16[48,3200]{1,0:T(8,128)(2,1)}, u32[]{:S(2)}, u32[]{:S(2)}) collective-permute-start(bf16[48,3200]{1,0:T(8,128)(2,1)S(1)} %get-tuple-element.67.refs_1_.refs_10_), channel_id=1, source_target_pairs={{0,96},{16,112},{32,0},{48,16},{64,32},{80,48},{96,64},{112,80},{1... | collective-permute-start | bytes 921608 | tf_op jit(solution)/shard_map/ppermute | solution.py:80
  13.3 8.3 %copy-start.10 = (bf16[1,384,768]{1,2,0:T(8,128)(2,1)S(1)}, bf16[1,384,768]{1,2,0:T(8,128)(2,1)}, u32[]{:S(2)}) copy-start(bf16[1,384,768]{1,2,0:T(8,128)(2,1)} %copy.55) | copy-start | bytes 1769476
  18.7 13.5 %copy-start.14 = (bf16[48,3200]{1,0:T(8,128)(2,1)}, bf16[48,3200]{1,0:T(8,128)(2,1)S(1)}, u32[]{:S(2)}) copy-start(bf16[48,3200]{1,0:T(8,128)(2,1)S(1)} %collective-permute-done.refs_2_.refs_11_) | copy-start | bytes 921604
  18.8 8.1 %collective-permute-start.2 = (bf16[48,3200]{1,0:T(8,128)(2,1)S(1)}, bf16[48,3200]{1,0:T(8,128)(2,1)S(1)}, u32[]{:S(2)}, u32[]{:S(2)}) collective-permute-start(bf16[48,3200]{1,0:T(8,128)(2,1)S(1)} %get-tuple-element.67.refs_1_.refs_10_), channel_id=1, source_target_pairs={{0,32},{16,48},{32,64},{48,80},{64,96},{80,112},{96,0},{112,16},{1... | collective-permute-start | bytes 921608 | tf_op jit(solution)/shard_map/ppermute | solution.py:80
  20.0 6.9 %collective-permute-start.3 = (bf16[48,3200]{1,0:T(8,128)(2,1)S(1)}, bf16[48,3200]{1,0:T(8,128)(2,1)S(1)}, u32[]{:S(2)}, u32[]{:S(2)}) collective-permute-start(bf16[48,3200]{1,0:T(8,128)(2,1)S(1)} %get-tuple-element.68.refs_0_.refs_9_), channel_id=1, source_target_pairs={{0,96},{16,112},{32,0},{48,16},{64,32},{80,48},{96,64},{112,80},{1... | collective-permute-start | bytes 921608 | tf_op jit(solution)/shard_map/ppermute | solution.py:80
  21.6 8.4 %copy-start.12 = (s32[1,197,2]{1,2,0:T(2,128)S(1)}, s32[1,197,2]{1,2,0:T(2,128)}, u32[]{:S(2)}) copy-start(s32[1,197,2]{1,2,0:T(2,128)} %param.24) | copy-start | bytes 4732
  21.6 13.5 %copy-start.13 = (s32[1,197,2]{1,2,0:T(2,128)S(1)}, s32[1,197,2]{1,2,0:T(2,128)}, u32[]{:S(2)}) copy-start(s32[1,197,2]{1,2,0:T(2,128)} %param.25) | copy-start | bytes 4732
  26.9 16.4 %copy-start.15 = (bf16[48,3200]{1,0:T(8,128)(2,1)}, bf16[48,3200]{1,0:T(8,128)(2,1)S(1)}, u32[]{:S(2)}) copy-start(bf16[48,3200]{1,0:T(8,128)(2,1)S(1)} %collective-permute-done.2.refs_3_.refs_12_) | copy-start | bytes 921604
  26.9 16.4 %copy-start.16 = (bf16[48,3200]{1,0:T(8,128)(2,1)}, bf16[48,3200]{1,0:T(8,128)(2,1)S(1)}, u32[]{:S(2)}) copy-start(bf16[48,3200]{1,0:T(8,128)(2,1)S(1)} %collective-permute-done.3.refs_4_.refs_13_) | copy-start | bytes 921604
  27.0 8.3 %collective-permute-start.6 = (bf16[48,3200]{1,0:T(8,128)(2,1)S(1)}, bf16[48,3200]{1,0:T(8,128)(2,1)S(1)}, u32[]{:S(2)}, u32[]{:S(2)}) collective-permute-start(bf16[48,3200]{1,0:T(8,128)(2,1)S(1)} %get-tuple-element.68.refs_0_.refs_9_), channel_id=1, source_target_pairs={{0,16},{16,0},{32,48},{48,32},{64,80},{80,64},{96,112},{112,96},{1... | collective-permute-start | bytes 921608 | tf_op jit(solution)/shard_map/ppermute | solution.py:83
  29.8 6.1 %collective-permute-start.7 = (bf16[48,3200]{1,0:T(8,128)(2,1)S(1)}, bf16[48,3200]{1,0:T(8,128)(2,1)S(1)}, u32[]{:S(2)}, u32[]{:S(2)}) collective-permute-start(bf16[48,3200]{1,0:T(8,128)(2,1)S(1)} %get-tuple-element.67.refs_1_.refs_10_), channel_id=1, source_target_pairs={{0,16},{16,0},{32,48},{48,32},{64,80},{80,64},{96,112},{112,96},{1... | collective-permute-start | bytes 921608 | tf_op jit(solution)/shard_map/ppermute | solution.py:83
  31.7 4.4 %collective-permute-start.8 = (bf16[48,3200]{1,0:T(8,128)(2,1)S(1)}, bf16[48,3200]{1,0:T(8,128)(2,1)S(1)}, u32[]{:S(2)}, u32[]{:S(2)}) collective-permute-start(bf16[48,3200]{1,0:T(8,128)(2,1)S(1)} %collective-permute-done.refs_2_.refs_11_), channel_id=1, source_target_pairs={{0,16},{16,0},{32,48},{48,32},{64,80},{80,64},{96,112},{112,96},{1... | collective-permute-start | bytes 921608 | tf_op jit(solution)/shard_map/ppermute | solution.py:83
  32.2 10.0 %collective-permute-start.4 = (bf16[48,3200]{1,0:T(8,128)(2,1)S(1)}, bf16[48,3200]{1,0:T(8,128)(2,1)S(1)}, u32[]{:S(2)}, u32[]{:S(2)}) collective-permute-start(bf16[48,3200]{1,0:T(8,128)(2,1)S(1)} %collective-permute-done.refs_2_.refs_11_), channel_id=1, source_target_pairs={{0,32},{16,48},{32,64},{48,80},{64,96},{80,112},{96,0},{112,16},{1... | collective-permute-start | bytes 921608 | tf_op jit(solution)/shard_map/ppermute | solution.py:80
  33.1 10.0 %collective-permute-start.5 = (bf16[48,3200]{1,0:T(8,128)(2,1)}, bf16[48,3200]{1,0:T(8,128)(2,1)}, u32[]{:S(2)}, u32[]{:S(2)}) collective-permute-start(bf16[48,3200]{1,0:T(8,128)(2,1)} %collective-permute-done.1.refs_5_.refs_14_), channel_id=1, source_target_pairs={{0,96},{16,112},{32,0},{48,16},{64,32},{80,48},{96,64},{112,80},{1... | collective-permute-start | bytes 921608 | tf_op jit(solution)/shard_map/ppermute | solution.py:80
  35.2 10.4 %copy-start.17 = (bf16[48,3200]{1,0:T(8,128)(2,1)}, bf16[48,3200]{1,0:T(8,128)(2,1)S(1)}, u32[]{:S(2)}) copy-start(bf16[48,3200]{1,0:T(8,128)(2,1)S(1)} %collective-permute-done.6.refs_8_.refs_17_) | copy-start | bytes 921604
  35.2 8.2 %collective-permute-start.11 = (bf16[48,3200]{1,0:T(8,128)(2,1)}, bf16[48,3200]{1,0:T(8,128)(2,1)S(1)}, u32[]{:S(2)}, u32[]{:S(2)}) collective-permute-start(bf16[48,3200]{1,0:T(8,128)(2,1)} %collective-permute-done.1.refs_5_.refs_14_), channel_id=1, source_target_pairs={{0,16},{16,0},{32,48},{48,32},{64,80},{80,64},{96,112},{112,96},{1... | collective-permute-start | bytes 921608 | tf_op jit(solution)/shard_map/ppermute | solution.py:83
  36.0 9.6 %copy-start.18 = (bf16[48,3200]{1,0:T(8,128)(2,1)}, bf16[48,3200]{1,0:T(8,128)(2,1)S(1)}, u32[]{:S(2)}) copy-start(bf16[48,3200]{1,0:T(8,128)(2,1)S(1)} %collective-permute-done.7.refs_9_.refs_18_) | copy-start | bytes 921604
  36.0 7.5 %collective-permute-start.9 = (bf16[48,3200]{1,0:T(8,128)(2,1)S(1)}, bf16[48,3200]{1,0:T(8,128)(2,1)}, u32[]{:S(2)}, u32[]{:S(2)}) collective-permute-start(bf16[48,3200]{1,0:T(8,128)(2,1)S(1)} %collective-permute-done.2.refs_3_.refs_12_), channel_id=1, source_target_pairs={{0,16},{16,0},{32,48},{48,32},{64,80},{80,64},{96,112},{112,96},{1... | collective-permute-start | bytes 921608 | tf_op jit(solution)/shard_map/ppermute | solution.py:83
  36.1 9.5 %copy-start.19 = (bf16[48,3200]{1,0:T(8,128)(2,1)}, bf16[48,3200]{1,0:T(8,128)(2,1)S(1)}, u32[]{:S(2)}) copy-start(bf16[48,3200]{1,0:T(8,128)(2,1)S(1)} %collective-permute-done.8.refs_10_.refs_19_) | copy-start | bytes 921604
  36.1 7.4 %collective-permute-start.10 = (bf16[48,3200]{1,0:T(8,128)(2,1)S(1)}, bf16[48,3200]{1,0:T(8,128)(2,1)}, u32[]{:S(2)}, u32[]{:S(2)}) collective-permute-start(bf16[48,3200]{1,0:T(8,128)(2,1)S(1)} %collective-permute-done.3.refs_4_.refs_13_), channel_id=1, source_target_pairs={{0,16},{16,0},{32,48},{48,32},{64,80},{80,64},{96,112},{112,96},{1... | collective-permute-start | bytes 921608 | tf_op jit(solution)/shard_map/ppermute | solution.py:83
  42.2 3.4 %copy-start.20 = (bf16[48,3200]{1,0:T(8,128)(2,1)}, bf16[48,3200]{1,0:T(8,128)(2,1)S(1)}, u32[]{:S(2)}) copy-start(bf16[48,3200]{1,0:T(8,128)(2,1)S(1)} %collective-permute-done.4.refs_6_.refs_15_) | copy-start | bytes 921604
  42.2 2.5 %collective-permute-start.12 = (bf16[48,3200]{1,0:T(8,128)(2,1)S(1)}, bf16[48,3200]{1,0:T(8,128)(2,1)S(1)}, u32[]{:S(2)}, u32[]{:S(2)}) collective-permute-start(bf16[48,3200]{1,0:T(8,128)(2,1)S(1)} %collective-permute-done.4.refs_6_.refs_15_), channel_id=1, source_target_pairs={{0,16},{16,0},{32,48},{48,32},{64,80},{80,64},{96,112},{112,96},{1... | collective-permute-start | bytes 921608 | tf_op jit(solution)/shard_map/ppermute | solution.py:83
  43.1 2.5 %collective-permute-start.13 = (bf16[48,3200]{1,0:T(8,128)(2,1)}, bf16[48,3200]{1,0:T(8,128)(2,1)}, u32[]{:S(2)}, u32[]{:S(2)}) collective-permute-start(bf16[48,3200]{1,0:T(8,128)(2,1)} %collective-permute-done.5.refs_7_.refs_16_), channel_id=1, source_target_pairs={{0,16},{16,0},{32,48},{48,32},{64,80},{80,64},{96,112},{112,96},{1... | collective-permute-start | bytes 921608 | tf_op jit(solution)/shard_map/ppermute | solution.py:83
  43.4 2.2 copy-start.21
  44.7 1.0 copy-start.22
  103.0 32.3 %all-to-all-start.1 = ((bf16[16,400,128]{2,1,0:T(8,128)(2,1)}), bf16[16,400,128]{2,1,0:T(8,128)(2,1)S(1)}, u32[]{:S(2)}, u32[]{:S(2)}) async-start(bf16[16,400,128]{2,1,0:T(8,128)(2,1)} %get-tuple-element.72), calls=%async_computation.1 | async-start | bytes 3276800 | tf_op jit(solution)/shard_map/all_to_all | solution.py:687
  109.7 98.1 %reduce-scatter.2.cloned.1.call-start = ((), (), s32[]{:S(2)}) async-start(), calls=%async_computation.6 | async-start | bytes 10616832 | tf_op jit(solution)/shard_map/reduce_scatter | solution.py:751
  149.4 6.5 %collective-permute-start.14 = (bf16[16,208,384]{2,1,0:T(8,128)(2,1)}, bf16[16,208,384]{2,1,0:T(8,128)(2,1)S(1)}, u32[]{:S(2)}, u32[]{:S(2)}) collective-permute-start(bf16[16,208,384]{2,1,0:T(8,128)(2,1)} %get-tuple-element.83), channel_id=1, source_target_pairs={{0,16},{16,0},{32,48},{48,32},{64,80},{80,64},{96,112},{112,96},{1... | collective-permute-start | bytes 7667720 | tf_op jit(solution)/shard_map/ppermute | solution.py:695
  194.6 11.7 %copy-start.11 = (f32[1,197,768]{2,1,0:T(8,128)S(1)}, f32[1,197,768]{2,1,0:T(8,128)}, u32[]{:S(2)}) copy-start(f32[1,197,768]{2,1,0:T(8,128)} %get-tuple-element.129) | copy-start | bytes 1815556
  194.6 4.2 %collective-permute-start.15 = (bf16[49,384]{1,0:T(8,128)(2,1)S(1)}, bf16[49,384]{1,0:T(8,128)(2,1)S(1)}, u32[]{:S(2)}, u32[]{:S(2)}) collective-permute-start(bf16[49,384]{1,0:T(8,128)(2,1)S(1)} %get-tuple-element.148), channel_id=1, source_target_pairs={{0,32},{16,48},{32,64},{48,80},{64,96},{80,112},{96,0},{112,16},{1... | collective-permute-start | bytes 112904 | tf_op jit(solution)/shard_map/ppermute | solution.py:693
  194.7 4.1 %collective-permute-start.17 = (bf16[49,384]{1,0:T(8,128)(2,1)S(1)}, bf16[49,384]{1,0:T(8,128)(2,1)S(1)}, u32[]{:S(2)}, u32[]{:S(2)}) collective-permute-start(bf16[49,384]{1,0:T(8,128)(2,1)S(1)} %get-tuple-element.149), channel_id=1, source_target_pairs={{0,96},{16,112},{32,0},{48,16},{64,32},{80,48},{96,64},{112,80},{1... | collective-permute-start | bytes 112904 | tf_op jit(solution)/shard_map/ppermute | solution.py:693
  197.4 4.4 %collective-permute-start.16 = (bf16[49,384]{1,0:T(8,128)(2,1)S(1)}, bf16[49,384]{1,0:T(8,128)(2,1)S(1)}, u32[]{:S(2)}, u32[]{:S(2)}) collective-permute-start(bf16[49,384]{1,0:T(8,128)(2,1)S(1)} %get-tuple-element.150), channel_id=1, source_target_pairs={{0,64},{16,80},{32,96},{48,112},{64,0},{80,16},{96,32},{112,48},{1... | collective-permute-start | bytes 112904 | tf_op jit(solution)/shard_map/ppermute | solution.py:693
  202.7 13.6 %all-to-all-start.3 = ((bf16[16,49,384]{2,1,0:T(8,128)(2,1)}), bf16[16,49,384]{2,1,0:T(8,128)(2,1)S(1)}, u32[]{:S(2)}, u32[]{:S(2)}) async-start(bf16[16,49,384]{2,1,0:T(8,128)(2,1)} %broadcast_in_dim.16), calls=%async_computation.3 | async-start | bytes 1376256 | tf_op jit(solution)/shard_map/all_to_all | solution.py:687
  207.8 8.6 %copy-start = (f32[96,16]{0,1:T(8,128)S(1)}, f32[96,16]{0,1:T(8,128)}, u32[]{:S(2)}) copy-start(f32[96,16]{0,1:T(8,128)} %param.32) | copy-start | bytes 18436
  207.8 8.6 %copy-start.1 = (f32[96,16]{0,1:T(8,128)S(1)}, f32[96,16]{0,1:T(8,128)}, u32[]{:S(2)}) copy-start(f32[96,16]{0,1:T(8,128)} %param.33) | copy-start | bytes 18436
  207.8 8.6 %copy-start.2 = (f32[96,16]{0,1:T(8,128)S(1)}, f32[96,16]{0,1:T(8,128)}, u32[]{:S(2)}) copy-start(f32[96,16]{0,1:T(8,128)} %param.34) | copy-start | bytes 18436
  207.8 8.6 %copy-start.3 = (f32[96,4]{0,1:T(4,128)S(1)}, f32[96,4]{0,1:T(4,128)}, u32[]{:S(2)}) copy-start(f32[96,4]{0,1:T(4,128)} %param.35) | copy-start | bytes 4612
  207.8 8.6 %copy-start.4 = (f32[96,4]{0,1:T(4,128)S(1)}, f32[96,4]{0,1:T(4,128)}, u32[]{:S(2)}) copy-start(f32[96,4]{0,1:T(4,128)} %param.36) | copy-start | bytes 4612
  207.8 8.6 %copy-start.5 = (f32[96,4]{0,1:T(4,128)S(1)}, f32[96,4]{0,1:T(4,128)}, u32[]{:S(2)}) copy-start(f32[96,4]{0,1:T(4,128)} %param.37) | copy-start | bytes 4612
Sparse Core Ops, SparseCore 0:
  27.1 59.1 all-gather.1
  121.7 57.1 reduce-scatter.1

commit v6 on v5

--- a/solution.py
+++ b/solution.py
@@ -74,7 +74,7 @@
         out_ref[:, 3072:3200] = rest[rows, :]
 
 
-def dense_pieces(first, second):
+def dense_pieces(first, second, target):
     def along(step, value):
         hops = [(2 * x + c, 2 * ((x + step) % 4) + c) for x in range(4) for c in range(2)]
         return lax.ppermute(value, "grp", hops)
@@ -83,13 +83,13 @@
         return lax.ppermute(value, "grp", [(i, i ^ 1) for i in range(GRP)])
 
     up_first, down_second = along(1, first), along(3, second)
-    up_first, down_second, again, other = lax.optimization_barrier(
-        (up_first, down_second, second, first)
+    up_first, down_second, again, other, target = lax.optimization_barrier(
+        (up_first, down_second, second, first, target)
     )
     up_second, down_first = along(1, again), along(3, other)
     far_first, far_second = along(1, up_first), along(3, down_second)
     here = [first, second, up_first, up_second, down_first, down_second, far_first, far_second]
-    return here + [across(piece) for piece in here]
+    return here + [across(piece) for piece in here], target
 
 
 def piece_rows(place):
@@ -725,12 +725,6 @@
     outer_first,
     outer_second,
 ):
-    pieces = dense_pieces(*pack(qkv_master, proj_master, router_master, norm_master))
-    rows = piece_rows(lax.axis_index("grp"))
-    mine = jnp.concatenate([inner_master[0].astype(low), outer_master[0].astype(low).T], axis=1)
-    mine, *_ = lax.optimization_barrier((mine, pieces[3], pieces[4]))
-    weights = lax.all_gather(mine, "grp", axis=0, tiled=True)
-
     ids = expert_ids.reshape(TOK, 2)
     kept = kept_routes.reshape(TOK, 2)
     flat = ids.reshape(-1)
@@ -742,6 +736,13 @@
     target = jnp.pad(target, padding, constant_values=-1)
     ids = jnp.pad(ids, padding, constant_values=-1)
     keep = jnp.pad(kept.astype(full), padding)
+
+    packed = pack(qkv_master, proj_master, router_master, norm_master)
+    pieces, target = dense_pieces(*packed, target)
+    rows = piece_rows(lax.axis_index("grp"))
+    mine = jnp.concatenate([inner_master[0].astype(low), outer_master[0].astype(low).T], axis=1)
+    mine, *_ = lax.optimization_barrier((mine, pieces[3], pieces[4]))
+    weights = lax.all_gather(mine, "grp", axis=0, tiled=True)
 
     send, m, a, qkv, p, o, c, r = token_forward(
         rows, ids, keep, target.T, images, cotangent, *pieces

time: 231 us -> 231 us (level)
  transfers between devices with their start and end apart: 22 -> 22, of which waited for: 12 -> 11; matrix products, arithmetic and copies ran while one was open for 4% -> 5% of each run, Pallas kernels for 18% -> 18%
where the time goes in v6:
time: 231 us; the launch traced here: 227 us
  blocking collectives  66.5 us (29%)
  Pallas kernels  63.9 us (28%)
  waiting for transfers between devices  42.7 us (18%)
  starting transfers between devices  29 us (13%)
  between operations  14.5 us (6%)
  other arithmetic  5.52 us (2%)
  local copies, waits for them, and re-layouts  5.17 us (2%)
    all_to_all x2, blocking collectives, exchange(): return lax.all_to_all(value, 'exp', split_axis=0, concat_axis=0, tiled=True)  66.5 us
    ppermute x9, waiting for transfers between devices, along(): return lax.ppermute(value, 'grp', hops)  17.6 us
    pallas_call x1, Pallas kernels, experts_both_ways(): pl.pallas_call(expert_kernel, grid=(GRP // 2,), out_shape=(pltpu.VMEM((EX...  16.7 us
    all_to_all x2, waiting for transfers between devices, exchange(): return lax.all_to_all(value, 'exp', split_axis=0, concat_axis=0, tiled=True)  14.7 us
    pallas_call x1, Pallas kernels, token_backward(): pl.pallas_call(backward_kernel, out_shape=outs, in_specs=[in_smem()] + in...  14.3 us
    pallas_call x1, Pallas kernels, expert_grads(): pl.pallas_call(expert_grad_kernel, grid=(GRP // 2,), out_shape=hbm(GRP *...  11.8 us
    ppermute x9, starting transfers between devices, along(): return lax.ppermute(value, 'grp', hops)  11.7 us
    all_to_all x2, starting transfers between devices, exchange(): return lax.all_to_all(value, 'exp', split_axis=0, concat_axis=0, tiled=True)  10.3 us
  transfers between devices with their start and end apart: 22, of which 11 were waited for; matrix products, arithmetic and copies ran while one was open for 5% of the time, Pallas kernels for 18%

profile of v6, /device:TPU:1, one launch (start us, length us, event | category | flops | bytes accessed | tf_op | source)
XLA Modules:
  0.0 227.4 jit_solution(17272386979807062315)
XLA Ops:
  7.2 0.0 all-gather.2.cloned.1.call-start
  7.3 1.4 pack.1
  8.7 0.0 copy-start.7
  8.7 0.0 copy-start.9
  8.7 2.1 collective-permute-start
  10.8 1.4 collective-permute-start.1
  12.2 0.8 copy.48
  13.0 0.1 eq.32
  13.2 1.2 reduce-window.6
  14.3 0.2 slice_reduce_fusion
  14.6 0.1 bitcast_bitcast_fusion
  14.7 0.1 reshape.74
  14.8 0.1 copy.49
  15.0 1.1 copy.55
  16.1 2.7 %collective-permute-done.refs_2_.refs_11_ = bf16[48,3200]{1,0:T(8,128)(2,1)} collective-permute-done((bf16[48,3200]{1,0:T(8,128)(2,1)S(1)}, bf16[48,3200]{1,0:T(8,128)(2,1)}, u32[]{:S(2)}, u32[]{:S(2)}) %collective-permute-start) | collective-permute-done | bytes 307232 | tf_op jit(solution)/shard_map/ppermute | solution.py:80
  18.8 1.2 collective-permute-start.2
  20.0 1.5 collective-permute-start.3
  21.4 0.1 convert_bitcast_fusion.1
  21.5 1.1 pad_maximum_fusion
  22.6 4.3 %collective-permute-done.2.refs_3_.refs_12_ = bf16[48,3200]{1,0:T(8,128)(2,1)} collective-permute-done((bf16[48,3200]{1,0:T(8,128)(2,1)S(1)}, bf16[48,3200]{1,0:T(8,128)(2,1)}, u32[]{:S(2)}, u32[]{:S(2)}) %collective-permute-start.2) | collective-permute-done | bytes 307232 | tf_op jit(solution)/shard_map/ppermute | solution.py:80
  27.0 0.0 all-gather.2.cloned.1.call-update
  27.0 2.9 %collective-permute-start.6 = (bf16[48,3200]{1,0:T(8,128)(2,1)S(1)}, bf16[48,3200]{1,0:T(8,128)(2,1)S(1)}, u32[]{:S(2)}, u32[]{:S(2)}) collective-permute-start(bf16[48,3200]{1,0:T(8,128)(2,1)S(1)} %get-tuple-element.70.refs_0_.refs_9_), channel_id=1, source_target_pairs={{0,16},{16,0},{32,48},{48,32},{64,80},{80,64},{96,112},{112,96},{1... | collective-permute-start | bytes 921608 | tf_op jit(solution)/shard_map/ppermute | solution.py:83
  29.9 0.1 collective-permute-start.7
  30.0 0.4 collective-permute-start.8
  30.4 0.9 collective-permute-start.4
  31.3 1.8 collective-permute-start.5
  33.1 0.6 collective-permute-start.11
  33.7 0.1 collective-permute-start.9
  33.8 0.4 collective-permute-start.10
  34.3 6.4 %collective-permute-done.4.refs_6_.refs_15_ = bf16[48,3200]{1,0:T(8,128)(2,1)S(1)} collective-permute-done((bf16[48,3200]{1,0:T(8,128)(2,1)}, bf16[48,3200]{1,0:T(8,128)(2,1)S(1)}, u32[]{:S(2)}, u32[]{:S(2)}) %collective-permute-start.4) | collective-permute-done | bytes 307232 | tf_op jit(solution)/shard_map/ppermute | solution.py:80
  40.6 0.9 collective-permute-start.12
  41.5 0.1 collective-permute-start.13
  41.7 0.1 stack.75.rows_ref
  41.8 0.1 copy.54.trow_ref
  41.9 0.0 collective-permute-done.9.refs_11_.refs_20_
  42.0 0.9 collective-permute-done.12.refs_14_.refs_23_
  42.9 0.4 collective-permute-done.13.refs_15_.refs_24_
  43.4 8.2 %token_forward.1 = (bf16[16,400,128]{2,1,0:T(8,128)(2,1)S(1)}, f32[208,768]{1,0:T(8,128)}, bf16[208,768]{1,0:T(8,128)(2,1)}, bf16[208,2304]{1,0:T(8,128)(2,1)}, ...) custom-call(s32[18]{0:T(128)S(1)} %stack.75.rows_ref, ...), custom_call_target="tpu_custom_call" | custom-call | flops 4000000000 | bytes 12000000 | tf_op jit(solution)/shard_map/token_forward/pallas_call | solution.py:572
  51.6 30.9 %all_to_all.20.got_ref = bf16[16,400,128]{2,1,0:T(8,128)(2,1)S(1)} all-to-all(bf16[16,400,128]{2,1,0:T(8,128)(2,1)S(1)} %get-tuple-element.72), channel_id=1, replica_groups=mesh['grp'=8,'exp'=16] {'exp'}, dimensions={0} | all-to-all | bytes 3276800 | tf_op jit(solution)/shard_map/all_to_all | solution.py:687
  82.5 3.9 %all-gather.2.cloned.1.call-done.w_ref = bf16[6144,768]{1,0:T(8,128)(2,1)} async-done(((bf16[768,768]{1,0:T(8,128)(2,1)}), bf16[6144,768]{1,0:T(8,128)(2,1)}) %all-gather.2.cloned.1.call-update) | async-done | bytes 9437200 | tf_op jit(solution)/shard_map/all_gather | solution.py:745
  86.4 16.7 %experts.1 = (bf16[16,400,128]{2,1,0:T(8,128)(2,1)}, bf16[528,3072]{1,0:T(8,128)(2,1)}, bf16[528,3072]{1,0:T(8,128)(2,1)}, bf16[768,528]{1,0:T(8,128)(2,1)}, bf16[768,528]{1,0:T(8,128)(2,1)}) custom-call(bf16[16,400,128]{2,1,0:T(8,128)(2,1)S(1)} %all_to_all.20.got_ref, bf16[6144,768]{1,0:T(8,128)(2,1)} %all-gather.2.cloned.1.call-done.w_ref), custom_call_target="tpu_custom_call" | custom-call | flops 10000000000 | bytes 23000000 | tf_op jit(solution)/shard_map/experts/pallas_call | solution.py:602
  103.1 6.7 %all-to-all-start.1 = ((bf16[16,400,128]{2,1,0:T(8,128)(2,1)}), bf16[16,400,128]{2,1,0:T(8,128)(2,1)S(1)}, u32[]{:S(2)}, u32[]{:S(2)}) async-start(bf16[16,400,128]{2,1,0:T(8,128)(2,1)} %get-tuple-element.74), calls=%async_computation.1 | async-start | bytes 3276800 | tf_op jit(solution)/shard_map/all_to_all | solution.py:687
  109.8 0.0 reduce-scatter.2.cloned.1.call-start
  109.9 11.8 %expert_grads.1 = bf16[6144,768]{1,0:T(8,128)(2,1)} custom-call(bf16[528,3072]{1,0:T(8,128)(2,1)} %get-tuple-element.86.h_ref, bf16[528,3072]{1,0:T(8,128)(2,1)} %get-tuple-element.87.du_ref, bf16[768,528]{1,0:T(8,128)(2,1)} %get-tuple-element.88.xt_ref, bf16[768,528]{1,0:T(8,128)(2,1)} %get-tuple-element.89.dzt_ref), custom_call_target="tpu_custom_call" | custom-call | flops 6000000000 | bytes 18000000 | tf_op jit(solution)/shard_map/expert_grads/pallas_call | solution.py:624
  121.7 0.0 reduce-scatter.2.cloned.1.call-update
  121.7 13.6 %all-to-all-done.1.back_ref = bf16[16,400,128]{2,1,0:T(8,128)(2,1)S(1)} async-done(((bf16[16,400,128]{2,1,0:T(8,128)(2,1)}), bf16[16,400,128]{2,1,0:T(8,128)(2,1)S(1)}, u32[]{:S(2)}, u32[]{:S(2)}) %all-to-all-start.1) | async-done | bytes 1638432 | tf_op jit(solution)/shard_map/all_to_all | solution.py:687
  135.4 14.3 %token_backward.1 = (bf16[1,197,768]{2,1,0:T(8,128)(2,1)}, f32[1,197,768]{2,1,0:T(8,128)}, bf16[16,208,384]{2,1,0:T(8,128)(2,1)}, bf16[16,208,384]{2,1,0:T(8,128)(2,1)}) custom-call(s32[18]{0:T(128)S(1)} %stack.75.rows_ref, s32[208,2]{1,0:T(8,128)S(1)} %pad.15.ids_ref, s32[208,2]{1,0:T(8,128)S(1)} %pad.17.tcol_ref, f32[208,2]{1,0:T(8,128)S(1)} %pad.18.keep_ref, ...), custom_call_target="tpu_custom_call" | custom-call | flops 399999991808 | bytes 18000000 | tf_op jit(solution)/shard_map/token_backward/pallas_call | solution.py:645
  149.6 1.4 collective-permute-start.14
  151.1 5.1 %collective-permute-done.14 = bf16[16,208,384]{2,1,0:T(8,128)(2,1)S(1)} collective-permute-done((bf16[16,208,384]{2,1,0:T(8,128)(2,1)}, bf16[16,208,384]{2,1,0:T(8,128)(2,1)S(1)}, u32[]{:S(2)}, u32[]{:S(2)}) %collective-permute-start.14) | collective-permute-done | bytes 2555936 | tf_op jit(solution)/shard_map/ppermute | solution.py:695
  156.1 2.6 %add_convert_fusion = bf16[16,208,384]{2,1,0:T(8,128)(2,1)S(1)} fusion(bf16[16,208,384]{2,1,0:T(8,128)(2,1)S(1)} %collective-permute-done.14, bf16[16,208,384]{2,1,0:T(8,128)(2,1)} %get-tuple-element.84), kind=kLoop, calls=%fused_computation.1 | loop fusion | flops 5111808 | bytes 7667712 | tf_op jit(solution)/shard_map/convert_element_type | solution.py:696
  158.7 35.6 %all_to_all.21 = bf16[16,208,384]{2,1,0:T(8,128)(2,1)S(1)} all-to-all(bf16[16,208,384]{2,1,0:T(8,128)(2,1)S(1)} %add_convert_fusion), channel_id=1, replica_groups=mesh['grp'=8,'exp'=16] {'exp'}, dimensions={0} | all-to-all | bytes 5111808 | tf_op jit(solution)/shard_map/all_to_all | solution.py:687
  194.3 0.4 convert_reduce_fusion
  194.8 0.1 collective-permute-start.15
  194.9 2.7 %collective-permute-start.17 = (bf16[49,384]{1,0:T(8,128)(2,1)S(1)}, bf16[49,384]{1,0:T(8,128)(2,1)S(1)}, u32[]{:S(2)}, u32[]{:S(2)}) collective-permute-start(bf16[49,384]{1,0:T(8,128)(2,1)S(1)} %get-tuple-element.151), channel_id=1, source_target_pairs={{0,96},{16,112},{32,0},{48,16},{64,32},{80,48},{96,64},{112,80},{1... | collective-permute-start | bytes 112904 | tf_op jit(solution)/shard_map/ppermute | solution.py:693
  197.6 0.2 collective-permute-start.16
  197.7 1.2 collective-permute-done.15
  199.0 3.0 %collective-permute-done.16 = bf16[49,384]{1,0:T(8,128)(2,1)S(1)} collective-permute-done((bf16[49,384]{1,0:T(8,128)(2,1)S(1)}, bf16[49,384]{1,0:T(8,128)(2,1)S(1)}, u32[]{:S(2)}, u32[]{:S(2)}) %collective-permute-start.16) | collective-permute-done | bytes 37664 | tf_op jit(solution)/shard_map/ppermute | solution.py:693
  202.0 0.9 broadcast_in_dim.16
  202.9 3.6 %all-to-all-start.3 = ((bf16[16,49,384]{2,1,0:T(8,128)(2,1)}), bf16[16,49,384]{2,1,0:T(8,128)(2,1)S(1)}, u32[]{:S(2)}, u32[]{:S(2)}) async-start(bf16[16,49,384]{2,1,0:T(8,128)(2,1)} %broadcast_in_dim.16), calls=%async_computation.3 | async-start | bytes 1376256 | tf_op jit(solution)/shard_map/all_to_all | solution.py:687
  206.5 1.4 copy.56
  208.0 0.0 reduce-scatter.2.cloned.1.call-done.grad_ref
  208.0 7.5 %expert_step.1 = (f32[1,768,384]{2,1,0:T(8,128)}, f32[1,768,384]{2,1,0:T(8,128)}, f32[1,768,384]{2,1,0:T(8,128)}, f32[1,384,768]{2,1,0:T(8,128)}, f32[1,384,768]{2,1,0:T(8,128)}, /*index=5*/f32[1,384,768]{2,1,0:T(8,128)}) custom-call(bf16[768,768]{1,0:T(8,128)(2,1)} %reduce-scatter.2.cloned.1.call-done.grad_ref, f32[1,768,384]{2,1,0:T(8,128)} %refs_0_.2, ...), custom_call_target="tpu_custom_call" | custom-call | flops 10000000 | bytes 8000000 | tf_op jit(solution)/shard_map/expert_step/pallas_call | solution.py:496
  215.5 1.0 all-to-all-done.3.pieces_ref
  216.6 4.0 %owner_step.1 = (f32[96,2304]{1,0:T(8,128)}, f32[96,2304]{1,0:T(8,128)}, f32[96,2304]{1,0:T(8,128)}, f32[96,768]{1,0:T(8,128)}, f32[96,768]{1,0:T(8,128)}, /*ind...) custom-call(bf16[16,49,384]{2,1,0:T(8,128)(2,1)S(1)} %all-to-all-don, ...), custom_call_target="tpu_custom_call" | custom-call | flops 10000000 | bytes 8000000 | tf_op jit(solution)/shard_map/owner_step/pallas_call | solution.py:672
  (63 shorter events, 0.4 us)
Async XLA Ops:
  7.2 7.6 %copy-start.12 = (s32[1,197,2]{1,2,0:T(2,128)S(1)}, s32[1,197,2]{1,2,0:T(2,128)}, u32[]{:S(2)}) copy-start(s32[1,197,2]{1,2,0:T(2,128)} %param.25) | copy-start | bytes 4732
  7.2 7.8 %copy-start.8 = (f32[1,384,768]{2,1,0:T(8,128)S(1)}, f32[1,384,768]{2,1,0:T(8,128)}, u32[]{:S(2)}) copy-start(f32[1,384,768]{2,1,0:T(8,128)} %refs_3_.2) | copy-start | bytes 3538948
  7.2 79.2 %all-gather.2.cloned.1.call-start = ((), (), s32[]{:S(2)}) async-start(), calls=%async_computation.5 | async-start | bytes 10616832 | tf_op jit(solution)/shard_map/all_gather | solution.py:745
  8.7 18.3 %copy-start.6 = (bf16[48,3200]{1,0:T(8,128)(2,1)}, bf16[48,3200]{1,0:T(8,128)(2,1)S(1)}, u32[]{:S(2)}) copy-start(bf16[48,3200]{1,0:T(8,128)(2,1)S(1)} %get-tuple-element.70.refs_0_.refs_9_) | copy-start | bytes 921604
  8.7 21.2 %copy-start.7 = (bf16[48,3200]{1,0:T(8,128)(2,1)}, bf16[48,3200]{1,0:T(8,128)(2,1)S(1)}, u32[]{:S(2)}) copy-start(bf16[48,3200]{1,0:T(8,128)(2,1)S(1)} %get-tuple-element.69.refs_1_.refs_10_) | copy-start | bytes 921604
  8.7 12.7 %copy-start.9 = (f32[1,768,384]{2,1,0:T(8,128)S(1)}, f32[1,768,384]{2,1,0:T(8,128)}, u32[]{:S(2)}) copy-start(f32[1,768,384]{2,1,0:T(8,128)} %refs_0_.2) | copy-start | bytes 3538948
  8.7 10.0 %collective-permute-start = (bf16[48,3200]{1,0:T(8,128)(2,1)S(1)}, bf16[48,3200]{1,0:T(8,128)(2,1)}, u32[]{:S(2)}, u32[]{:S(2)}) collective-permute-start(bf16[48,3200]{1,0:T(8,128)(2,1)S(1)} %get-tuple-element.70.refs_0_.refs_9_), channel_id=1, source_target_pairs={{0,32},{16,48},{32,64},{48,80},{64,96},{80,112},{96,0},{112,16},{1... | collective-permute-start | bytes 921608 | tf_op jit(solution)/shard_map/ppermute | solution.py:80
  10.8 7.9 %collective-permute-start.1 = (bf16[48,3200]{1,0:T(8,128)(2,1)S(1)}, bf16[48,3200]{1,0:T(8,128)(2,1)}, u32[]{:S(2)}, u32[]{:S(2)}) collective-permute-start(bf16[48,3200]{1,0:T(8,128)(2,1)S(1)} %get-tuple-element.69.refs_1_.refs_10_), channel_id=1, source_target_pairs={{0,96},{16,112},{32,0},{48,16},{64,32},{80,48},{96,64},{112,80},{1... | collective-permute-start | bytes 921608 | tf_op jit(solution)/shard_map/ppermute | solution.py:80
  16.0 5.5 %copy-start.10 = (bf16[1,384,768]{1,2,0:T(8,128)(2,1)S(1)}, bf16[1,384,768]{1,2,0:T(8,128)(2,1)}, u32[]{:S(2)}) copy-start(bf16[1,384,768]{1,2,0:T(8,128)(2,1)} %copy.55) | copy-start | bytes 1769476
  18.8 8.2 %collective-permute-start.2 = (bf16[48,3200]{1,0:T(8,128)(2,1)S(1)}, bf16[48,3200]{1,0:T(8,128)(2,1)}, u32[]{:S(2)}, u32[]{:S(2)}) collective-permute-start(bf16[48,3200]{1,0:T(8,128)(2,1)S(1)} %get-tuple-element.69.refs_1_.refs_10_), channel_id=1, source_target_pairs={{0,32},{16,48},{32,64},{48,80},{64,96},{80,112},{96,0},{112,16},{1... | collective-permute-start | bytes 921608 | tf_op jit(solution)/shard_map/ppermute | solution.py:80
  20.0 7.0 %collective-permute-start.3 = (bf16[48,3200]{1,0:T(8,128)(2,1)S(1)}, bf16[48,3200]{1,0:T(8,128)(2,1)}, u32[]{:S(2)}, u32[]{:S(2)}) collective-permute-start(bf16[48,3200]{1,0:T(8,128)(2,1)S(1)} %get-tuple-element.70.refs_0_.refs_9_), channel_id=1, source_target_pairs={{0,96},{16,112},{32,0},{48,16},{64,32},{80,48},{96,64},{112,80},{1... | collective-permute-start | bytes 921608 | tf_op jit(solution)/shard_map/ppermute | solution.py:80
  27.0 6.1 %collective-permute-start.6 = (bf16[48,3200]{1,0:T(8,128)(2,1)S(1)}, bf16[48,3200]{1,0:T(8,128)(2,1)S(1)}, u32[]{:S(2)}, u32[]{:S(2)}) collective-permute-start(bf16[48,3200]{1,0:T(8,128)(2,1)S(1)} %get-tuple-element.70.refs_0_.refs_9_), channel_id=1, source_target_pairs={{0,16},{16,0},{32,48},{48,32},{64,80},{80,64},{96,112},{112,96},{1... | collective-permute-start | bytes 921608 | tf_op jit(solution)/shard_map/ppermute | solution.py:83
  29.9 3.9 %collective-permute-start.7 = (bf16[48,3200]{1,0:T(8,128)(2,1)S(1)}, bf16[48,3200]{1,0:T(8,128)(2,1)S(1)}, u32[]{:S(2)}, u32[]{:S(2)}) collective-permute-start(bf16[48,3200]{1,0:T(8,128)(2,1)S(1)} %get-tuple-element.69.refs_1_.refs_10_), channel_id=1, source_target_pairs={{0,16},{16,0},{32,48},{48,32},{64,80},{80,64},{96,112},{112,96},{1... | collective-permute-start | bytes 921608 | tf_op jit(solution)/shard_map/ppermute | solution.py:83
  30.0 3.9 %collective-permute-start.8 = (bf16[48,3200]{1,0:T(8,128)(2,1)}, bf16[48,3200]{1,0:T(8,128)(2,1)S(1)}, u32[]{:S(2)}, u32[]{:S(2)}) collective-permute-start(bf16[48,3200]{1,0:T(8,128)(2,1)} %collective-permute-done.refs_2_.refs_11_), channel_id=1, source_target_pairs={{0,16},{16,0},{32,48},{48,32},{64,80},{80,64},{96,112},{112,96},{1... | collective-permute-start | bytes 921608 | tf_op jit(solution)/shard_map/ppermute | solution.py:83
  30.4 10.3 %collective-permute-start.4 = (bf16[48,3200]{1,0:T(8,128)(2,1)}, bf16[48,3200]{1,0:T(8,128)(2,1)S(1)}, u32[]{:S(2)}, u32[]{:S(2)}) collective-permute-start(bf16[48,3200]{1,0:T(8,128)(2,1)} %collective-permute-done.refs_2_.refs_11_), channel_id=1, source_target_pairs={{0,32},{16,48},{32,64},{48,80},{64,96},{80,112},{96,0},{112,16},{1... | collective-permute-start | bytes 921608 | tf_op jit(solution)/shard_map/ppermute | solution.py:80
  31.3 10.2 %collective-permute-start.5 = (bf16[48,3200]{1,0:T(8,128)(2,1)}, bf16[48,3200]{1,0:T(8,128)(2,1)S(1)}, u32[]{:S(2)}, u32[]{:S(2)}) collective-permute-start(bf16[48,3200]{1,0:T(8,128)(2,1)} %collective-permute-done.1.refs_5_.refs_14_), channel_id=1, source_target_pairs={{0,96},{16,112},{32,0},{48,16},{64,32},{80,48},{96,64},{112,80},{1... | collective-permute-start | bytes 921608 | tf_op jit(solution)/shard_map/ppermute | solution.py:80
  33.1 10.2 %copy-start.13 = (bf16[48,3200]{1,0:T(8,128)(2,1)}, bf16[48,3200]{1,0:T(8,128)(2,1)S(1)}, u32[]{:S(2)}) copy-start(bf16[48,3200]{1,0:T(8,128)(2,1)S(1)} %collective-permute-done.6.refs_8_.refs_17_) | copy-start | bytes 921604
  33.1 8.8 %collective-permute-start.11 = (bf16[48,3200]{1,0:T(8,128)(2,1)}, bf16[48,3200]{1,0:T(8,128)(2,1)S(1)}, u32[]{:S(2)}, u32[]{:S(2)}) collective-permute-start(bf16[48,3200]{1,0:T(8,128)(2,1)} %collective-permute-done.1.refs_5_.refs_14_), channel_id=1, source_target_pairs={{0,16},{16,0},{32,48},{48,32},{64,80},{80,64},{96,112},{112,96},{1... | collective-permute-start | bytes 921608 | tf_op jit(solution)/shard_map/ppermute | solution.py:83
  33.7 9.6 %copy-start.14 = (bf16[48,3200]{1,0:T(8,128)(2,1)}, bf16[48,3200]{1,0:T(8,128)(2,1)S(1)}, u32[]{:S(2)}) copy-start(bf16[48,3200]{1,0:T(8,128)(2,1)S(1)} %collective-permute-done.7.refs_9_.refs_18_) | copy-start | bytes 921604
  33.7 8.2 %collective-permute-start.9 = (bf16[48,3200]{1,0:T(8,128)(2,1)}, bf16[48,3200]{1,0:T(8,128)(2,1)S(1)}, u32[]{:S(2)}, u32[]{:S(2)}) collective-permute-start(bf16[48,3200]{1,0:T(8,128)(2,1)} %collective-permute-done.2.refs_3_.refs_12_), channel_id=1, source_target_pairs={{0,16},{16,0},{32,48},{48,32},{64,80},{80,64},{96,112},{112,96},{1... | collective-permute-start | bytes 921608 | tf_op jit(solution)/shard_map/ppermute | solution.py:83
  33.8 9.5 %copy-start.15 = (bf16[48,3200]{1,0:T(8,128)(2,1)}, bf16[48,3200]{1,0:T(8,128)(2,1)S(1)}, u32[]{:S(2)}) copy-start(bf16[48,3200]{1,0:T(8,128)(2,1)S(1)} %collective-permute-done.8.refs_10_.refs_19_) | copy-start | bytes 921604
  33.8 8.1 %collective-permute-start.10 = (bf16[48,3200]{1,0:T(8,128)(2,1)}, bf16[48,3200]{1,0:T(8,128)(2,1)}, u32[]{:S(2)}, u32[]{:S(2)}) collective-permute-start(bf16[48,3200]{1,0:T(8,128)(2,1)} %collective-permute-done.3.refs_4_.refs_13_), channel_id=1, source_target_pairs={{0,16},{16,0},{32,48},{48,32},{64,80},{80,64},{96,112},{112,96},{1... | collective-permute-start | bytes 921608 | tf_op jit(solution)/shard_map/ppermute | solution.py:83
  40.6 2.7 %copy-start.16 = (bf16[48,3200]{1,0:T(8,128)(2,1)}, bf16[48,3200]{1,0:T(8,128)(2,1)S(1)}, u32[]{:S(2)}) copy-start(bf16[48,3200]{1,0:T(8,128)(2,1)S(1)} %collective-permute-done.4.refs_6_.refs_15_) | copy-start | bytes 921604
  40.6 2.2 collective-permute-start.12
  41.5 1.8 copy-start.17
  41.5 1.8 collective-permute-start.13
  41.9 1.4 copy-start.18
  41.9 1.4 copy-start.19
  103.1 32.2 %all-to-all-start.1 = ((bf16[16,400,128]{2,1,0:T(8,128)(2,1)}), bf16[16,400,128]{2,1,0:T(8,128)(2,1)S(1)}, u32[]{:S(2)}, u32[]{:S(2)}) async-start(bf16[16,400,128]{2,1,0:T(8,128)(2,1)} %get-tuple-element.74), calls=%async_computation.1 | async-start | bytes 3276800 | tf_op jit(solution)/shard_map/all_to_all | solution.py:687
  109.8 98.2 %reduce-scatter.2.cloned.1.call-start = ((), (), s32[]{:S(2)}) async-start(), calls=%async_computation.6 | async-start | bytes 10616832 | tf_op jit(solution)/shard_map/reduce_scatter | solution.py:752
  149.6 6.5 %collective-permute-start.14 = (bf16[16,208,384]{2,1,0:T(8,128)(2,1)}, bf16[16,208,384]{2,1,0:T(8,128)(2,1)S(1)}, u32[]{:S(2)}, u32[]{:S(2)}) collective-permute-start(bf16[16,208,384]{2,1,0:T(8,128)(2,1)} %get-tuple-element.85), channel_id=1, source_target_pairs={{0,16},{16,0},{32,48},{48,32},{64,80},{80,64},{96,112},{112,96},{1... | collective-permute-start | bytes 7667720 | tf_op jit(solution)/shard_map/ppermute | solution.py:695
  194.8 11.7 %copy-start.11 = (f32[1,197,768]{2,1,0:T(8,128)S(1)}, f32[1,197,768]{2,1,0:T(8,128)}, u32[]{:S(2)}) copy-start(f32[1,197,768]{2,1,0:T(8,128)} %get-tuple-element.131) | copy-start | bytes 1815556
  194.8 4.2 %collective-permute-start.15 = (bf16[49,384]{1,0:T(8,128)(2,1)S(1)}, bf16[49,384]{1,0:T(8,128)(2,1)S(1)}, u32[]{:S(2)}, u32[]{:S(2)}) collective-permute-start(bf16[49,384]{1,0:T(8,128)(2,1)S(1)} %get-tuple-element.150), channel_id=1, source_target_pairs={{0,32},{16,48},{32,64},{48,80},{64,96},{80,112},{96,0},{112,16},{1... | collective-permute-start | bytes 112904 | tf_op jit(solution)/shard_map/ppermute | solution.py:693
  194.9 4.1 %collective-permute-start.17 = (bf16[49,384]{1,0:T(8,128)(2,1)S(1)}, bf16[49,384]{1,0:T(8,128)(2,1)S(1)}, u32[]{:S(2)}, u32[]{:S(2)}) collective-permute-start(bf16[49,384]{1,0:T(8,128)(2,1)S(1)} %get-tuple-element.151), channel_id=1, source_target_pairs={{0,96},{16,112},{32,0},{48,16},{64,32},{80,48},{96,64},{112,80},{1... | collective-permute-start | bytes 112904 | tf_op jit(solution)/shard_map/ppermute | solution.py:693
  197.6 4.4 %collective-permute-start.16 = (bf16[49,384]{1,0:T(8,128)(2,1)S(1)}, bf16[49,384]{1,0:T(8,128)(2,1)S(1)}, u32[]{:S(2)}, u32[]{:S(2)}) collective-permute-start(bf16[49,384]{1,0:T(8,128)(2,1)S(1)} %get-tuple-element.152), channel_id=1, source_target_pairs={{0,64},{16,80},{32,96},{48,112},{64,0},{80,16},{96,32},{112,48},{1... | collective-permute-start | bytes 112904 | tf_op jit(solution)/shard_map/ppermute | solution.py:693
  202.9 13.6 %all-to-all-start.3 = ((bf16[16,49,384]{2,1,0:T(8,128)(2,1)}), bf16[16,49,384]{2,1,0:T(8,128)(2,1)S(1)}, u32[]{:S(2)}, u32[]{:S(2)}) async-start(bf16[16,49,384]{2,1,0:T(8,128)(2,1)} %broadcast_in_dim.16), calls=%async_computation.3 | async-start | bytes 1376256 | tf_op jit(solution)/shard_map/all_to_all | solution.py:687
  207.9 8.6 %copy-start = (f32[96,16]{0,1:T(8,128)S(1)}, f32[96,16]{0,1:T(8,128)}, u32[]{:S(2)}) copy-start(f32[96,16]{0,1:T(8,128)} %param.32) | copy-start | bytes 18436
  207.9 8.6 %copy-start.1 = (f32[96,16]{0,1:T(8,128)S(1)}, f32[96,16]{0,1:T(8,128)}, u32[]{:S(2)}) copy-start(f32[96,16]{0,1:T(8,128)} %param.33) | copy-start | bytes 18436
  208.0 8.6 %copy-start.2 = (f32[96,16]{0,1:T(8,128)S(1)}, f32[96,16]{0,1:T(8,128)}, u32[]{:S(2)}) copy-start(f32[96,16]{0,1:T(8,128)} %param.34) | copy-start | bytes 18436
  208.0 8.6 %copy-start.3 = (f32[96,4]{0,1:T(4,128)S(1)}, f32[96,4]{0,1:T(4,128)}, u32[]{:S(2)}) copy-start(f32[96,4]{0,1:T(4,128)} %param.35) | copy-start | bytes 4612
  208.0 8.6 %copy-start.4 = (f32[96,4]{0,1:T(4,128)S(1)}, f32[96,4]{0,1:T(4,128)}, u32[]{:S(2)}) copy-start(f32[96,4]{0,1:T(4,128)} %param.36) | copy-start | bytes 4612
  208.0 8.6 %copy-start.5 = (f32[96,4]{0,1:T(4,128)S(1)}, f32[96,4]{0,1:T(4,128)}, u32[]{:S(2)}) copy-start(f32[96,4]{0,1:T(4,128)} %param.37) | copy-start | bytes 4612
Sparse Core Ops, SparseCore 0:
  27.1 59.2 all-gather.1
  121.9 57.1 reduce-scatter.1
